TPU v7x, 32 devices: a whole 2x2x4 slice. The times are simulated.
32 devices in a mesh: mol: 2 (over x), row: 16 (over z, y, core).
Axes of the slice: x: 2, y: 2, z: 4, core: 2. Of those that a mesh axis runs over, the one named last changes fastest.
Arguments:
- amplitude: float32 [32, 15, 256, 256], P(('mol', 'row')), parts along dimension 0, may hold values from -0.375 to 0.375
- integral: float32 [32, 15, 256, 256], P(('mol', 'row')), parts along dimension 0, may hold values from -6 to 6
- pair_gap: float32 [32, 256], P(('mol', 'row')), parts along dimension 0, may hold values from 0.5 to 2
- present: int32 [32, 15], P(('mol', 'row')), parts along dimension 0, may hold values from 0 to 1, as said below
Outputs:
- new_amplitude: float32 [32, 15, 256, 256], P(('mol', 'row')), parts along dimension 0
- energy: float32 [2], P('mol'), parts along dimension 0
There are 2 independent parts, one for each index of `mol`. A program takes and returns all parts, laid end to end along the dimension named above; each array names one. Nothing has to cross between parts.
Inputs may be any that keep to these rules, and one draw needn't show every extreme that they name: Symmetric: present[I,s] equals present[I + s - 7, 14 - s]; slot 7 is always 1; slots whose column block lies outside 0 to 15 are 0; some block has every slot 1.
All inputs are finite; a program needn't handle non-finite values.
Results may differ from a plain program's by a relative error of at most 0.000053.
Values sent between devices are 32-bit elements; how exact they have to be, the bound alone decides.
No kernel may reach another device: no remote copies, remote signals or barrier semaphores. Data moves between devices by JAX's collectives and lax.ppermute only.
A program may use at most 64 MiB of HBM per device.

v0:
```python
import jax
import jax.numpy as jnp
from jax import lax
from jax.sharding import PartitionSpec as P


def passed_along(value, axis, steps):
    count = lax.axis_size(axis)
    first, last = (max(0, -steps), min(count, count - steps))
    return lax.ppermute(value, axis, [(source, source + steps) for source in range(first, last)])


def block_terms(amp_block, int_block):
    hi = lax.Precision.HIGHEST
    first = jnp.dot(amp_block, int_block, precision=hi, preferred_element_type=jnp.float32)
    second = jnp.dot(amp_block, int_block.T, precision=hi, preferred_element_type=jnp.float32)
    third = jnp.dot(first, amp_block.T, precision=hi, preferred_element_type=jnp.float32)
    return first + second - 0.5 * third


def per_device(amplitude, integral, pair_gap, present):
    slots = amplitude.shape[1]
    width = amplitude.shape[2]
    reach = (slots - 1) // 2
    own_amp = amplitude[0]
    own_int = integral[0]
    own_gap = pair_gap[0]
    flags = present[0]
    cycle = jax.vmap(block_terms)(own_amp, own_int)
    mirror_list = [None] * slots
    gap_list = [None] * slots
    mirror_list[reach] = cycle[reach].T
    gap_list[reach] = own_gap
    for block_offset in range(1, reach + 1):
        arrived, arrived_gap = passed_along(
            (cycle[reach - block_offset], own_gap), "row", -block_offset
        )
        mirror_list[reach + block_offset] = arrived.T
        gap_list[reach + block_offset] = arrived_gap
        arrived, arrived_gap = passed_along(
            (cycle[reach + block_offset], own_gap), "row", block_offset
        )
        mirror_list[reach - block_offset] = arrived.T
        gap_list[reach - block_offset] = arrived_gap
    mirrored = jnp.stack(mirror_list, axis=0)
    gap_col = jnp.stack(gap_list, axis=0)
    denom = own_gap[None, :, None] + gap_col[:, None, :]
    total = own_int + cycle + mirrored
    updated = jnp.where(flags[:, None, None] > 0, total / denom, jnp.float32(0.0))
    partial_sum = jnp.sum(updated * own_int)
    whole = lax.psum(partial_sum, "row")
    blocks_all = lax.axis_size("row") * amplitude.shape[0]
    energy = whole / (width * width * blocks_all)
    return (updated[None], jnp.reshape(energy, (1,)))


def solution(mesh):
    in_specs = (
        P(("mol", "row"), None, None, None),
        P(("mol", "row"), None, None, None),
        P(("mol", "row"), None),
        P(("mol", "row"), None),
    )
    out_specs = (P(("mol", "row"), None, None, None), P("mol"))
    return jax.shard_map(
        per_device, mesh=mesh, in_specs=in_specs, out_specs=out_specs, check_vma=False
    )
```

profile of v0, /device:TPU:0, one launch (start us, length us, event | category | flops | bytes accessed | tf_op | source)
XLA Modules:
  0.0 191.4 jit_solution(14995902828672772148)
XLA Ops:
  0.7 7.5 %fusion = f32[15,256,256]{2,1,0:T(8,128)S(1)} fusion(f32[1,15,256,256]{3,2,1,0:T(8,128)} %param.5, f32[1,15,256,256]{3,2,1,0:T(8,128)} %param.4), kind=kOutput, calls=%fused_computation | convolution fusion | flops 3019898880 | bytes 11796480 | tf_op jit(solution)/shard_map/vmap()/dot_general | solution.py:15
  8.1 4.0 %fusion.2 = f32[15,256,256]{2,1,0:T(8,128)S(1)} fusion(f32[1,15,256,256]{3,2,1,0:T(8,128)S(1)} %copy-done, f32[1,15,256,256]{3,2,1,0:T(8,128)S(1)} %copy-done.1), kind=kOutput, calls=%fused_computation.2 | convolution fusion | flops 3019898880 | bytes 11796480 | tf_op jit(solution)/shard_map/vmap()/dot_general | solution.py:16
  12.2 4.6 %multiply_subtract_fusion = f32[15,256,256]{2,1,0:T(8,128)S(1)} fusion(f32[15,256,256]{2,1,0:T(8,128)S(1)} %fusion, f32[15,256,256]{2,1,0:T(8,128)S(1)} %fusion.2, f32[1,15,256,256]{3,2,1,0:T(8,128)S(1)} %copy-done.1), kind=kOutput, calls=%fused_computation.14 | convolution fusion | flops 3022848000 | bytes 15728640 | tf_op jit(solution)/shard_map/vmap()/dot_general | solution.py:17
  16.8 1.9 copy-done.2
  18.6 1.1 slice_bitcast_fusion
  19.7 6.0 %collective-permute-start = (f32[256,256]{1,0:T(8,128)}, f32[256,256]{1,0:T(8,128)}, u32[]{:S(2)}, u32[]{:S(2)}) collective-permute-start(f32[256,256]{1,0:T(8,128)} %get-tuple-element.19), channel_id=1, source_target_pairs={{0,7},{1,8},{2,9},{3,10},{4,11},{5,12},{6,13},{7,14},{8,15},{16,23... | collective-permute-start | bytes 786440 | tf_op jit(solution)/shard_map/ppermute | solution.py:10
  25.7 4.1 %collective-permute-start.14 = (f32[256]{0:T(256)S(1)}, f32[256]{0:T(256)S(1)}, u32[]{:S(2)}, u32[]{:S(2)}) collective-permute-start(f32[256]{0:T(256)S(1)} %bitcast.143), channel_id=1, source_target_pairs={{0,7},{1,8},{2,9},{3,10},{4,11},{5,12},{6,13},{7,14},{8,15},{16,23... | collective-permute-start | bytes 3080 | tf_op jit(solution)/shard_map/ppermute | solution.py:10
  29.8 1.6 collective-permute-start.15
  31.5 1.3 collective-permute-start.16
  32.8 1.6 collective-permute-start.17
  34.3 3.5 %collective-permute-start.18 = (f32[256]{0:T(256)S(1)}, f32[256]{0:T(256)S(1)}, u32[]{:S(2)}, u32[]{:S(2)}) collective-permute-start(f32[256]{0:T(256)S(1)} %bitcast.147), channel_id=1, source_target_pairs={{0,3},{1,4},{2,5},{3,6},{4,7},{5,8},{6,9},{7,10},{8,11},{9,12},{10... | collective-permute-start | bytes 3080 | tf_op jit(solution)/shard_map/ppermute | solution.py:10
  37.8 3.6 %collective-permute-start.19 = (f32[256]{0:T(256)S(1)}, f32[256]{0:T(256)S(1)}, u32[]{:S(2)}, u32[]{:S(2)}) collective-permute-start(f32[256]{0:T(256)S(1)} %bitcast.148), channel_id=1, source_target_pairs={{0,2},{1,3},{2,4},{3,5},{4,6},{5,7},{6,8},{7,9},{8,10},{9,11},{10,... | collective-permute-start | bytes 3080 | tf_op jit(solution)/shard_map/ppermute | solution.py:10
  41.4 4.8 %collective-permute-start.20 = (f32[256]{0:T(256)S(1)}, f32[256]{0:T(256)S(1)}, u32[]{:S(2)}, u32[]{:S(2)}) collective-permute-start(f32[256]{0:T(256)S(1)} %bitcast.149), channel_id=1, source_target_pairs={{0,1},{1,2},{2,3},{3,4},{4,5},{5,6},{6,7},{7,8},{8,9},{9,10},{10,1... | collective-permute-start | bytes 3080 | tf_op jit(solution)/shard_map/ppermute | solution.py:10
  46.3 1.3 collective-permute-start.21
  47.6 1.3 collective-permute-start.22
  48.9 1.3 collective-permute-start.23
  50.2 1.3 collective-permute-start.24
  51.5 1.3 collective-permute-start.25
  52.8 1.9 %collective-permute-done.22 = f32[256]{0:T(256)S(1)} collective-permute-done((f32[256]{0:T(256)S(1)}, f32[256]{0:T(256)S(1)}, u32[]{:S(2)}, u32[]{:S(2)}) %collective-permute-start.22) | collective-permute-done | bytes 1056 | tf_op jit(solution)/shard_map/ppermute | solution.py:10
  54.7 1.3 collective-permute-start.26
  56.1 1.3 collective-permute-start.27
  57.4 2.7 %collective-permute-done.24 = f32[256]{0:T(256)S(1)} collective-permute-done((f32[256]{0:T(256)S(1)}, f32[256]{0:T(256)S(1)}, u32[]{:S(2)}, u32[]{:S(2)}) %collective-permute-start.24) | collective-permute-done | bytes 1056 | tf_op jit(solution)/shard_map/ppermute | solution.py:10
  60.1 6.6 %collective-permute-start.1 = (f32[256,256]{1,0:T(8,128)S(1)}, f32[256,256]{1,0:T(8,128)}, u32[]{:S(2)}, u32[]{:S(2)}) collective-permute-start(f32[256,256]{1,0:T(8,128)S(1)} %get-tuple-element.18), channel_id=1, source_target_pairs={{0,6},{1,7},{2,8},{3,9},{4,10},{5,11},{6,12},{7,13},{8,14},{9,15},... | collective-permute-start | bytes 786440 | tf_op jit(solution)/shard_map/ppermute | solution.py:10
  66.7 5.5 %copy.9 = f32[15,256,256]{1,2,0:T(8,128)} copy(f32[15,256,256]{2,1,0:T(8,128)} %copy-done.2) | data formatting | bytes 7864320 | tf_op jit(solution)/shard_map/vmap()/sub | solution.py:18
  72.1 5.4 %copy.6 = f32[1,15,256,256]{2,3,1,0:T(8,128)} copy(f32[1,15,256,256]{3,2,1,0:T(8,128)} %param.5) | data formatting | bytes 7864320 | tf_op args[1]
  77.6 4.5 %collective-permute-start.2 = (f32[256,256]{1,0:T(8,128)S(1)}, f32[256,256]{1,0:T(8,128)}, u32[]{:S(2)}, u32[]{:S(2)}) collective-permute-start(f32[256,256]{1,0:T(8,128)S(1)} %get-tuple-element.17), channel_id=1, source_target_pairs={{0,5},{1,6},{2,7},{3,8},{4,9},{5,10},{6,11},{7,12},{8,13},{9,14},{... | collective-permute-start | bytes 786440 | tf_op jit(solution)/shard_map/ppermute | solution.py:10
  82.1 5.3 %collective-permute-start.3 = (f32[256,256]{1,0:T(8,128)S(1)}, f32[256,256]{1,0:T(8,128)}, u32[]{:S(2)}, u32[]{:S(2)}) collective-permute-start(f32[256,256]{1,0:T(8,128)S(1)} %get-tuple-element.16), channel_id=1, source_target_pairs={{0,4},{1,5},{2,6},{3,7},{4,8},{5,9},{6,10},{7,11},{8,12},{9,13},{1... | collective-permute-start | bytes 786440 | tf_op jit(solution)/shard_map/ppermute | solution.py:10
  87.4 2.6 %collective-permute-start.4 = (f32[256,256]{1,0:T(8,128)S(1)}, f32[256,256]{1,0:T(8,128)}, u32[]{:S(2)}, u32[]{:S(2)}) collective-permute-start(f32[256,256]{1,0:T(8,128)S(1)} %get-tuple-element.15), channel_id=1, source_target_pairs={{0,3},{1,4},{2,5},{3,6},{4,7},{5,8},{6,9},{7,10},{8,11},{9,12},{10... | collective-permute-start | bytes 786440 | tf_op jit(solution)/shard_map/ppermute | solution.py:10
  90.0 2.2 %collective-permute-start.5 = (f32[256,256]{1,0:T(8,128)S(1)}, f32[256,256]{1,0:T(8,128)S(1)}, u32[]{:S(2)}, u32[]{:S(2)}) collective-permute-start(f32[256,256]{1,0:T(8,128)S(1)} %get-tuple-element.14), channel_id=1, source_target_pairs={{0,2},{1,3},{2,4},{3,5},{4,6},{5,7},{6,8},{7,9},{8,10},{9,11},{10,... | collective-permute-start | bytes 786440 | tf_op jit(solution)/shard_map/ppermute | solution.py:10
  92.2 1.0 bitcast_dynamic-update-slice_fusion.13
  93.2 1.4 collective-permute-start.6
  95.7 1.3 collective-permute-start.7
  98.0 1.3 collective-permute-start.8
  100.2 1.3 collective-permute-start.9
  102.5 1.3 collective-permute-start.10
  103.9 1.3 collective-permute-start.11
  105.2 1.0 fusion.14
  106.2 1.3 collective-permute-start.12
  107.5 2.9 %collective-permute-done.8 = f32[256,256]{1,0:T(8,128)S(1)} collective-permute-done((f32[256,256]{1,0:T(8,128)S(1)}, f32[256,256]{1,0:T(8,128)S(1)}, u32[]{:S(2)}, u32[]{:S(2)}) %collective-permute-start.8) | collective-permute-done | bytes 262176 | tf_op jit(solution)/shard_map/ppermute | solution.py:10
  110.4 1.3 collective-permute-start.13
  111.7 1.1 collective-permute-done.9
  112.8 11.3 %collective-permute-done.10 = f32[256,256]{1,0:T(8,128)S(1)} collective-permute-done((f32[256,256]{1,0:T(8,128)S(1)}, f32[256,256]{1,0:T(8,128)S(1)}, u32[]{:S(2)}, u32[]{:S(2)}) %collective-permute-start.10) | collective-permute-done | bytes 262176 | tf_op jit(solution)/shard_map/ppermute | solution.py:10
  124.1 1.6 collective-permute-done.11
  125.8 2.9 %collective-permute-done.12 = f32[256,256]{1,0:T(8,128)S(1)} collective-permute-done((f32[256,256]{1,0:T(8,128)S(1)}, f32[256,256]{1,0:T(8,128)S(1)}, u32[]{:S(2)}, u32[]{:S(2)}) %collective-permute-start.12) | collective-permute-done | bytes 262176 | tf_op jit(solution)/shard_map/ppermute | solution.py:10
  128.6 3.6 %collective-permute-done.13 = f32[256,256]{1,0:T(8,128)S(1)} collective-permute-done((f32[256,256]{1,0:T(8,128)S(1)}, f32[256,256]{1,0:T(8,128)S(1)}, u32[]{:S(2)}, u32[]{:S(2)}) %collective-permute-start.13) | collective-permute-done | bytes 262176 | tf_op jit(solution)/shard_map/ppermute | solution.py:10
  132.3 3.5 %fusion.8 = (f32[]{:T(128)}, f32[1,15,256,256]{2,3,1,0:T(8,128)}) fusion(f32[1,15,256,256]{2,3,1,0:T(8,128)S(1)} %copy-done.4, f32[15,256]{1,0:T(8,128)S(1)} %stack.123, f32[256]{0:T(256)S(1)} %bitcast.157, f32[15,256,256]{1,2,0:T(8,128)S(1)} %bitcast_dynamic-update-slice_fusion, f32[15,256,256]{1,2,0:T(8,128)S(1)} %copy-done.3, ...), kind=kLoop, calls=%fused_computation.10 | loop fusion | flops 6881279 | bytes 15745043 | tf_op jit(solution)/shard_map/reduce_sum | solution.py:50
  135.8 5.4 %copy.10 = f32[1,15,256,256]{3,2,1,0:T(8,128)} copy(f32[1,15,256,256]{2,3,1,0:T(8,128)} %get-tuple-element.5) | data formatting | bytes 7864320
  141.3 48.4 %psum.7 = f32[]{:T(128)} all-reduce(f32[]{:T(128)} %get-tuple-element.4), channel_id=1, replica_groups=mesh['mol'=2,'row'=16] {'row'}, use_global_device_ids=true, to_apply=%region_1.2 | all-reduce | flops 1 | bytes 8 | tf_op jit(solution)/shard_map/psum | solution.py:51
  (48 shorter events, 4.3 us)
Async XLA Ops:
  0.6 7.5 %copy-start.1 = (f32[1,15,256,256]{3,2,1,0:T(8,128)S(1)}, f32[1,15,256,256]{3,2,1,0:T(8,128)}, u32[]{:S(2)}) copy-start(f32[1,15,256,256]{3,2,1,0:T(8,128)} %param.4) | copy-start | bytes 11796484
  0.6 7.5 %copy-start = (f32[1,15,256,256]{3,2,1,0:T(8,128)S(1)}, f32[1,15,256,256]{3,2,1,0:T(8,128)}, u32[]{:S(2)}) copy-start(f32[1,15,256,256]{3,2,1,0:T(8,128)} %param.5) | copy-start | bytes 11796484
  16.8 1.9 copy-start.2
  18.6 7.1 %copy-start.5 = (f32[1,256]{1,0:T(1,128)S(1)}, f32[1,256]{1,0:T(1,128)}, u32[]{:S(2)}) copy-start(f32[1,256]{1,0:T(1,128)} %param.6) | copy-start | bytes 3076
  18.6 48.0 %copy-start.6 = (s32[1,15]{1,0:T(1,128)S(1)}, s32[1,15]{1,0:T(1,128)}, u32[]{:S(2)}) copy-start(s32[1,15]{1,0:T(1,128)} %param.7) | copy-start | bytes 184
  19.7 70.3 %collective-permute-start = (f32[256,256]{1,0:T(8,128)}, f32[256,256]{1,0:T(8,128)}, u32[]{:S(2)}, u32[]{:S(2)}) collective-permute-start(f32[256,256]{1,0:T(8,128)} %get-tuple-element.19), channel_id=1, source_target_pairs={{0,7},{1,8},{2,9},{3,10},{4,11},{5,12},{6,13},{7,14},{8,15},{16,23... | collective-permute-start | bytes 786440 | tf_op jit(solution)/shard_map/ppermute | solution.py:10
  25.7 8.6 %collective-permute-start.14 = (f32[256]{0:T(256)S(1)}, f32[256]{0:T(256)S(1)}, u32[]{:S(2)}, u32[]{:S(2)}) collective-permute-start(f32[256]{0:T(256)S(1)} %bitcast.143), channel_id=1, source_target_pairs={{0,7},{1,8},{2,9},{3,10},{4,11},{5,12},{6,13},{7,14},{8,15},{16,23... | collective-permute-start | bytes 3080 | tf_op jit(solution)/shard_map/ppermute | solution.py:10
  29.8 8.0 %collective-permute-start.15 = (f32[256]{0:T(256)S(1)}, f32[256]{0:T(256)S(1)}, u32[]{:S(2)}, u32[]{:S(2)}) collective-permute-start(f32[256]{0:T(256)S(1)} %bitcast.144), channel_id=1, source_target_pairs={{0,6},{1,7},{2,8},{3,9},{4,10},{5,11},{6,12},{7,13},{8,14},{9,15},... | collective-permute-start | bytes 3080 | tf_op jit(solution)/shard_map/ppermute | solution.py:10
  31.5 9.9 %collective-permute-start.16 = (f32[256]{0:T(256)S(1)}, f32[256]{0:T(256)S(1)}, u32[]{:S(2)}, u32[]{:S(2)}) collective-permute-start(f32[256]{0:T(256)S(1)} %bitcast.145), channel_id=1, source_target_pairs={{0,5},{1,6},{2,7},{3,8},{4,9},{5,10},{6,11},{7,12},{8,13},{9,14},{... | collective-permute-start | bytes 3080 | tf_op jit(solution)/shard_map/ppermute | solution.py:10
  32.8 13.5 %collective-permute-start.17 = (f32[256]{0:T(256)S(1)}, f32[256]{0:T(256)S(1)}, u32[]{:S(2)}, u32[]{:S(2)}) collective-permute-start(f32[256]{0:T(256)S(1)} %bitcast.146), channel_id=1, source_target_pairs={{0,4},{1,5},{2,6},{3,7},{4,8},{5,9},{6,10},{7,11},{8,12},{9,13},{1... | collective-permute-start | bytes 3080 | tf_op jit(solution)/shard_map/ppermute | solution.py:10
  34.3 13.2 %collective-permute-start.18 = (f32[256]{0:T(256)S(1)}, f32[256]{0:T(256)S(1)}, u32[]{:S(2)}, u32[]{:S(2)}) collective-permute-start(f32[256]{0:T(256)S(1)} %bitcast.147), channel_id=1, source_target_pairs={{0,3},{1,4},{2,5},{3,6},{4,7},{5,8},{6,9},{7,10},{8,11},{9,12},{10... | collective-permute-start | bytes 3080 | tf_op jit(solution)/shard_map/ppermute | solution.py:10
  37.8 11.1 %collective-permute-start.19 = (f32[256]{0:T(256)S(1)}, f32[256]{0:T(256)S(1)}, u32[]{:S(2)}, u32[]{:S(2)}) collective-permute-start(f32[256]{0:T(256)S(1)} %bitcast.148), channel_id=1, source_target_pairs={{0,2},{1,3},{2,4},{3,5},{4,6},{5,7},{6,8},{7,9},{8,10},{9,11},{10,... | collective-permute-start | bytes 3080 | tf_op jit(solution)/shard_map/ppermute | solution.py:10
  41.4 8.8 %collective-permute-start.20 = (f32[256]{0:T(256)S(1)}, f32[256]{0:T(256)S(1)}, u32[]{:S(2)}, u32[]{:S(2)}) collective-permute-start(f32[256]{0:T(256)S(1)} %bitcast.149), channel_id=1, source_target_pairs={{0,1},{1,2},{2,3},{3,4},{4,5},{5,6},{6,7},{7,8},{8,9},{9,10},{10,1... | collective-permute-start | bytes 3080 | tf_op jit(solution)/shard_map/ppermute | solution.py:10
  46.3 5.2 %collective-permute-start.21 = (f32[256]{0:T(256)S(1)}, f32[256]{0:T(256)S(1)}, u32[]{:S(2)}, u32[]{:S(2)}) collective-permute-start(f32[256]{0:T(256)S(1)} %bitcast.150), channel_id=1, source_target_pairs={{1,0},{2,1},{3,2},{4,3},{5,4},{6,5},{7,6},{8,7},{9,8},{10,9},{11,1... | collective-permute-start | bytes 3080 | tf_op jit(solution)/shard_map/ppermute | solution.py:10
  47.6 7.2 %collective-permute-start.22 = (f32[256]{0:T(256)S(1)}, f32[256]{0:T(256)S(1)}, u32[]{:S(2)}, u32[]{:S(2)}) collective-permute-start(f32[256]{0:T(256)S(1)} %bitcast.151), channel_id=1, source_target_pairs={{2,0},{3,1},{4,2},{5,3},{6,4},{7,5},{8,6},{9,7},{10,8},{11,9},{12,... | collective-permute-start | bytes 3080 | tf_op jit(solution)/shard_map/ppermute | solution.py:10
  48.9 7.2 %collective-permute-start.23 = (f32[256]{0:T(256)S(1)}, f32[256]{0:T(256)S(1)}, u32[]{:S(2)}, u32[]{:S(2)}) collective-permute-start(f32[256]{0:T(256)S(1)} %bitcast.152), channel_id=1, source_target_pairs={{3,0},{4,1},{5,2},{6,3},{7,4},{8,5},{9,6},{10,7},{11,8},{12,9},{13... | collective-permute-start | bytes 3080 | tf_op jit(solution)/shard_map/ppermute | solution.py:10
  50.2 9.9 %collective-permute-start.24 = (f32[256]{0:T(256)S(1)}, f32[256]{0:T(256)S(1)}, u32[]{:S(2)}, u32[]{:S(2)}) collective-permute-start(f32[256]{0:T(256)S(1)} %bitcast.153), channel_id=1, source_target_pairs={{4,0},{5,1},{6,2},{7,3},{8,4},{9,5},{10,6},{11,7},{12,8},{13,9},{1... | collective-permute-start | bytes 3080 | tf_op jit(solution)/shard_map/ppermute | solution.py:10
  51.5 26.1 %collective-permute-start.25 = (f32[256]{0:T(256)S(1)}, f32[256]{0:T(256)S(1)}, u32[]{:S(2)}, u32[]{:S(2)}) collective-permute-start(f32[256]{0:T(256)S(1)} %bitcast.154), channel_id=1, source_target_pairs={{5,0},{6,1},{7,2},{8,3},{9,4},{10,5},{11,6},{12,7},{13,8},{14,9},{... | collective-permute-start | bytes 3080 | tf_op jit(solution)/shard_map/ppermute | solution.py:10
  54.7 27.3 %collective-permute-start.26 = (f32[256]{0:T(256)S(1)}, f32[256]{0:T(256)S(1)}, u32[]{:S(2)}, u32[]{:S(2)}) collective-permute-start(f32[256]{0:T(256)S(1)} %bitcast.155), channel_id=1, source_target_pairs={{6,0},{7,1},{8,2},{9,3},{10,4},{11,5},{12,6},{13,7},{14,8},{15,9},... | collective-permute-start | bytes 3080 | tf_op jit(solution)/shard_map/ppermute | solution.py:10
  56.1 31.2 %collective-permute-start.27 = (f32[256]{0:T(256)S(1)}, f32[256]{0:T(256)S(1)}, u32[]{:S(2)}, u32[]{:S(2)}) collective-permute-start(f32[256]{0:T(256)S(1)} %bitcast.156), channel_id=1, source_target_pairs={{7,0},{8,1},{9,2},{10,3},{11,4},{12,5},{13,6},{14,7},{15,8},{23,16... | collective-permute-start | bytes 3080 | tf_op jit(solution)/shard_map/ppermute | solution.py:10
  60.1 33.2 %collective-permute-start.1 = (f32[256,256]{1,0:T(8,128)S(1)}, f32[256,256]{1,0:T(8,128)}, u32[]{:S(2)}, u32[]{:S(2)}) collective-permute-start(f32[256,256]{1,0:T(8,128)S(1)} %get-tuple-element.18), channel_id=1, source_target_pairs={{0,6},{1,7},{2,8},{3,9},{4,10},{5,11},{6,12},{7,13},{8,14},{9,15},... | collective-permute-start | bytes 786440 | tf_op jit(solution)/shard_map/ppermute | solution.py:10
  77.6 18.1 %collective-permute-start.2 = (f32[256,256]{1,0:T(8,128)S(1)}, f32[256,256]{1,0:T(8,128)}, u32[]{:S(2)}, u32[]{:S(2)}) collective-permute-start(f32[256,256]{1,0:T(8,128)S(1)} %get-tuple-element.17), channel_id=1, source_target_pairs={{0,5},{1,6},{2,7},{3,8},{4,9},{5,10},{6,11},{7,12},{8,13},{9,14},{... | collective-permute-start | bytes 786440 | tf_op jit(solution)/shard_map/ppermute | solution.py:10
  82.1 15.9 %collective-permute-start.3 = (f32[256,256]{1,0:T(8,128)S(1)}, f32[256,256]{1,0:T(8,128)}, u32[]{:S(2)}, u32[]{:S(2)}) collective-permute-start(f32[256,256]{1,0:T(8,128)S(1)} %get-tuple-element.16), channel_id=1, source_target_pairs={{0,4},{1,5},{2,6},{3,7},{4,8},{5,9},{6,10},{7,11},{8,12},{9,13},{1... | collective-permute-start | bytes 786440 | tf_op jit(solution)/shard_map/ppermute | solution.py:10
  87.4 12.9 %collective-permute-start.4 = (f32[256,256]{1,0:T(8,128)S(1)}, f32[256,256]{1,0:T(8,128)}, u32[]{:S(2)}, u32[]{:S(2)}) collective-permute-start(f32[256,256]{1,0:T(8,128)S(1)} %get-tuple-element.15), channel_id=1, source_target_pairs={{0,3},{1,4},{2,5},{3,6},{4,7},{5,8},{6,9},{7,10},{8,11},{9,12},{10... | collective-permute-start | bytes 786440 | tf_op jit(solution)/shard_map/ppermute | solution.py:10
  90.0 42.3 %copy-start.3 = (f32[15,256,256]{1,2,0:T(8,128)S(1)}, f32[15,256,256]{1,2,0:T(8,128)}, u32[]{:S(2)}) copy-start(f32[15,256,256]{1,2,0:T(8,128)} %copy.9) | copy-start | bytes 11796484
  90.0 42.3 %copy-start.4 = (f32[1,15,256,256]{2,3,1,0:T(8,128)S(1)}, f32[1,15,256,256]{2,3,1,0:T(8,128)}, u32[]{:S(2)}) copy-start(f32[1,15,256,256]{2,3,1,0:T(8,128)} %copy.6) | copy-start | bytes 11796484
  90.0 12.5 %collective-permute-start.5 = (f32[256,256]{1,0:T(8,128)S(1)}, f32[256,256]{1,0:T(8,128)S(1)}, u32[]{:S(2)}, u32[]{:S(2)}) collective-permute-start(f32[256,256]{1,0:T(8,128)S(1)} %get-tuple-element.14), channel_id=1, source_target_pairs={{0,2},{1,3},{2,4},{3,5},{4,6},{5,7},{6,8},{7,9},{8,10},{9,11},{10,... | collective-permute-start | bytes 786440 | tf_op jit(solution)/shard_map/ppermute | solution.py:10
  93.2 10.6 %collective-permute-start.6 = (f32[256,256]{1,0:T(8,128)S(1)}, f32[256,256]{1,0:T(8,128)S(1)}, u32[]{:S(2)}, u32[]{:S(2)}) collective-permute-start(f32[256,256]{1,0:T(8,128)S(1)} %get-tuple-element.13), channel_id=1, source_target_pairs={{0,1},{1,2},{2,3},{3,4},{4,5},{5,6},{6,7},{7,8},{8,9},{9,10},{10,1... | collective-permute-start | bytes 786440 | tf_op jit(solution)/shard_map/ppermute | solution.py:10
  95.7 10.5 %collective-permute-start.7 = (f32[256,256]{1,0:T(8,128)S(1)}, f32[256,256]{1,0:T(8,128)S(1)}, u32[]{:S(2)}, u32[]{:S(2)}) collective-permute-start(f32[256,256]{1,0:T(8,128)S(1)} %get-tuple-element.12), channel_id=1, source_target_pairs={{1,0},{2,1},{3,2},{4,3},{5,4},{6,5},{7,6},{8,7},{9,8},{10,9},{11,1... | collective-permute-start | bytes 786440 | tf_op jit(solution)/shard_map/ppermute | solution.py:10
  98.0 12.4 %collective-permute-start.8 = (f32[256,256]{1,0:T(8,128)S(1)}, f32[256,256]{1,0:T(8,128)S(1)}, u32[]{:S(2)}, u32[]{:S(2)}) collective-permute-start(f32[256,256]{1,0:T(8,128)S(1)} %get-tuple-element.11), channel_id=1, source_target_pairs={{2,0},{3,1},{4,2},{5,3},{6,4},{7,5},{8,6},{9,7},{10,8},{11,9},{12,... | collective-permute-start | bytes 786440 | tf_op jit(solution)/shard_map/ppermute | solution.py:10
  100.2 12.5 %collective-permute-start.9 = (f32[256,256]{1,0:T(8,128)S(1)}, f32[256,256]{1,0:T(8,128)S(1)}, u32[]{:S(2)}, u32[]{:S(2)}) collective-permute-start(f32[256,256]{1,0:T(8,128)S(1)} %get-tuple-element.10), channel_id=1, source_target_pairs={{3,0},{4,1},{5,2},{6,3},{7,4},{8,5},{9,6},{10,7},{11,8},{12,9},{13... | collective-permute-start | bytes 786440 | tf_op jit(solution)/shard_map/ppermute | solution.py:10
  102.5 21.6 %collective-permute-start.10 = (f32[256,256]{1,0:T(8,128)S(1)}, f32[256,256]{1,0:T(8,128)S(1)}, u32[]{:S(2)}, u32[]{:S(2)}) collective-permute-start(f32[256,256]{1,0:T(8,128)S(1)} %get-tuple-element.9), channel_id=1, source_target_pairs={{4,0},{5,1},{6,2},{7,3},{8,4},{9,5},{10,6},{11,7},{12,8},{13,9},{1... | collective-permute-start | bytes 786440 | tf_op jit(solution)/shard_map/ppermute | solution.py:10
  103.9 21.9 %collective-permute-start.11 = (f32[256,256]{1,0:T(8,128)S(1)}, f32[256,256]{1,0:T(8,128)S(1)}, u32[]{:S(2)}, u32[]{:S(2)}) collective-permute-start(f32[256,256]{1,0:T(8,128)S(1)} %get-tuple-element.8), channel_id=1, source_target_pairs={{5,0},{6,1},{7,2},{8,3},{9,4},{10,5},{11,6},{12,7},{13,8},{14,9},{... | collective-permute-start | bytes 786440 | tf_op jit(solution)/shard_map/ppermute | solution.py:10
  106.2 22.4 %collective-permute-start.12 = (f32[256,256]{1,0:T(8,128)S(1)}, f32[256,256]{1,0:T(8,128)S(1)}, u32[]{:S(2)}, u32[]{:S(2)}) collective-permute-start(f32[256,256]{1,0:T(8,128)S(1)} %get-tuple-element.7), channel_id=1, source_target_pairs={{6,0},{7,1},{8,2},{9,3},{10,4},{11,5},{12,6},{13,7},{14,8},{15,9},... | collective-permute-start | bytes 786440 | tf_op jit(solution)/shard_map/ppermute | solution.py:10
  110.4 21.9 %collective-permute-start.13 = (f32[256,256]{1,0:T(8,128)S(1)}, f32[256,256]{1,0:T(8,128)S(1)}, u32[]{:S(2)}, u32[]{:S(2)}) collective-permute-start(f32[256,256]{1,0:T(8,128)S(1)} %get-tuple-element.6), channel_id=1, source_target_pairs={{7,0},{8,1},{9,2},{10,3},{11,4},{12,5},{13,6},{14,7},{15,8},{23,16... | collective-permute-start | bytes 786440 | tf_op jit(solution)/shard_map/ppermute | solution.py:10
where the time goes:
time: 193 us; the launch traced here: 191 us
  starting transfers between devices  67 us (35%)
  blocking collectives  48.4 us (25%)
  waiting for transfers between devices  28.1 us (15%)
  local copies, waits for them, and re-layouts  25.4 us (13%)
  matrix products  16.1 us (8%)
  other arithmetic  3.54 us (2%)
  between operations  2.89 us (1%)
    ppermute x28, starting transfers between devices, passed_along(): lax.ppermute(value, axis, [(source, source + steps) for source in range(f...  67 us
    psum x1, blocking collectives, per_device(): whole = lax.psum(partial_sum, 'row')  48.4 us
    ppermute x28, waiting for transfers between devices, passed_along(): lax.ppermute(value, axis, [(source, source + steps) for source in range(f...  28.1 us
    unnamed x30, local copies, waits for them, and re-layouts  18.8 us
    dot_general x1, matrix products, block_terms(): jnp.dot(amp_block, int_block, precision=hi, preferred_element_type=jnp.fl...  7.47 us
    sub x1, local copies, waits for them, and re-layouts, block_terms(): return first + second - 0.5 * third  5.46 us
    dot_general x1, matrix products, block_terms(): jnp.dot(first, amp_block.T, precision=hi, preferred_element_type=jnp.floa...  4.59 us
    dot_general x1, matrix products, block_terms(): jnp.dot(amp_block, int_block.T, precision=hi, preferred_element_type=jnp....  4.01 us
  transfers between devices with their start and end apart: 28, of which 9 were waited for; matrix products, arithmetic and copies ran while one was open for 9% of the time, Pallas kernels for 0%

commit v1 on v0

v1 whole, which is shorter than its diff:
```python
import functools

import jax
import jax.numpy as jnp
from jax import lax
from jax.experimental import pallas as pl
from jax.experimental.pallas import tpu as pltpu
from jax.sharding import PartitionSpec as P

F32 = jnp.float32
EXTRA = 8


def own_slot(reach, offset, core):
    return reach + 2 * offset


def give_slot(reach, offset, core):
    return reach + 2 * offset + 1 - 2 * core


def twin_slot(reach, core):
    return reach + 1 - 2 * core


def far_slot(reach, core):
    return 2 * reach * core


def split(value):
    high = value.astype(jnp.bfloat16)
    low = (value - high.astype(F32)).astype(jnp.bfloat16)
    return high, low


def product(left, right, dims):
    def one(a, b):
        return lax.dot_general(a, b, (dims, ((), ())), preferred_element_type=F32)

    (left_high, left_low), (right_high, right_low) = left, right
    return one(left_high, right_high) + (one(left_high, right_low) + one(left_low, right_high))


def cycle_of(amp, integ):
    amp_parts = split(amp)
    inner = product(split(integ), amp_parts, ((1,), (1,)))
    inner = integ + integ.T - 0.5 * inner
    return product(amp_parts, split(inner), ((1,), (0,)))


def pick(index, options):
    value = options[-1]
    for place in range(len(options) - 2, -1, -1):
        value = jnp.where(index == place, options[place], value)
    return value


def give_kernel(core_ref, amp_ref, int_ref, gap_ref, out_ref):
    width = amp_ref.shape[-1]
    out_ref[0, :width, :] = cycle_of(amp_ref[0, 0], int_ref[0, 0])
    out_ref[0, width:, :] = jnp.broadcast_to(gap_ref[...], (EXTRA, width))


def bundle_kernel(paired, core_ref, amp_ref, int_ref, gap_ref, twin_ref, *outs):
    width = amp_ref.shape[-1]
    height = width + EXTRA
    step = pl.program_id(0)
    cycle = cycle_of(amp_ref[0, 0], int_ref[0, 0])
    for place, out_ref in enumerate(outs):

        @pl.when(step == place)
        def _():
            out_ref[:width, :] = cycle
            out_ref[width:height, :] = jnp.broadcast_to(gap_ref[...], (EXTRA, width))
            if paired[place]:
                out_ref[height:, :] = twin_ref[0]


def update(own, arrived, integ, gap_row, gap_other, flag):
    gap_column = jnp.broadcast_to(gap_row, (8, gap_row.shape[1])).T[:, :1]
    total = integ + own + arrived.T
    fresh = total / (gap_column + gap_other)
    return jnp.where(flag > 0, fresh, F32(0.0))


def fold(value):
    return jnp.sum(value.reshape(value.shape[0] // 8, 8, value.shape[1]), axis=0)


def first_kernel(core_ref, present_ref, amp_ref, int_ref, gap_ref, own_ref, arrived_ref, out_ref, part_ref):
    width = amp_ref.shape[-1]
    slots = present_ref.shape[1]
    reach = (slots - 1) // 2
    integ = int_ref[0, 0]
    step = pl.program_id(0)

    @pl.when(step == 0)
    def _():
        cycle = cycle_of(amp_ref[0, 0], integ)
        fresh = update(cycle, cycle, integ, gap_ref[...], gap_ref[...], present_ref[0, reach])
        out_ref[0, 0] = fresh
        part_ref[...] = fold(fresh * integ)

    @pl.when(step == 1)
    def _():
        flag = present_ref[0, twin_slot(reach, core_ref[0])]
        fresh = update(
            own_ref[0, :width], arrived_ref[0, :width], integ, gap_ref[...], arrived_ref[0, width : width + 1], flag
        )
        out_ref[0, 0] = fresh
        part_ref[...] += fold(fresh * integ)


def bundle_update_kernel(
    offset, core_ref, present_ref, int_ref, gap_ref, own_ref, given_ref, arrived_ref, before_ref, part_in_ref, out_ref, part_ref
):
    width = int_ref.shape[-1]
    reach = (present_ref.shape[1] - 1) // 2
    integ = int_ref[0, 0]
    step = pl.program_id(0)

    def one(own, slot, part):
        fresh = update(
            own, arrived_ref[:width], integ, gap_ref[...], arrived_ref[width : width + 1], present_ref[0, slot]
        )
        out_ref[0, 0] = fresh
        part_ref[...] = part + fold(fresh * integ)

    @pl.when(step == 0)
    def _():
        one(own_ref[:width], own_slot(reach, -offset, core_ref[0]), part_in_ref[...])

    @pl.when(step == 1)
    def _():
        one(given_ref[0, :width], give_slot(reach, -offset, core_ref[0]), part_ref[...])


def far_update_kernel(
    core_ref, present_ref, int_ref, gap_ref, own_ref, arrived_ref, before_ref, part_in_ref, out_ref, part_ref
):
    width = int_ref.shape[-1]
    reach = (present_ref.shape[1] - 1) // 2
    integ = int_ref[0, 0]
    fresh = update(
        own_ref[:width],
        arrived_ref[:width],
        integ,
        gap_ref[...],
        arrived_ref[width : width + 1],
        present_ref[0, far_slot(reach, core_ref[0])],
    )
    out_ref[0, 0] = fresh
    part_ref[...] = part_in_ref[...] + fold(fresh * integ)


def cost(blocks, width, products):
    return pl.CostEstimate(
        flops=blocks * products * 2 * width**3, bytes_accessed=blocks * 4 * 4 * width**2, transcendentals=0
    )


PARAMS = pltpu.CompilerParams(vmem_limit_bytes=32 * 1024 * 1024)


def per_device(amplitude, integral, pair_gap, present):
    slots, width = amplitude.shape[1], amplitude.shape[2]
    reach = (slots - 1) // 2
    height = width + EXTRA
    count = lax.axis_size("row")
    core = jnp.reshape(lax.rem(lax.axis_index("row"), 2), (1,)).astype(jnp.int32)

    def slot_spec(choose):
        return pl.BlockSpec((1, 1, width, width), lambda k, core_ref, *_: (0, choose(k, core_ref[0]), 0, 0))

    def whole(shape):
        return pl.BlockSpec(shape, lambda k, *_: (0,) * len(shape))

    gap_spec = whole((1, width))

    def shape(*dims):
        return jax.ShapeDtypeStruct(dims, F32)

    def gives(offsets, with_twin):
        def choose(k, c):
            options = [give_slot(reach, offset, c) for offset in offsets]
            return pick(k, options + ([twin_slot(reach, c)] if with_twin else []))

        blocks = len(offsets) + int(with_twin)
        return pl.pallas_call(
            give_kernel,
            grid_spec=pltpu.PrefetchScalarGridSpec(
                num_scalar_prefetch=1,
                grid=(blocks,),
                in_specs=[slot_spec(choose), slot_spec(choose), gap_spec],
                out_specs=pl.BlockSpec((1, height, width), lambda k, *_: (k, 0, 0)),
            ),
            out_shape=shape(blocks, height, width),
            compiler_params=PARAMS,
            cost_estimate=cost(blocks, width, 6),
            name="give_blocks",
        )(core, amplitude, integral, pair_gap)

    def bundles(offsets, with_far, swapped):
        def choose(k, c):
            options = [own_slot(reach, offset, c) for offset in offsets]
            return pick(k, options + ([far_slot(reach, c)] if with_far else []))

        paired = [True] * len(offsets) + [False] * int(with_far)
        heights = [2 * height if p else height for p in paired]
        return pl.pallas_call(
            functools.partial(bundle_kernel, paired),
            grid_spec=pltpu.PrefetchScalarGridSpec(
                num_scalar_prefetch=1,
                grid=(len(paired),),
                in_specs=[
                    slot_spec(choose),
                    slot_spec(choose),
                    gap_spec,
                    pl.BlockSpec((1, height, width), lambda k, *_: (jnp.minimum(k, len(offsets) - 1), 0, 0)),
                ],
                out_specs=[whole((h, width)) for h in heights],
            ),
            out_shape=[shape(h, width) for h in heights],
            compiler_params=PARAMS,
            cost_estimate=cost(len(paired), width, 6),
            name="bundles",
        )(core, amplitude, integral, pair_gap, swapped)

    def swap(value):
        return lax.ppermute(value, "row", [(place, place ^ 1) for place in range(count)])

    def along(value, steps):
        return lax.ppermute(
            value, "row", [(place, place + steps) for place in range(count) if 0 <= place + steps < count]
        )

    top = (reach - 1) // 2
    early = [2, -2]
    late = [3, -3, 1, -1]
    given_early = gives(early, False)
    swapped_early = swap(given_early)
    given_late = gives(late, True)
    swapped_late = swap(given_late)
    sent = dict(zip(early, bundles(early, False, swapped_early)))
    arrived = {offset: along(sent[offset], 2 * offset) for offset in early}
    *late_bundles, far = bundles(late, True, swapped_late)
    sent.update(zip(late, late_bundles))
    for offset in late:
        arrived[offset] = along(sent[offset], 2 * offset)
    far_pairs = [(place, place + reach) for place in range(1, count - reach, 2)]
    far_pairs += [(place, place - reach) for place in range(reach + 1, count, 2)]
    arrived_far = lax.ppermute(far, "row", far_pairs)
    given = {offset: (given_early, place) for place, offset in enumerate(early)}
    given.update({offset: (given_late, place) for place, offset in enumerate(late)})

    out_shape = [shape(1, slots, width, width), shape(8, width)]
    twin_place = len(late)
    twin_block = pl.BlockSpec((1, height, width), lambda k, *_: (twin_place, 0, 0))

    def first_choose(k, c):
        return jnp.where(k == 0, reach, twin_slot(reach, c))

    updated, part = pl.pallas_call(
        first_kernel,
        grid_spec=pltpu.PrefetchScalarGridSpec(
            num_scalar_prefetch=2,
            grid=(2,),
            in_specs=[
                slot_spec(lambda k, c: reach),
                slot_spec(first_choose),
                gap_spec,
                twin_block,
                twin_block,
            ],
            out_specs=[slot_spec(first_choose), whole((8, width))],
        ),
        out_shape=out_shape,
        compiler_params=PARAMS,
        cost_estimate=cost(2, width, 3),
        name="first_update",
    )(core, present, amplitude, integral, pair_gap, given_late, swapped_late)

    def bundle_update(offset, updated, part):
        source, place = given[-offset]

        def choose(k, c):
            return jnp.where(k == 0, own_slot(reach, -offset, c), give_slot(reach, -offset, c))

        return pl.pallas_call(
            functools.partial(bundle_update_kernel, offset),
            grid_spec=pltpu.PrefetchScalarGridSpec(
                num_scalar_prefetch=2,
                grid=(2,),
                in_specs=[
                    slot_spec(choose),
                    gap_spec,
                    whole((height, width)),
                    pl.BlockSpec((1, height, width), lambda k, *_: (place, 0, 0)),
                    pl.BlockSpec((height, width), lambda k, *_: (k, 0)),
                    pl.BlockSpec(memory_space=pl.ANY),
                    whole((8, width)),
                ],
                out_specs=[slot_spec(choose), whole((8, width))],
            ),
            out_shape=out_shape,
            input_output_aliases={7: 0},
            compiler_params=PARAMS,
            cost_estimate=cost(2, width, 0),
            name="bundle_update",
        )(core, present, integral, pair_gap, sent[-offset], source, arrived[offset], updated, part)

    for offset in early + late:
        updated, part = bundle_update(offset, updated, part)

    far_choose = lambda k, c: far_slot(reach, c)
    updated, part = pl.pallas_call(
        far_update_kernel,
        grid_spec=pltpu.PrefetchScalarGridSpec(
            num_scalar_prefetch=2,
            grid=(1,),
            in_specs=[
                slot_spec(far_choose),
                gap_spec,
                whole((height, width)),
                whole((height, width)),
                pl.BlockSpec(memory_space=pl.ANY),
                whole((8, width)),
            ],
            out_specs=[slot_spec(far_choose), whole((8, width))],
        ),
        out_shape=out_shape,
        input_output_aliases={6: 0},
        compiler_params=PARAMS,
        cost_estimate=cost(1, width, 0),
        name="far_update",
    )(core, present, integral, pair_gap, far, arrived_far, updated, part)

    summed = jnp.sum(part, axis=0).reshape(-1, 128).sum(axis=0)
    every = lax.all_to_all(jnp.broadcast_to(summed, (count, 128)), "row", 0, 0)
    blocks_all = count * amplitude.shape[0]
    energy = jnp.sum(every) / (width * width * blocks_all)
    return updated, jnp.reshape(energy, (1,))


def solution(mesh):
    in_specs = (
        P(("mol", "row"), None, None, None),
        P(("mol", "row"), None, None, None),
        P(("mol", "row"), None),
        P(("mol", "row"), None),
    )
    out_specs = (P(("mol", "row"), None, None, None), P("mol"))
    return jax.shard_map(per_device, mesh=mesh, in_specs=in_specs, out_specs=out_specs, check_vma=False)
```

time: 193 us -> 96.6 us (0.50)
  starting transfers between devices: 67 us -> 19.2 us
  blocking collectives: 48.4 us -> 19.5 us
  Pallas kernels: 0 us -> 25.3 us
  local copies, waits for them, and re-layouts: 25.4 us -> 4.92 us
  matrix products: 16.1 us -> 0 us
  waiting for transfers between devices: 28.1 us -> 24.1 us
  other arithmetic: 3.54 us -> 0.64 us
    psum x1 -> x0, blocking collectives: 48.4 us -> none  [per_device(): whole = lax.psum(partial_sum, 'row')]
    ppermute x28 -> x9, starting transfers between devices: 67 us -> 19.2 us  [the longest x6 17.7 us: along(): lax.ppermute(value, 'row', [(place, place + steps) for place in range(cou...]
    pallas_call x0 -> x12, Pallas kernels: none -> 25.3 us  [the longest x6 11.1 us: bundle_update(): pl.pallas_call(functools.partial(bundle_update_kernel, offset), grid_spec...]
    all_to_all x0 -> x1, blocking collectives: none -> 19.5 us  [per_device(): every = lax.all_to_all(jnp.broadcast_to(summed, (count, 128)), 'row', 0, 0)]
    dot_general x3 -> x0, matrix products: 16.1 us -> none  [the longest x1 7.47 us: block_terms(): jnp.dot(amp_block, int_block, precision=hi, preferred_element_type=jnp.fl...]
    unnamed x30 -> x10, local copies, waits for them, and re-layouts: 18.8 us -> 4.91 us
    sub x1 -> x0, local copies, waits for them, and re-layouts: 5.46 us -> none  [block_terms(): return first + second - 0.5 * third]
    ppermute x28 -> x9, waiting for transfers between devices: 28.1 us -> 24.1 us  [the longest x6 22.1 us: along(): lax.ppermute(value, 'row', [(place, place + steps) for place in range(cou...]
  transfers between devices with their start and end apart: 28 -> 9, of which waited for: 9 -> 3; matrix products, arithmetic and copies ran while one was open for 9% -> 0% of each run, Pallas kernels for 0% -> 21%
where the time goes in v1:
time: 96.6 us; the launch traced here: 96.2 us
  Pallas kernels  25.3 us (26%)
  waiting for transfers between devices  24.1 us (25%)
  blocking collectives  19.5 us (20%)
  starting transfers between devices  19.2 us (20%)
  local copies, waits for them, and re-layouts  4.92 us (5%)
  between operations  2.57 us (3%)
    ppermute x6, waiting for transfers between devices, along(): lax.ppermute(value, 'row', [(place, place + steps) for place in range(cou...  22.1 us
    all_to_all x1, blocking collectives, per_device(): every = lax.all_to_all(jnp.broadcast_to(summed, (count, 128)), 'row', 0, 0)  19.5 us
    ppermute x6, starting transfers between devices, along(): lax.ppermute(value, 'row', [(place, place + steps) for place in range(cou...  17.7 us
    pallas_call x6, Pallas kernels, bundle_update(): pl.pallas_call(functools.partial(bundle_update_kernel, offset), grid_spec...  11.1 us
    pallas_call x2, Pallas kernels, bundles(): pl.pallas_call(functools.partial(bundle_kernel, paired), grid_spec=pltpu....  5.32 us
    pallas_call x2, Pallas kernels, gives(): pl.pallas_call(give_kernel, grid_spec=pltpu.PrefetchScalarGridSpec(num_sc...  5 us
    unnamed x10, local copies, waits for them, and re-layouts  4.91 us
    pallas_call x1, Pallas kernels, per_device(): pl.pallas_call(first_kernel, grid_spec=pltpu.PrefetchScalarGridSpec(num_s...  2.41 us
  transfers between devices with their start and end apart: 9, of which 3 were waited for; matrix products, arithmetic and copies ran while one was open for 0% of the time, Pallas kernels for 21%

profile of v1, /device:TPU:0, one launch (start us, length us, event | category | flops | bytes accessed | tf_op | source)
XLA Modules:
  0.0 96.2 jit_solution(11543918254294018922)
XLA Ops:
  0.6 0.0 copy-start
  0.6 2.1 %copy-done = f32[1,15,256,256]{3,2,1,0:T(8,128)S(1)} copy-done((f32[1,15,256,256]{3,2,1,0:T(8,128)S(1)}, f32[1,15,256,256]{3,2,1,0:T(8,128)}, u32[]{:S(2)}) %copy-start) | copy-done | bytes 3932184
  2.8 0.0 copy-start.2
  2.8 2.1 %copy-done.2 = f32[1,15,256,256]{3,2,1,0:T(8,128)S(1)} copy-done((f32[1,15,256,256]{3,2,1,0:T(8,128)S(1)}, f32[1,15,256,256]{3,2,1,0:T(8,128)}, u32[]{:S(2)}) %copy-start.2) | copy-done | bytes 3932184
  4.9 0.0 copy-start.3
  4.9 0.7 copy-done.3
  5.5 3.6 %give_blocks.2.own_ref.given_ref = f32[5,264,256]{2,1,0:T(8,128)S(1)} custom-call(s32[1]{0:T(128)} %bitcast.core_ref, f32[1,15,256,256]{3,2,1,0:T(8,128)S(1)} %copy-done.2, f32[1,15,256,256]{3,2,1,0:T(8,128)S(1)} %copy-done, f32[1,256]{1,0:T(1,128)S(1)} %copy-done.3), custom_call_target="tpu_custom_call" | custom-call | flops 1006632960 | bytes 5242880 | tf_op jit(solution)/shard_map/give_blocks/pallas_call | solution.py:189
  9.1 0.5 collective-permute-start
  9.6 1.4 %give_blocks.3.given_ref = f32[2,264,256]{2,1,0:T(8,128)S(1)} custom-call(s32[1]{0:T(128)} %bitcast.core_ref, f32[1,15,256,256]{3,2,1,0:T(8,128)S(1)} %copy-done.2, f32[1,15,256,256]{3,2,1,0:T(8,128)S(1)} %copy-done, f32[1,256]{1,0:T(1,128)S(1)} %copy-done.3), custom_call_target="tpu_custom_call" | custom-call | flops 402653184 | bytes 2097152 | tf_op jit(solution)/shard_map/give_blocks/pallas_call | solution.py:189
  11.1 0.1 collective-permute-start.6
  11.2 1.9 %collective-permute-done.6.twin_ref = f32[2,264,256]{2,1,0:T(8,128)S(1)} collective-permute-done((f32[2,264,256]{2,1,0:T(8,128)S(1)}, f32[2,264,256]{2,1,0:T(8,128)S(1)}, u32[]{:S(2)}, u32[]{:S(2)}) %collective-permute-start.6) | collective-permute-done | bytes 540704 | tf_op jit(solution)/shard_map/ppermute | solution.py:230
  13.1 1.5 %bundles.3 = (f32[528,256]{1,0:T(8,128)S(1)}, f32[528,256]{1,0:T(8,128)S(1)}) custom-call(s32[1]{0:T(128)} %bitcast.core_ref, f32[1,15,256,256]{3,2,1,0:T(8,128)S(1)} %copy-done.2, f32[1,15,256,256]{3,2,1,0:T(8,128)S(1)} %copy-done, f32[1,256]{1,0:T(1,128)S(1)} %copy-done.3, f32[2,264,256]{2,1,0:T(8,128)S(1)} %collective-permute-done.6.twin_ref), custom_call_target="tpu_custom_call" | custom-call | flops 402653184 | bytes 2097152 | tf_op jit(solution)/shard_map/bundles/pallas_call | solution.py:210
  14.6 4.9 %collective-permute-start.8 = (f32[528,256]{1,0:T(8,128)S(1)}, f32[528,256]{1,0:T(8,128)S(1)}, u32[]{:S(2)}, u32[]{:S(2)}) collective-permute-start(f32[528,256]{1,0:T(8,128)S(1)} %get-tuple-element.30.own_ref), channel_id=1, source_target_pairs={{0,4},{1,5},{2,6},{3,7},{4,8},{5,9},{6,10},{7,11},{8,12},{9,13},{1... | collective-permute-start | bytes 1622024 | tf_op jit(solution)/shard_map/ppermute | solution.py:233
  19.5 0.0 copy-start.4
  19.5 1.3 %collective-permute-start.7 = (f32[528,256]{1,0:T(8,128)S(1)}, f32[528,256]{1,0:T(8,128)S(1)}, u32[]{:S(2)}, u32[]{:S(2)}) collective-permute-start(f32[528,256]{1,0:T(8,128)S(1)} %get-tuple-element.31.own_ref), channel_id=1, source_target_pairs={{4,0},{5,1},{6,2},{7,3},{8,4},{9,5},{10,6},{11,7},{12,8},{13,9},{1... | collective-permute-start | bytes 1622024 | tf_op jit(solution)/shard_map/ppermute | solution.py:233
  20.8 0.0 collective-permute-done.twin_ref.arrived_ref
  20.9 3.8 %bundles.2 = (f32[528,256]{1,0:T(8,128)S(1)}, f32[528,256]{1,0:T(8,128)S(1)}, f32[528,256]{1,0:T(8,128)S(1)}, f32[528,256]{1,0:T(8,128)S(1)}, f32[264,256]{1,0:T(8,128)S(1)}) custom-call(s32[1]{0:T(128)} %bitcast.core_ref, f32[1,15,256,256]{3,2,1,0:T(8,128)S(1)} %copy-done.2, f32[1,15,256,256]{3,2,1,0:T(8,128)S(1)} %copy-done, f32[1,256]{1,0:T(1,128)S(1)} %copy-done.3, ...), custom_call_target="tpu_custom_call" | custom-call | flops 1006632960 | bytes 5242880 | tf_op jit(solution)/shard_map/bundles/pallas_call | solution.py:210
  24.7 5.5 %collective-permute-start.5 = (f32[528,256]{1,0:T(8,128)S(1)}, f32[528,256]{1,0:T(8,128)S(1)}, u32[]{:S(2)}, u32[]{:S(2)}) collective-permute-start(f32[528,256]{1,0:T(8,128)S(1)} %get-tuple-element.28.own_ref), channel_id=1, source_target_pairs={{0,6},{1,7},{2,8},{3,9},{4,10},{5,11},{6,12},{7,13},{8,14},{9,15},... | collective-permute-start | bytes 1622024 | tf_op jit(solution)/shard_map/ppermute | solution.py:233
  30.2 1.3 %collective-permute-start.4 = (f32[528,256]{1,0:T(8,128)S(1)}, f32[528,256]{1,0:T(8,128)S(1)}, u32[]{:S(2)}, u32[]{:S(2)}) collective-permute-start(f32[528,256]{1,0:T(8,128)S(1)} %get-tuple-element.29.own_ref), channel_id=1, source_target_pairs={{6,0},{7,1},{8,2},{9,3},{10,4},{11,5},{12,6},{13,7},{14,8},{15,9},... | collective-permute-start | bytes 1622024 | tf_op jit(solution)/shard_map/ppermute | solution.py:233
  31.5 3.4 %collective-permute-start.3 = (f32[528,256]{1,0:T(8,128)S(1)}, f32[528,256]{1,0:T(8,128)S(1)}, u32[]{:S(2)}, u32[]{:S(2)}) collective-permute-start(f32[528,256]{1,0:T(8,128)S(1)} %get-tuple-element.26.own_ref), channel_id=1, source_target_pairs={{0,2},{1,3},{2,4},{3,5},{4,6},{5,7},{6,8},{7,9},{8,10},{9,11},{10,... | collective-permute-start | bytes 1622024 | tf_op jit(solution)/shard_map/ppermute | solution.py:233
  35.0 0.0 collective-permute-done.8.arrived_ref
  35.0 1.3 %collective-permute-start.2 = (f32[528,256]{1,0:T(8,128)S(1)}, f32[528,256]{1,0:T(8,128)S(1)}, u32[]{:S(2)}, u32[]{:S(2)}) collective-permute-start(f32[528,256]{1,0:T(8,128)S(1)} %get-tuple-element.27.own_ref), channel_id=1, source_target_pairs={{2,0},{3,1},{4,2},{5,3},{6,4},{7,5},{8,6},{9,7},{10,8},{11,9},{12,... | collective-permute-start | bytes 1622024 | tf_op jit(solution)/shard_map/ppermute | solution.py:233
  36.3 0.0 collective-permute-done.7.arrived_ref
  36.3 0.0 copy-start.1
  36.3 0.8 collective-permute-start.1
  37.1 0.0 copy-done.4
  37.1 2.4 %first_update.1 = (f32[1,15,256,256]{3,2,1,0:T(8,128)}, f32[8,256]{1,0:T(8,128)S(1)}) custom-call(s32[1]{0:T(128)} %bitcast.core_ref, s32[1,15]{1,0:T(1,128)S(1)} %copy-done.4, f32[1,15,256,256]{3,2,1,0:T(8,128)S(1)} %copy-done.2, f32[1,15,256,256]{3,2,1,0:T(8,128)S(1)} %copy-done, f32[1,256]{1,0:T(1,128)S(1)} %copy-done.3, ...), custom_call_target="tpu_custom_call" | custom-call | flops 201326592 | bytes 2097152 | tf_op jit(solution)/shard_map/first_update/pallas_call | solution.py:263
  39.5 0.0 copy-done.1
  39.5 1.9 %bundle_update.6 = (f32[1,15,256,256]{3,2,1,0:T(8,128)}, f32[8,256]{1,0:T(8,128)S(1)}) custom-call(s32[1]{0:T(128)} %bitcast.core_ref, s32[1,15]{1,0:T(1,128)S(1)} %copy-done.4, f32[1,15,256,256]{3,2,1,0:T(8,128)S(1)} %copy-done.1, f32[1,256]{1,0:T(1,128)S(1)} %copy-done.3, ...), custom_call_target="tpu_custom_call", output_to_operand_aliasing={{0}: (7, {})} | custom-call | bytes 2097152 | tf_op jit(solution)/shard_map/bundle_update/pallas_call | solution.py:289
  41.4 1.9 %bundle_update.7 = (f32[1,15,256,256]{3,2,1,0:T(8,128)}, f32[8,256]{1,0:T(8,128)S(1)}) custom-call(s32[1]{0:T(128)} %bitcast.core_ref, s32[1,15]{1,0:T(1,128)S(1)} %copy-done.4, f32[1,15,256,256]{3,2,1,0:T(8,128)S(1)} %copy-done.1, f32[1,256]{1,0:T(1,128)S(1)} %copy-done.3, ...), custom_call_target="tpu_custom_call", output_to_operand_aliasing={{0}: (7, {})} | custom-call | bytes 2097152 | tf_op jit(solution)/shard_map/bundle_update/pallas_call | solution.py:289
  43.2 7.5 %collective-permute-done.5.arrived_ref = f32[528,256]{1,0:T(8,128)S(1)} collective-permute-done((f32[528,256]{1,0:T(8,128)S(1)}, f32[528,256]{1,0:T(8,128)S(1)}, u32[]{:S(2)}, u32[]{:S(2)}) %collective-permute-start.5) | collective-permute-done | bytes 540704 | tf_op jit(solution)/shard_map/ppermute | solution.py:233
  50.8 1.8 %bundle_update.8 = (f32[1,15,256,256]{3,2,1,0:T(8,128)}, f32[8,256]{1,0:T(8,128)S(1)}) custom-call(s32[1]{0:T(128)} %bitcast.core_ref, s32[1,15]{1,0:T(1,128)S(1)} %copy-done.4, f32[1,15,256,256]{3,2,1,0:T(8,128)S(1)} %copy-done.1, f32[1,256]{1,0:T(1,128)S(1)} %copy-done.3, ...), custom_call_target="tpu_custom_call", output_to_operand_aliasing={{0}: (7, {})} | custom-call | bytes 2097152 | tf_op jit(solution)/shard_map/bundle_update/pallas_call | solution.py:289
  52.6 0.0 collective-permute-done.4.arrived_ref
  52.6 1.9 %bundle_update.9 = (f32[1,15,256,256]{3,2,1,0:T(8,128)}, f32[8,256]{1,0:T(8,128)S(1)}) custom-call(s32[1]{0:T(128)} %bitcast.core_ref, s32[1,15]{1,0:T(1,128)S(1)} %copy-done.4, f32[1,15,256,256]{3,2,1,0:T(8,128)S(1)} %copy-done.1, f32[1,256]{1,0:T(1,128)S(1)} %copy-done.3, ...), custom_call_target="tpu_custom_call", output_to_operand_aliasing={{0}: (7, {})} | custom-call | bytes 2097152 | tf_op jit(solution)/shard_map/bundle_update/pallas_call | solution.py:289
  54.5 14.6 %collective-permute-done.3.arrived_ref = f32[528,256]{1,0:T(8,128)S(1)} collective-permute-done((f32[528,256]{1,0:T(8,128)S(1)}, f32[528,256]{1,0:T(8,128)S(1)}, u32[]{:S(2)}, u32[]{:S(2)}) %collective-permute-start.3) | collective-permute-done | bytes 540704 | tf_op jit(solution)/shard_map/ppermute | solution.py:233
  69.1 1.8 %bundle_update.10 = (f32[1,15,256,256]{3,2,1,0:T(8,128)}, f32[8,256]{1,0:T(8,128)S(1)}) custom-call(s32[1]{0:T(128)} %bitcast.core_ref, s32[1,15]{1,0:T(1,128)S(1)} %copy-done.4, f32[1,15,256,256]{3,2,1,0:T(8,128)S(1)} %copy-done.1, f32[1,256]{1,0:T(1,128)S(1)} %copy-done.3, ...), custom_call_target="tpu_custom_call", output_to_operand_aliasing={{0}: (7, {})} | custom-call | bytes 2097152 | tf_op jit(solution)/shard_map/bundle_update/pallas_call | solution.py:289
  70.9 0.0 collective-permute-done.2.arrived_ref
  70.9 1.9 %bundle_update.11 = (f32[1,15,256,256]{3,2,1,0:T(8,128)}, f32[8,256]{1,0:T(8,128)S(1)}) custom-call(s32[1]{0:T(128)} %bitcast.core_ref, s32[1,15]{1,0:T(1,128)S(1)} %copy-done.4, f32[1,15,256,256]{3,2,1,0:T(8,128)S(1)} %copy-done.1, f32[1,256]{1,0:T(1,128)S(1)} %copy-done.3, ...), custom_call_target="tpu_custom_call", output_to_operand_aliasing={{0}: (7, {})} | custom-call | bytes 2097152 | tf_op jit(solution)/shard_map/bundle_update/pallas_call | solution.py:289
  72.8 0.0 collective-permute-done.1.arrived_ref
  72.8 1.5 %far_update.1 = (f32[1,15,256,256]{3,2,1,0:T(8,128)}, f32[8,256]{1,0:T(8,128)S(1)}) custom-call(s32[1]{0:T(128)} %bitcast.core_ref, s32[1,15]{1,0:T(1,128)S(1)} %copy-done.4, f32[1,15,256,256]{3,2,1,0:T(8,128)S(1)} %copy-done.1, f32[1,256]{1,0:T(1,128)S(1)} %copy-done.3, f32[264,256]{1,0:T(8,128)S(1)} %get-tuple-element.25.own_ref, ...), custom_call_target="tpu_custom_call", output_to_operand_aliasing={{0}: (6, {})} | custom-call | bytes 1048576 | tf_op jit(solution)/shard_map/far_update/pallas_call | solution.py:316
  74.3 19.5 %all_to_all.6 = f32[16,1,128]{2,1,0:T(1,128)S(1)} all-to-all(f32[16,1,128]{2,1,0:T(1,128)S(1)} %broadcast_in_dim.3), channel_id=1, replica_groups=mesh['mol'=2,'row'=16] {'row'}, dimensions={0} | all-to-all | bytes 16384 | tf_op jit(solution)/shard_map/all_to_all | solution.py:339
  93.9 0.6 reduce_sum.29
  (3 shorter events, 0.0 us)
Async XLA Ops:
  0.6 2.1 %copy-start = (f32[1,15,256,256]{3,2,1,0:T(8,128)S(1)}, f32[1,15,256,256]{3,2,1,0:T(8,128)}, u32[]{:S(2)}) copy-start(f32[1,15,256,256]{3,2,1,0:T(8,128)} %int_ref.23) | copy-start | bytes 11796484
  2.8 2.1 %copy-start.2 = (f32[1,15,256,256]{3,2,1,0:T(8,128)S(1)}, f32[1,15,256,256]{3,2,1,0:T(8,128)}, u32[]{:S(2)}) copy-start(f32[1,15,256,256]{3,2,1,0:T(8,128)} %amp_ref.9) | copy-start | bytes 11796484
  4.9 0.7 copy-start.3
  9.1 11.7 %collective-permute-start = (f32[5,264,256]{2,1,0:T(8,128)S(1)}, f32[5,264,256]{2,1,0:T(8,128)S(1)}, u32[]{:S(2)}, u32[]{:S(2)}) collective-permute-start(f32[5,264,256]{2,1,0:T(8,128)S(1)} %give_blocks.2.own_ref.given_ref), channel_id=1, source_target_pairs={{0,1},{1,0},{2,3},{3,2},{4,5},{5,4},{6,7},{7,6},{8,9},{9,8},{10,11... | collective-permute-start | bytes 4055048 | tf_op jit(solution)/shard_map/ppermute | solution.py:230
  11.1 2.1 %collective-permute-start.6 = (f32[2,264,256]{2,1,0:T(8,128)S(1)}, f32[2,264,256]{2,1,0:T(8,128)S(1)}, u32[]{:S(2)}, u32[]{:S(2)}) collective-permute-start(f32[2,264,256]{2,1,0:T(8,128)S(1)} %give_blocks.3.given_ref), channel_id=1, source_target_pairs={{0,1},{1,0},{2,3},{3,2},{4,5},{5,4},{6,7},{7,6},{8,9},{9,8},{10,11... | collective-permute-start | bytes 1622024 | tf_op jit(solution)/shard_map/ppermute | solution.py:230
  14.6 20.3 %collective-permute-start.8 = (f32[528,256]{1,0:T(8,128)S(1)}, f32[528,256]{1,0:T(8,128)S(1)}, u32[]{:S(2)}, u32[]{:S(2)}) collective-permute-start(f32[528,256]{1,0:T(8,128)S(1)} %get-tuple-element.30.own_ref), channel_id=1, source_target_pairs={{0,4},{1,5},{2,6},{3,7},{4,8},{5,9},{6,10},{7,11},{8,12},{9,13},{1... | collective-permute-start | bytes 1622024 | tf_op jit(solution)/shard_map/ppermute | solution.py:233
  19.5 17.6 %copy-start.4 = (s32[1,15]{1,0:T(1,128)S(1)}, s32[1,15]{1,0:T(1,128)}, u32[]{:S(2)}) copy-start(s32[1,15]{1,0:T(1,128)} %present_ref.15) | copy-start | bytes 184
  19.5 16.7 %collective-permute-start.7 = (f32[528,256]{1,0:T(8,128)S(1)}, f32[528,256]{1,0:T(8,128)S(1)}, u32[]{:S(2)}, u32[]{:S(2)}) collective-permute-start(f32[528,256]{1,0:T(8,128)S(1)} %get-tuple-element.31.own_ref), channel_id=1, source_target_pairs={{4,0},{5,1},{6,2},{7,3},{8,4},{9,5},{10,6},{11,7},{12,8},{13,9},{1... | collective-permute-start | bytes 1622024 | tf_op jit(solution)/shard_map/ppermute | solution.py:233
  24.7 26.1 %collective-permute-start.5 = (f32[528,256]{1,0:T(8,128)S(1)}, f32[528,256]{1,0:T(8,128)S(1)}, u32[]{:S(2)}, u32[]{:S(2)}) collective-permute-start(f32[528,256]{1,0:T(8,128)S(1)} %get-tuple-element.28.own_ref), channel_id=1, source_target_pairs={{0,6},{1,7},{2,8},{3,9},{4,10},{5,11},{6,12},{7,13},{8,14},{9,15},... | collective-permute-start | bytes 1622024 | tf_op jit(solution)/shard_map/ppermute | solution.py:233
  30.2 22.4 %collective-permute-start.4 = (f32[528,256]{1,0:T(8,128)S(1)}, f32[528,256]{1,0:T(8,128)S(1)}, u32[]{:S(2)}, u32[]{:S(2)}) collective-permute-start(f32[528,256]{1,0:T(8,128)S(1)} %get-tuple-element.29.own_ref), channel_id=1, source_target_pairs={{6,0},{7,1},{8,2},{9,3},{10,4},{11,5},{12,6},{13,7},{14,8},{15,9},... | collective-permute-start | bytes 1622024 | tf_op jit(solution)/shard_map/ppermute | solution.py:233
  31.5 37.5 %collective-permute-start.3 = (f32[528,256]{1,0:T(8,128)S(1)}, f32[528,256]{1,0:T(8,128)S(1)}, u32[]{:S(2)}, u32[]{:S(2)}) collective-permute-start(f32[528,256]{1,0:T(8,128)S(1)} %get-tuple-element.26.own_ref), channel_id=1, source_target_pairs={{0,2},{1,3},{2,4},{3,5},{4,6},{5,7},{6,8},{7,9},{8,10},{9,11},{10,... | collective-permute-start | bytes 1622024 | tf_op jit(solution)/shard_map/ppermute | solution.py:233
  35.0 36.0 %collective-permute-start.2 = (f32[528,256]{1,0:T(8,128)S(1)}, f32[528,256]{1,0:T(8,128)S(1)}, u32[]{:S(2)}, u32[]{:S(2)}) collective-permute-start(f32[528,256]{1,0:T(8,128)S(1)} %get-tuple-element.27.own_ref), channel_id=1, source_target_pairs={{2,0},{3,1},{4,2},{5,3},{6,4},{7,5},{8,6},{9,7},{10,8},{11,9},{12,... | collective-permute-start | bytes 1622024 | tf_op jit(solution)/shard_map/ppermute | solution.py:233
  36.3 3.3 %copy-start.1 = (f32[1,15,256,256]{3,2,1,0:T(8,128)S(1)}, f32[1,15,256,256]{3,2,1,0:T(8,128)}, u32[]{:S(2)}) copy-start(f32[1,15,256,256]{3,2,1,0:T(8,128)} %int_ref.23) | copy-start | bytes 11796484
  36.3 36.5 %collective-permute-start.1 = (f32[264,256]{1,0:T(8,128)S(1)}, f32[264,256]{1,0:T(8,128)S(1)}, u32[]{:S(2)}, u32[]{:S(2)}) collective-permute-start(f32[264,256]{1,0:T(8,128)S(1)} %get-tuple-element.25.own_ref), channel_id=1, source_target_pairs={{1,8},{3,10},{5,12},{7,14},{8,1},{10,3},{12,5},{14,7},{17,24},{19,... | collective-permute-start | bytes 811016 | tf_op jit(solution)/shard_map/ppermute | solution.py:252

commit v2 on v0

v2 whole, which is shorter than its diff:
```python
import functools

import jax
import jax.numpy as jnp
from jax import lax
from jax.experimental import pallas as pl
from jax.experimental.pallas import tpu as pltpu
from jax.sharding import PartitionSpec as P

F32 = jnp.float32
EXTRA = 8

SENDS = (
    (2, 7, -1, 6, 1, 10, 13, 3, 14, 8, 9, 4, 5, 12, 15, 11),
    (6, 0, 7, -1, 11, 3, 9, 2, 13, 4, 5, 12, -1, 8, -1, 10),
    (7, -1, 3, 10, 5, 12, -1, 1, 9, 2, 4, 13, -1, 11, -1, 8),
    (-1, 6, -1, -1, -1, 9, 11, 4, 10, 3, 13, -1, 8, -1, 7, -1),
    (-1, 8, -1, 7, 6, 4, 2, 12, 3, 10, 11, 5, -1, -1, -1, 9),
    (1, 4, 5, -1, 3, 8, 0, 9, 12, 7, 14, 6, 10, 15, 11, 13),
    (-1, 5, 6, 2, 9, 1, 7, 8, 4, 11, 3, -1, 15, -1, 13, 14),
    (5, -1, -1, 4, -1, 11, 10, 6, 2, 14, 12, 7, 9, -1, 8, -1),
    (4, 3, -1, 5, 8, -1, 12, 0, 11, 6, 7, -1, 14, -1, 9, -1),
    (-1, 2, -1, 0, 10, 7, 8, 5, 1, -1, -1, 15, -1, 9, 12, -1),
    (-1, -1, 0, -1, 2, 6, 4, 10, 5, 13, 15, 8, 11, -1, -1, -1),
    (-1, -1, 4, 1, 0, -1, 3, 13, 6, 12, 8, 10, -1, 14, -1, -1),
    (3, -1, -1, -1, 7, 0, 1, 14, 15, 5, 6, 9, -1, -1, 10, 12),
    (-1, -1, 1, -1, -1, 2, 5, 11, 7, 15, -1, 14, 13, 10, -1, -1),
)
RELAYS = (
    (2, 0, 9, 0, 10),
    (3, 1, 9, 1, 11),
    (12, 14, 7, 1, 11),
    (12, 14, 6, 2, 13),
    (3, 1, 8, 3, 12),
    (13, 15, 6, 3, 9),
    (2, 0, 8, 4, 13),
    (13, 15, 7, 4, 10),
)


def rounds_of(count, reach):
    rounds = []
    if count != len(SENDS[0]):
        for step in range(reach, 0, -1):
            for offset in (step, -step):
                pairs = [(row, row + offset) for row in range(count) if 0 <= row + offset < count]
                rounds.append((pairs, [reach + offset] * count, [reach - offset] * count))
        return rounds, ()
    for number, targets in enumerate(SENDS):
        pairs, sent, received = [], [None] * count, [None] * count
        for row, target in enumerate(targets):
            if target >= 0:
                pairs.append((row, target))
                sent[row], received[target] = reach + target - row, reach + row - target
        for origin, by, to, first, second in RELAYS:
            if number == first:
                pairs.append((origin, by))
                sent[origin] = reach + to - origin
            if number == second:
                pairs.append((by, to))
                received[to] = reach + origin - to
        rounds.append((pairs, sent, received))
    for row in range(count):
        for kind in (1, 2):
            used = {turn[kind][row] for turn in rounds}
            spare = [slot for slot in range(2 * reach + 1) if slot != reach and slot not in used]
            for turn in rounds:
                if turn[kind][row] is None:
                    turn[kind][row] = spare.pop()
    return rounds, RELAYS


def lookup(values, here):
    if len(set(values)) == 1:
        return values[0]
    words = [sum(value << 4 * place for place, value in enumerate(values[at : at + 8])) for at in (0, 8)]
    low, high = [word - 2**32 if word >= 2**31 else word for word in words]
    word = jnp.where(here < 8, jnp.int32(low), jnp.int32(high))
    return lax.shift_right_logical(word, 4 * lax.rem(here, 8)) & 15


def split(value):
    high = value.astype(jnp.bfloat16)
    low = (value - high.astype(F32)).astype(jnp.bfloat16)
    return high, low


def product(left, right):
    def one(a, b):
        return jnp.dot(a, b, preferred_element_type=F32)

    (left_high, left_low), (right_high, right_low) = left, right
    return one(left_high, right_high) + (one(left_high, right_low) + one(left_low, right_high))


def cycle_of(amp, integ):
    inner = product(split(integ), split(amp.T))
    inner = integ + integ.T - 0.5 * inner
    return product(split(amp), split(inner))


def put_cycles(slots, here, amp_ref, int_ref, gap_rows, kept_ref, outs):
    width = amp_ref.shape[-1]
    for number, slot in enumerate(slots):
        index = lookup(slot, here)
        cycle = cycle_of(amp_ref[index], int_ref[index])
        kept_ref[index] = cycle
        if number < len(outs):
            outs[number][:width, :] = cycle
            outs[number][width:, :] = gap_rows


def first_kernel(order, amp_hbm, int_hbm, gap_hbm, present_hbm, *refs):
    amp_ref, int_ref, gap_ref, present_ref, kept_ref, *outs = refs[:-3]
    gap_buf, block_sem, small_sem = refs[-3:]
    here = lax.axis_index("row")
    loads = []
    for number, slot in enumerate(order):
        index = lookup(slot, here)
        loads.append(pltpu.make_async_copy(amp_hbm.at[0, index], amp_ref.at[index], block_sem.at[number, 0]))
        loads.append(pltpu.make_async_copy(int_hbm.at[0, index], int_ref.at[index], block_sem.at[number, 1]))
        loads[-2].start()
        loads[-1].start()
        if number == 0:
            small = [
                pltpu.make_async_copy(gap_hbm, gap_buf, small_sem.at[0]),
                pltpu.make_async_copy(present_hbm, present_ref, small_sem.at[1]),
            ]
            for copy in small:
                copy.start()
    for copy in loads[: 2 * len(outs)] + small:
        copy.wait()
    gap_rows = jnp.broadcast_to(gap_buf[...], (EXTRA, amp_ref.shape[-1]))
    gap_ref[...] = gap_rows
    put_cycles(order[: len(outs)], here, amp_ref, int_ref, gap_rows, kept_ref, outs)
    for copy in loads[2 * len(outs) :]:
        copy.wait()


def cycle_kernel(order, relays, arrays, amp_ref, int_ref, gap_ref, _, *refs):
    arrived, kept_ref, outs = refs[:arrays], refs[arrays], refs[arrays + 1 :]
    here = lax.axis_index("row")
    put_cycles(order, here, amp_ref, int_ref, gap_ref[...], kept_ref, outs)
    for row, output, array in relays:

        @pl.when(here == row)
        def _():
            outs[output][...] = arrived[array][...]


def update_kernel(slots, first, int_ref, gap_ref, present_ref, kept_ref, *refs):
    arrived, refs = refs[: len(slots)], refs[len(slots) :]
    if not first:
        before_ref, refs = refs[1], refs[2:]
    out_ref, part_ref, out_buf, out_sem = refs
    width = int_ref.shape[-1]
    middle = (present_ref.shape[1] - 1) // 2
    here = lax.axis_index("row")
    gap_column = gap_ref[...].T[:, :1]
    part = jnp.zeros(part_ref.shape, F32) if first else before_ref[...]
    stores = []
    items = [(lookup(slot, here), ref) for slot, ref in zip(slots, arrived)]
    if first:
        items.append((middle, None))
    for number, (index, ref) in enumerate(items):
        integ, mine = int_ref[index], kept_ref[index]
        theirs = mine if ref is None else ref[:width, :]
        gap_other = gap_ref[:1, :] if ref is None else ref[width : width + 1, :]
        at_slot = lax.broadcasted_iota(jnp.int32, present_ref.shape, 1) == index
        flag = jnp.sum(jnp.where(at_slot, present_ref[...], 0), axis=1, keepdims=True)
        total = integ + mine + theirs.T
        fresh = jnp.where(flag > 0, total / (gap_column + gap_other), F32(0.0))
        out_buf[number] = fresh
        stores.append(pltpu.make_async_copy(out_buf.at[number], out_ref.at[0, index], out_sem.at[number]))
        stores[-1].start()
        part = part + jnp.sum((fresh * integ).reshape(width // 8, 8, width), axis=0)
    part_ref[...] = part
    for copy in stores:
        copy.wait()


PARAMS = pltpu.CompilerParams(vmem_limit_bytes=16 * 1024 * 1024)
IN_HBM = pl.BlockSpec(memory_space=pltpu.HBM)
IN_VMEM = pl.BlockSpec(memory_space=pltpu.VMEM)
DMA = pltpu.SemaphoreType.DMA
SMALL = pl.CostEstimate(flops=1, bytes_accessed=1, transcendentals=0)
FIRST, SECOND = 4, 8
UPDATES = (0, 5, 10, 14)


def per_device(amplitude, integral, pair_gap, present):
    slots, width = amplitude.shape[1], amplitude.shape[2]
    reach = (slots - 1) // 2
    height = width + EXTRA
    count = lax.axis_size("row")
    rounds, relays = rounds_of(count, reach)
    order = [turn[1] for turn in rounds] + [[reach]]

    def hbm(*values):
        return [pltpu.with_memory_space_constraint(value, pltpu.HBM) for value in values]

    def vmem(*values):
        return [pltpu.with_memory_space_constraint(value, pltpu.VMEM) for value in values]

    cube = pltpu.VMEM((slots, width, width), F32)
    block = pltpu.VMEM((height, width), F32)
    amp, integ, gap, flags, kept, *sent = pl.pallas_call(
        functools.partial(first_kernel, order),
        in_specs=[IN_HBM] * 4,
        out_specs=[IN_VMEM] * (5 + FIRST),
        out_shape=[cube, cube, pltpu.VMEM((EXTRA, width), F32), pltpu.VMEM(present.shape, present.dtype), cube]
        + [block] * FIRST,
        scratch_shapes=[pltpu.VMEM((1, width), F32), DMA((slots, 2)), DMA((2,))],
        compiler_params=PARAMS,
        cost_estimate=SMALL,
        name="first_blocks",
    )(*hbm(amplitude, integral, pair_gap, present))

    def cycles(name, start, stop, kept, arrived):
        passed = [(by, second - start, first) for _, by, _, first, second in relays if start <= second < stop]
        arrived = arrived if passed else []
        some = order[start:stop] + ([order[-1]] if stop == len(rounds) else [])
        kept, *sent = pl.pallas_call(
            functools.partial(cycle_kernel, some, passed, len(arrived)),
            in_specs=[IN_VMEM] * (4 + len(arrived)),
            out_specs=[IN_VMEM] * (1 + stop - start),
            out_shape=[cube] + [block] * (stop - start),
            input_output_aliases={3: 0},
            compiler_params=PARAMS,
            cost_estimate=SMALL,
            name=name,
        )(*vmem(amp, integ, gap, kept, *arrived))
        return kept, sent

    def send(start, stop):
        return [lax.ppermute(sent[number], "row", rounds[number][0]) for number in range(start, stop)]

    arrived = send(0, FIRST)
    kept, more = cycles("second_blocks", FIRST, SECOND, kept, [])
    sent += more
    arrived += send(FIRST, SECOND)
    passing = 1 + max([first for _, _, _, first, _ in relays], default=-1)
    kept, more = cycles("third_blocks", SECOND, len(rounds), kept, arrived[:passing])
    sent += more
    arrived += send(SECOND, len(rounds))

    def updates(start, stop, before):
        some = [turn[2] for turn in rounds[start:stop]]
        first = before is None
        n = len(some) + int(first)
        return pl.pallas_call(
            functools.partial(update_kernel, some, first),
            in_specs=[IN_VMEM] * (4 + len(some)) + ([] if first else [IN_HBM, IN_VMEM]),
            out_specs=[IN_HBM, IN_VMEM],
            out_shape=[pltpu.HBM((1, slots, width, width), F32), pltpu.VMEM((8, width), F32)],
            scratch_shapes=[pltpu.VMEM((n, width, width), F32), DMA((n,))],
            input_output_aliases={} if first else {4 + len(some): 0},
            compiler_params=PARAMS,
            cost_estimate=SMALL,
            name="update",
        )(
            *vmem(integ, gap, flags, kept, *arrived[start:stop]),
            *([] if first else [*hbm(before[0]), *vmem(before[1])]),
        )

    state = None
    for start, stop in zip(UPDATES[:-1], UPDATES[1:]):
        state = updates(start, stop, state)
    updated, part = state

    summed = jnp.sum(part, axis=0).reshape(-1, 128).sum(axis=0)
    every = lax.all_to_all(jnp.broadcast_to(summed, (count, 128)), "row", 0, 0)
    blocks_all = count * amplitude.shape[0]
    energy = jnp.sum(every) / (width * width * blocks_all)
    return updated, jnp.reshape(energy, (1,))


def solution(mesh):
    in_specs = (
        P(("mol", "row"), None, None, None),
        P(("mol", "row"), None, None, None),
        P(("mol", "row"), None),
        P(("mol", "row"), None),
    )
    out_specs = (P(("mol", "row"), None, None, None), P("mol"))
    return jax.shard_map(per_device, mesh=mesh, in_specs=in_specs, out_specs=out_specs, check_vma=False)
```

time: 193 us -> 74.3 us (0.38)
  blocking collectives: 48.4 us -> 15.5 us
  waiting for transfers between devices: 28.1 us -> 1.26 us
  starting transfers between devices: 67 us -> 41 us
  local copies, waits for them, and re-layouts: 25.4 us -> 0.01 us
  matrix products: 16.1 us -> 0 us
  Pallas kernels: 0 us -> 12.7 us
  other arithmetic: 3.54 us -> 0.64 us
    psum x1 -> x0, blocking collectives: 48.4 us -> none  [per_device(): whole = lax.psum(partial_sum, 'row')]
    ppermute x28 -> x14, waiting for transfers between devices: 28.1 us -> 1.26 us  [send(): lax.ppermute(sent[number], 'row', rounds[number][0])]
    ppermute x28 -> x14, starting transfers between devices: 67 us -> 41 us  [send(): lax.ppermute(sent[number], 'row', rounds[number][0])]
    unnamed x30 -> x0, local copies, waits for them, and re-layouts: 18.8 us -> none
    dot_general x3 -> x0, matrix products: 16.1 us -> none  [the longest x1 7.47 us: block_terms(): jnp.dot(amp_block, int_block, precision=hi, preferred_element_type=jnp.fl...]
    all_to_all x0 -> x1, blocking collectives: none -> 15.5 us  [per_device(): every = lax.all_to_all(jnp.broadcast_to(summed, (count, 128)), 'row', 0, 0)]
    pallas_call x0 -> x6, Pallas kernels: none -> 12.7 us  [the longest x1 4.76 us: per_device(): pl.pallas_call(functools.partial(first_kernel, order), in_specs=[IN_HBM]...]
    sub x1 -> x0, local copies, waits for them, and re-layouts: 5.46 us -> none  [block_terms(): return first + second - 0.5 * third]
  transfers between devices with their start and end apart: 28 -> 14, of which waited for: 9 -> 3; matrix products, arithmetic and copies ran while one was open for 9% -> 0% of each run, Pallas kernels for 0% -> 9%
where the time goes in v2:
time: 74.3 us; the launch traced here: 73.8 us
  starting transfers between devices  41 us (55%)
  blocking collectives  15.5 us (21%)
  Pallas kernels  12.7 us (17%)
  between operations  2.65 us (4%)
  waiting for transfers between devices  1.26 us (2%)
    ppermute x14, starting transfers between devices, send(): lax.ppermute(sent[number], 'row', rounds[number][0])  41 us
    all_to_all x1, blocking collectives, per_device(): every = lax.all_to_all(jnp.broadcast_to(summed, (count, 128)), 'row', 0, 0)  15.5 us
    pallas_call x1, Pallas kernels, per_device(): pl.pallas_call(functools.partial(first_kernel, order), in_specs=[IN_HBM]...  4.76 us
    pallas_call x3, Pallas kernels, updates(): pl.pallas_call(functools.partial(update_kernel, some, first), in_specs=[I...  4.5 us
    pallas_call x2, Pallas kernels, cycles(): pl.pallas_call(functools.partial(cycle_kernel, some, passed, len(arrived)...  3.49 us
  transfers between devices with their start and end apart: 14, of which 3 were waited for; matrix products, arithmetic and copies ran while one was open for 0% of the time, Pallas kernels for 9%

profile of v2, /device:TPU:0, one launch (start us, length us, event | category | flops | bytes accessed | tf_op | source)
XLA Modules:
  0.0 73.8 jit_solution(4786413489331336324)
XLA Ops:
  0.6 4.8 %first_blocks.1 = (f32[15,256,256]{2,1,0:T(8,128)S(1)}, f32[15,256,256]{2,1,0:T(8,128)S(1)}, f32[8,256]{1,0:T(8,128)S(1)}, s32[1,15]{1,0:T(1,128)S(1)}, f32[15,2...) custom-call(f32[1,15,256,256]{3,2,1,0:T(8,128)} %amp_hbm.1, ...), custom_call_target="tpu_custom_call" | custom-call | flops 1 | bytes 1 | tf_op jit(solution)/shard_map/first_blocks/pallas_call | solution.py:207
  5.4 3.0 %collective-permute-start = (f32[264,256]{1,0:T(8,128)S(1)}, f32[264,256]{1,0:T(8,128)S(1)}, u32[]{:S(2)}, u32[]{:S(2)}) collective-permute-start(f32[264,256]{1,0:T(8,128)S(1)} %get-tuple-element.35), channel_id=1, source_target_pairs={{0,2},{1,7},{3,6},{4,1},{5,10},{6,13},{7,3},{8,14},{9,8},{10,9},{1... | collective-permute-start | bytes 811016 | tf_op jit(solution)/shard_map/ppermute | solution.py:236
  8.4 4.9 %collective-permute-start.1 = (f32[264,256]{1,0:T(8,128)S(1)}, f32[264,256]{1,0:T(8,128)S(1)}, u32[]{:S(2)}, u32[]{:S(2)}) collective-permute-start(f32[264,256]{1,0:T(8,128)S(1)} %get-tuple-element.36), channel_id=1, source_target_pairs={{0,6},{1,0},{2,7},{4,11},{5,3},{6,9},{7,2},{8,13},{9,4},{10,5},{11... | collective-permute-start | bytes 811016 | tf_op jit(solution)/shard_map/ppermute | solution.py:236
  13.3 1.3 %collective-permute-start.2 = (f32[264,256]{1,0:T(8,128)S(1)}, f32[264,256]{1,0:T(8,128)S(1)}, u32[]{:S(2)}, u32[]{:S(2)}) collective-permute-start(f32[264,256]{1,0:T(8,128)S(1)} %get-tuple-element.37), channel_id=1, source_target_pairs={{0,7},{2,3},{3,10},{4,5},{5,12},{7,1},{8,9},{9,2},{10,4},{11,13},{... | collective-permute-start | bytes 811016 | tf_op jit(solution)/shard_map/ppermute | solution.py:236
  14.6 0.7 collective-permute-start.3
  15.3 1.4 %second_blocks.1 = (f32[15,256,256]{2,1,0:T(8,128)S(1)}, f32[264,256]{1,0:T(8,128)S(1)}, f32[264,256]{1,0:T(8,128)S(1)}, f32[264,256]{1,0:T(8,128)S(1)}, f32[264,256]{1,0:T(8,128)S(1)}) custom-call(f32[15,256,256]{2,1,0:T(8,128)S(1)} %get-tuple-element.32.amp_ref, f32[15,256,256]{2,1,0:T(8,128)S(1)} %get-tuple-element.29.int_ref, ...), custom_call_target="tpu_custom_call", output_to_operand_aliasing={{0}: (3, {})} | custom-call | flops 1 | bytes 1 | tf_op jit(solution)/shard_map/second_blocks/pallas_call | solution.py:223
  16.7 1.3 %collective-permute-start.4 = (f32[264,256]{1,0:T(8,128)S(1)}, f32[264,256]{1,0:T(8,128)S(1)}, u32[]{:S(2)}, u32[]{:S(2)}) collective-permute-start(f32[264,256]{1,0:T(8,128)S(1)} %get-tuple-element.39), channel_id=1, source_target_pairs={{1,8},{3,7},{4,6},{5,4},{6,2},{7,12},{8,3},{9,10},{10,11},{11,5},{... | collective-permute-start | bytes 811016 | tf_op jit(solution)/shard_map/ppermute | solution.py:236
  18.0 0.0 collective-permute-done.refs_0_
  18.0 7.1 %collective-permute-start.9 = (f32[264,256]{1,0:T(8,128)S(1)}, f32[264,256]{1,0:T(8,128)S(1)}, u32[]{:S(2)}, u32[]{:S(2)}) collective-permute-start(f32[264,256]{1,0:T(8,128)S(1)} %get-tuple-element.45), channel_id=1, source_target_pairs={{0,1},{1,4},{2,5},{4,3},{5,8},{6,0},{7,9},{8,12},{9,7},{10,14},{11... | collective-permute-start | bytes 811016 | tf_op jit(solution)/shard_map/ppermute | solution.py:236
  25.2 0.0 collective-permute-done.1.refs_1_
  25.2 0.7 collective-permute-start.10
  25.9 0.0 collective-permute-done.2.refs_2_
  25.9 6.0 %collective-permute-start.11 = (f32[264,256]{1,0:T(8,128)S(1)}, f32[264,256]{1,0:T(8,128)S(1)}, u32[]{:S(2)}, u32[]{:S(2)}) collective-permute-start(f32[264,256]{1,0:T(8,128)S(1)} %get-tuple-element.47), channel_id=1, source_target_pairs={{0,5},{3,4},{5,11},{6,10},{7,6},{8,2},{9,14},{10,12},{11,7},{12,9}... | collective-permute-start | bytes 811016 | tf_op jit(solution)/shard_map/ppermute | solution.py:236
  31.8 0.0 collective-permute-done.3.refs_3_
  31.9 0.0 collective-permute-done.4.refs_4_
  31.9 2.1 %third_blocks.1 = (f32[15,256,256]{2,1,0:T(8,128)S(1)}, f32[264,256]{1,0:T(8,128)S(1)}, f32[264,256]{1,0:T(8,128)S(1)}, f32[264,256]{1,0:T(8,128)S(1)}, f32[264,...) custom-call(f32[15,256,256]{2,1,0:T(8,128)S(1)} %get-tuple-element.32.amp_r, ...), custom_call_target="tpu_custom_call", output_to_operand_aliasing={{0}: (3, {})} | custom-call | flops 1 | bytes 1 | tf_op jit(solution)/shard_map/third_blocks/pallas_call | solution.py:223
  34.0 1.9 %collective-permute-start.12 = (f32[264,256]{1,0:T(8,128)S(1)}, f32[264,256]{1,0:T(8,128)S(1)}, u32[]{:S(2)}, u32[]{:S(2)}) collective-permute-start(f32[264,256]{1,0:T(8,128)S(1)} %get-tuple-element.48), channel_id=1, source_target_pairs={{0,4},{1,3},{3,5},{4,8},{6,12},{7,0},{8,11},{9,6},{10,7},{12,14},{... | collective-permute-start | bytes 811016 | tf_op jit(solution)/shard_map/ppermute | solution.py:236
  35.9 4.5 %collective-permute-start.5 = (f32[264,256]{1,0:T(8,128)S(1)}, f32[264,256]{1,0:T(8,128)S(1)}, u32[]{:S(2)}, u32[]{:S(2)}) collective-permute-start(f32[264,256]{1,0:T(8,128)S(1)} %get-tuple-element.41), channel_id=1, source_target_pairs={{2,0},{4,2},{5,6},{6,4},{7,10},{8,5},{9,13},{10,15},{11,8},{12,11}... | collective-permute-start | bytes 811016 | tf_op jit(solution)/shard_map/ppermute | solution.py:236
  40.4 0.0 collective-permute-done.9.refs_0_
  40.4 1.3 %collective-permute-start.13 = (f32[264,256]{1,0:T(8,128)S(1)}, f32[264,256]{1,0:T(8,128)S(1)}, u32[]{:S(2)}, u32[]{:S(2)}) collective-permute-start(f32[264,256]{1,0:T(8,128)S(1)} %get-tuple-element.49), channel_id=1, source_target_pairs={{1,2},{3,0},{4,10},{5,7},{6,8},{7,5},{8,1},{11,15},{13,9},{14,12},... | collective-permute-start | bytes 811016 | tf_op jit(solution)/shard_map/ppermute | solution.py:236
  41.7 0.0 collective-permute-done.10.refs_1_
  41.7 1.3 %collective-permute-start.6 = (f32[264,256]{1,0:T(8,128)S(1)}, f32[264,256]{1,0:T(8,128)S(1)}, u32[]{:S(2)}, u32[]{:S(2)}) collective-permute-start(f32[264,256]{1,0:T(8,128)S(1)} %get-tuple-element.42), channel_id=1, source_target_pairs={{2,4},{3,1},{4,0},{6,3},{7,13},{8,6},{9,12},{10,8},{11,10},{13,14}... | collective-permute-start | bytes 811016 | tf_op jit(solution)/shard_map/ppermute | solution.py:236
  43.0 0.0 collective-permute-done.11.refs_2_
  43.0 4.9 %collective-permute-start.7 = (f32[264,256]{1,0:T(8,128)S(1)}, f32[264,256]{1,0:T(8,128)S(1)}, u32[]{:S(2)}, u32[]{:S(2)}) collective-permute-start(f32[264,256]{1,0:T(8,128)S(1)} %get-tuple-element.43), channel_id=1, source_target_pairs={{0,3},{4,7},{5,0},{6,1},{7,14},{8,15},{9,5},{10,6},{11,9},{14,10},... | collective-permute-start | bytes 811016 | tf_op jit(solution)/shard_map/ppermute | solution.py:236
  47.9 0.0 collective-permute-done.12.refs_3_
  47.9 2.2 %collective-permute-start.8 = (f32[264,256]{1,0:T(8,128)S(1)}, f32[264,256]{1,0:T(8,128)S(1)}, u32[]{:S(2)}, u32[]{:S(2)}) collective-permute-start(f32[264,256]{1,0:T(8,128)S(1)} %get-tuple-element.44), channel_id=1, source_target_pairs={{2,1},{5,2},{6,5},{7,11},{8,7},{9,15},{11,14},{12,13},{13,10},{14,... | collective-permute-start | bytes 811016 | tf_op jit(solution)/shard_map/ppermute | solution.py:236
  50.1 1.6 %update.3 = (f32[1,15,256,256]{3,2,1,0:T(8,128)}, f32[8,256]{1,0:T(8,128)S(1)}) custom-call(f32[15,256,256]{2,1,0:T(8,128)S(1)} %get-tuple-element.29.int_ref, f32[8,256]{1,0:T(8,128)S(1)} %get-tuple-element.30.gap_ref, s32[1,15]{1,0:T(1,128)S(1)} %get-tuple-element.31.present_ref, f32[15,256,256]{2,1,0:T(8,128)S(1)} %get-tuple-element.40.kept_ref, ...), custom_call_target="tpu_custom_call" | custom-call | flops 1 | bytes 1 | tf_op jit(solution)/shard_map/update/pallas_call | solution.py:251
  51.7 0.0 collective-permute-done.13.refs_4_
  51.7 1.5 %update.4 = (f32[1,15,256,256]{3,2,1,0:T(8,128)}, f32[8,256]{1,0:T(8,128)S(1)}) custom-call(f32[15,256,256]{2,1,0:T(8,128)S(1)} %get-tuple-element.29.int_ref, f32[8,256]{1,0:T(8,128)S(1)} %get-tuple-element.30.gap_ref, s32[1,15]{1,0:T(1,128)S(1)} %get-tuple-element.31.present_ref, ...), custom_call_target="tpu_custom_call", output_to_operand_aliasing={{0}: (9, {})} | custom-call | flops 1 | bytes 1 | tf_op jit(solution)/shard_map/update/pallas_call | solution.py:251
  53.3 0.0 collective-permute-done.5.refs_0_
  53.3 0.8 %collective-permute-done.6.refs_1_ = f32[264,256]{1,0:T(8,128)S(1)} collective-permute-done((f32[264,256]{1,0:T(8,128)S(1)}, f32[264,256]{1,0:T(8,128)S(1)}, u32[]{:S(2)}, u32[]{:S(2)}) %collective-permute-start.6) | collective-permute-done | bytes 270368 | tf_op jit(solution)/shard_map/ppermute | solution.py:236
  54.1 0.1 collective-permute-done.7.refs_2_
  54.1 0.4 collective-permute-done.8.refs_3_
  54.5 1.4 %update.5 = (f32[1,15,256,256]{3,2,1,0:T(8,128)}, f32[8,256]{1,0:T(8,128)S(1)}) custom-call(f32[15,256,256]{2,1,0:T(8,128)S(1)} %get-tuple-element.29.int_ref, f32[8,256]{1,0:T(8,128)S(1)} %get-tuple-element.30.gap_ref, s32[1,15]{1,0:T(1,128)S(1)} %get-tuple-element.31.present_ref, ...), custom_call_target="tpu_custom_call", output_to_operand_aliasing={{0}: (8, {})} | custom-call | flops 1 | bytes 1 | tf_op jit(solution)/shard_map/update/pallas_call | solution.py:251
  56.0 15.5 %all_to_all.6 = f32[16,1,128]{2,1,0:T(1,128)S(1)} all-to-all(f32[16,1,128]{2,1,0:T(1,128)S(1)} %broadcast_in_dim.3), channel_id=1, replica_groups=mesh['mol'=2,'row'=16] {'row'}, dimensions={0} | all-to-all | bytes 16384 | tf_op jit(solution)/shard_map/all_to_all | solution.py:272
  71.4 0.6 reduce_sum.29
  (3 shorter events, 0.0 us)
Async XLA Ops:
  5.4 12.6 %collective-permute-start = (f32[264,256]{1,0:T(8,128)S(1)}, f32[264,256]{1,0:T(8,128)S(1)}, u32[]{:S(2)}, u32[]{:S(2)}) collective-permute-start(f32[264,256]{1,0:T(8,128)S(1)} %get-tuple-element.35), channel_id=1, source_target_pairs={{0,2},{1,7},{3,6},{4,1},{5,10},{6,13},{7,3},{8,14},{9,8},{10,9},{1... | collective-permute-start | bytes 811016 | tf_op jit(solution)/shard_map/ppermute | solution.py:236
  8.4 16.7 %collective-permute-start.1 = (f32[264,256]{1,0:T(8,128)S(1)}, f32[264,256]{1,0:T(8,128)S(1)}, u32[]{:S(2)}, u32[]{:S(2)}) collective-permute-start(f32[264,256]{1,0:T(8,128)S(1)} %get-tuple-element.36), channel_id=1, source_target_pairs={{0,6},{1,0},{2,7},{4,11},{5,3},{6,9},{7,2},{8,13},{9,4},{10,5},{11... | collective-permute-start | bytes 811016 | tf_op jit(solution)/shard_map/ppermute | solution.py:236
  13.3 12.6 %collective-permute-start.2 = (f32[264,256]{1,0:T(8,128)S(1)}, f32[264,256]{1,0:T(8,128)S(1)}, u32[]{:S(2)}, u32[]{:S(2)}) collective-permute-start(f32[264,256]{1,0:T(8,128)S(1)} %get-tuple-element.37), channel_id=1, source_target_pairs={{0,7},{2,3},{3,10},{4,5},{5,12},{7,1},{8,9},{9,2},{10,4},{11,13},{... | collective-permute-start | bytes 811016 | tf_op jit(solution)/shard_map/ppermute | solution.py:236
  14.6 17.2 %collective-permute-start.3 = (f32[264,256]{1,0:T(8,128)S(1)}, f32[264,256]{1,0:T(8,128)S(1)}, u32[]{:S(2)}, u32[]{:S(2)}) collective-permute-start(f32[264,256]{1,0:T(8,128)S(1)} %get-tuple-element.38), channel_id=1, source_target_pairs={{1,6},{5,9},{6,11},{7,4},{8,10},{9,3},{10,13},{12,8},{14,7},{3,1},... | collective-permute-start | bytes 811016 | tf_op jit(solution)/shard_map/ppermute | solution.py:236
  16.7 15.1 %collective-permute-start.4 = (f32[264,256]{1,0:T(8,128)S(1)}, f32[264,256]{1,0:T(8,128)S(1)}, u32[]{:S(2)}, u32[]{:S(2)}) collective-permute-start(f32[264,256]{1,0:T(8,128)S(1)} %get-tuple-element.39), channel_id=1, source_target_pairs={{1,8},{3,7},{4,6},{5,4},{6,2},{7,12},{8,3},{9,10},{10,11},{11,5},{... | collective-permute-start | bytes 811016 | tf_op jit(solution)/shard_map/ppermute | solution.py:236
  18.0 22.3 %collective-permute-start.9 = (f32[264,256]{1,0:T(8,128)S(1)}, f32[264,256]{1,0:T(8,128)S(1)}, u32[]{:S(2)}, u32[]{:S(2)}) collective-permute-start(f32[264,256]{1,0:T(8,128)S(1)} %get-tuple-element.45), channel_id=1, source_target_pairs={{0,1},{1,4},{2,5},{4,3},{5,8},{6,0},{7,9},{8,12},{9,7},{10,14},{11... | collective-permute-start | bytes 811016 | tf_op jit(solution)/shard_map/ppermute | solution.py:236
  25.2 16.5 %collective-permute-start.10 = (f32[264,256]{1,0:T(8,128)S(1)}, f32[264,256]{1,0:T(8,128)S(1)}, u32[]{:S(2)}, u32[]{:S(2)}) collective-permute-start(f32[264,256]{1,0:T(8,128)S(1)} %get-tuple-element.46), channel_id=1, source_target_pairs={{1,5},{2,6},{3,2},{4,9},{5,1},{6,7},{7,8},{8,4},{9,11},{10,3},{12,... | collective-permute-start | bytes 811016 | tf_op jit(solution)/shard_map/ppermute | solution.py:236
  25.9 17.1 %collective-permute-start.11 = (f32[264,256]{1,0:T(8,128)S(1)}, f32[264,256]{1,0:T(8,128)S(1)}, u32[]{:S(2)}, u32[]{:S(2)}) collective-permute-start(f32[264,256]{1,0:T(8,128)S(1)} %get-tuple-element.47), channel_id=1, source_target_pairs={{0,5},{3,4},{5,11},{6,10},{7,6},{8,2},{9,14},{10,12},{11,7},{12,9}... | collective-permute-start | bytes 811016 | tf_op jit(solution)/shard_map/ppermute | solution.py:236
  34.0 14.0 %collective-permute-start.12 = (f32[264,256]{1,0:T(8,128)S(1)}, f32[264,256]{1,0:T(8,128)S(1)}, u32[]{:S(2)}, u32[]{:S(2)}) collective-permute-start(f32[264,256]{1,0:T(8,128)S(1)} %get-tuple-element.48), channel_id=1, source_target_pairs={{0,4},{1,3},{3,5},{4,8},{6,12},{7,0},{8,11},{9,6},{10,7},{12,14},{... | collective-permute-start | bytes 811016 | tf_op jit(solution)/shard_map/ppermute | solution.py:236
  35.9 17.4 %collective-permute-start.5 = (f32[264,256]{1,0:T(8,128)S(1)}, f32[264,256]{1,0:T(8,128)S(1)}, u32[]{:S(2)}, u32[]{:S(2)}) collective-permute-start(f32[264,256]{1,0:T(8,128)S(1)} %get-tuple-element.41), channel_id=1, source_target_pairs={{2,0},{4,2},{5,6},{6,4},{7,10},{8,5},{9,13},{10,15},{11,8},{12,11}... | collective-permute-start | bytes 811016 | tf_op jit(solution)/shard_map/ppermute | solution.py:236
  40.4 11.4 %collective-permute-start.13 = (f32[264,256]{1,0:T(8,128)S(1)}, f32[264,256]{1,0:T(8,128)S(1)}, u32[]{:S(2)}, u32[]{:S(2)}) collective-permute-start(f32[264,256]{1,0:T(8,128)S(1)} %get-tuple-element.49), channel_id=1, source_target_pairs={{1,2},{3,0},{4,10},{5,7},{6,8},{7,5},{8,1},{11,15},{13,9},{14,12},... | collective-permute-start | bytes 811016 | tf_op jit(solution)/shard_map/ppermute | solution.py:236
  41.7 12.4 %collective-permute-start.6 = (f32[264,256]{1,0:T(8,128)S(1)}, f32[264,256]{1,0:T(8,128)S(1)}, u32[]{:S(2)}, u32[]{:S(2)}) collective-permute-start(f32[264,256]{1,0:T(8,128)S(1)} %get-tuple-element.42), channel_id=1, source_target_pairs={{2,4},{3,1},{4,0},{6,3},{7,13},{8,6},{9,12},{10,8},{11,10},{13,14}... | collective-permute-start | bytes 811016 | tf_op jit(solution)/shard_map/ppermute | solution.py:236
  43.0 11.2 %collective-permute-start.7 = (f32[264,256]{1,0:T(8,128)S(1)}, f32[264,256]{1,0:T(8,128)S(1)}, u32[]{:S(2)}, u32[]{:S(2)}) collective-permute-start(f32[264,256]{1,0:T(8,128)S(1)} %get-tuple-element.43), channel_id=1, source_target_pairs={{0,3},{4,7},{5,0},{6,1},{7,14},{8,15},{9,5},{10,6},{11,9},{14,10},... | collective-permute-start | bytes 811016 | tf_op jit(solution)/shard_map/ppermute | solution.py:236
  47.9 6.6 %collective-permute-start.8 = (f32[264,256]{1,0:T(8,128)S(1)}, f32[264,256]{1,0:T(8,128)S(1)}, u32[]{:S(2)}, u32[]{:S(2)}) collective-permute-start(f32[264,256]{1,0:T(8,128)S(1)} %get-tuple-element.44), channel_id=1, source_target_pairs={{2,1},{5,2},{6,5},{7,11},{8,7},{9,15},{11,14},{12,13},{13,10},{14,... | collective-permute-start | bytes 811016 | tf_op jit(solution)/shard_map/ppermute | solution.py:236

commit v3 on v2

--- a/solution.py
+++ b/solution.py
@@ -11,30 +11,30 @@
 EXTRA = 8
 
 SENDS = (
-    (2, 7, -1, 6, 1, 10, 13, 3, 14, 8, 9, 4, 5, 12, 15, 11),
-    (6, 0, 7, -1, 11, 3, 9, 2, 13, 4, 5, 12, -1, 8, -1, 10),
-    (7, -1, 3, 10, 5, 12, -1, 1, 9, 2, 4, 13, -1, 11, -1, 8),
-    (-1, 6, -1, -1, -1, 9, 11, 4, 10, 3, 13, -1, 8, -1, 7, -1),
-    (-1, 8, -1, 7, 6, 4, 2, 12, 3, 10, 11, 5, -1, -1, -1, 9),
-    (1, 4, 5, -1, 3, 8, 0, 9, 12, 7, 14, 6, 10, 15, 11, 13),
-    (-1, 5, 6, 2, 9, 1, 7, 8, 4, 11, 3, -1, 15, -1, 13, 14),
-    (5, -1, -1, 4, -1, 11, 10, 6, 2, 14, 12, 7, 9, -1, 8, -1),
-    (4, 3, -1, 5, 8, -1, 12, 0, 11, 6, 7, -1, 14, -1, 9, -1),
-    (-1, 2, -1, 0, 10, 7, 8, 5, 1, -1, -1, 15, -1, 9, 12, -1),
-    (-1, -1, 0, -1, 2, 6, 4, 10, 5, 13, 15, 8, 11, -1, -1, -1),
-    (-1, -1, 4, 1, 0, -1, 3, 13, 6, 12, 8, 10, -1, 14, -1, -1),
-    (3, -1, -1, -1, 7, 0, 1, 14, 15, 5, 6, 9, -1, -1, 10, 12),
-    (-1, -1, 1, -1, -1, 2, 5, 11, 7, 15, -1, 14, 13, 10, -1, -1),
+    (2, 7, 6, -1, 16, 12, 3, 9, 10, 8, 14, 4, 5, -1, 13, 11),
+    (17, 8, -1, 7, 2, 4, 10, 5, 6, 12, 3, 15, -1, 11, 9, 29),
+    (4, 0, 19, -1, 11, 2, 7, 13, 9, 6, 5, 10, -1, 28, 31, 8),
+    (18, 6, -1, 5, 8, 1, 9, 3, 4, 11, 7, 14, 29, -1, 10, 28),
+    (19, 4, 7, 18, 22, 8, 12, 0, 1, 10, 9, 5, 29, 31, 27, 30),
+    (17, 5, 0, 18, 9, 7, 13, 6, 3, 15, 4, 26, 11, 12, 8, 30),
+    (7, 16, 17, 18, 21, 9, 8, 4, 11, 3, 12, 6, 29, 30, 15, 10),
+    (6, 3, 5, 1, 10, 0, 11, 2, 12, 4, 13, 9, 8, 15, 7, 30),
+    (1, -1, 19, 0, 5, 6, 4, 8, 14, 2, 27, 13, 10, 28, 31, -1),
+    (-1, 2, 19, 10, 0, 20, 5, 1, 15, 7, 6, 12, 29, 25, 11, 14),
+    (17, 21, 4, 2, 3, 11, 0, 10, 7, 13, 8, 31, 14, 9, 12, -1),
+    (3, -1, 16, 6, 1, 20, 2, 11, 5, 28, 15, 26, 9, 14, -1, 13),
+    (5, 16, 3, 4, 6, 10, 1, 12, 2, 14, 11, 7, 13, 8, 31, 9),
+    (-1, 16, 1, 18, 7, 3, 20, 14, 13, 5, 27, 8, 15, 10, -1, 12),
 )
 RELAYS = (
-    (2, 0, 9, 0, 10),
-    (3, 1, 9, 1, 11),
-    (12, 14, 7, 1, 11),
-    (12, 14, 6, 2, 13),
-    (3, 1, 8, 3, 12),
-    (13, 15, 6, 3, 9),
-    (2, 0, 8, 4, 13),
-    (13, 15, 7, 4, 10),
+    (3, 1, 8, 0, 11),
+    (13, 15, 6, 0, 10),
+    (2, 0, 8, 1, 9),
+    (12, 14, 6, 1, 13),
+    (3, 1, 9, 2, 8),
+    (12, 14, 7, 2, 11),
+    (2, 0, 9, 3, 13),
+    (13, 15, 7, 3, 8),
 )
 
 
@@ -43,14 +43,15 @@
     if count != len(SENDS[0]):
         for step in range(reach, 0, -1):
             for offset in (step, -step):
-                pairs = [(row, row + offset) for row in range(count) if 0 <= row + offset < count]
+                pairs = [(row, (row + offset) % count) for row in range(count)]
                 rounds.append((pairs, [reach + offset] * count, [reach - offset] * count))
         return rounds, ()
     for number, targets in enumerate(SENDS):
         pairs, sent, received = [], [None] * count, [None] * count
         for row, target in enumerate(targets):
             if target >= 0:
-                pairs.append((row, target))
+                pairs.append((row, target % count))
+            if 0 <= target < count:
                 sent[row], received[target] = reach + target - row, reach + row - target
         for origin, by, to, first, second in RELAYS:
             if number == first:
@@ -99,48 +100,43 @@
     return product(split(amp), split(inner))
 
 
-def put_cycles(slots, here, amp_ref, int_ref, gap_rows, kept_ref, outs):
-    width = amp_ref.shape[-1]
-    for number, slot in enumerate(slots):
-        index = lookup(slot, here)
-        cycle = cycle_of(amp_ref[index], int_ref[index])
-        kept_ref[index] = cycle
-        if number < len(outs):
-            outs[number][:width, :] = cycle
-            outs[number][width:, :] = gap_rows
+def put_cycle(amp, integ, gap_rows, kept_ref, out_ref):
+    cycle = cycle_of(amp, integ)
+    kept_ref[...] = cycle
+    if out_ref is not None:
+        out_ref[: cycle.shape[0], :] = cycle
+        out_ref[cycle.shape[0] :, :] = gap_rows
 
 
 def first_kernel(order, amp_hbm, int_hbm, gap_hbm, present_hbm, *refs):
-    amp_ref, int_ref, gap_ref, present_ref, kept_ref, *outs = refs[:-3]
-    gap_buf, block_sem, small_sem = refs[-3:]
+    gap_ref, present_ref, kept_ref, *outs = refs[:-5]
+    amp_buf, int_buf, gap_buf, block_sem, small_sem = refs[-5:]
     here = lax.axis_index("row")
+    places = [lookup(slot, here) for slot in order]
     loads = []
-    for number, slot in enumerate(order):
-        index = lookup(slot, here)
-        loads.append(pltpu.make_async_copy(amp_hbm.at[0, index], amp_ref.at[index], block_sem.at[number, 0]))
-        loads.append(pltpu.make_async_copy(int_hbm.at[0, index], int_ref.at[index], block_sem.at[number, 1]))
+    for number, index in enumerate(places):
+        loads.append(pltpu.make_async_copy(amp_hbm.at[0, index], amp_buf.at[number], block_sem.at[number, 0]))
+        loads.append(pltpu.make_async_copy(int_hbm.at[0, index], int_buf.at[number], block_sem.at[number, 1]))
         loads[-2].start()
         loads[-1].start()
-        if number == 0:
-            small = [
-                pltpu.make_async_copy(gap_hbm, gap_buf, small_sem.at[0]),
-                pltpu.make_async_copy(present_hbm, present_ref, small_sem.at[1]),
-            ]
-            for copy in small:
-                copy.start()
-    for copy in loads[: 2 * len(outs)] + small:
+    loads.append(pltpu.make_async_copy(gap_hbm, gap_buf, small_sem.at[0]))
+    loads.append(pltpu.make_async_copy(present_hbm, present_ref, small_sem.at[1]))
+    loads[-2].start()
+    loads[-1].start()
+    for copy in loads:
         copy.wait()
-    gap_rows = jnp.broadcast_to(gap_buf[...], (EXTRA, amp_ref.shape[-1]))
+    gap_rows = jnp.broadcast_to(gap_buf[...], (EXTRA, amp_buf.shape[-1]))
     gap_ref[...] = gap_rows
-    put_cycles(order[: len(outs)], here, amp_ref, int_ref, gap_rows, kept_ref, outs)
-    for copy in loads[2 * len(outs) :]:
-        copy.wait()
+    for number, index in enumerate(places):
+        put_cycle(amp_buf[number], int_buf[number], gap_rows, kept_ref.at[index], outs[number])
 
 
 def cycle_kernel(order, relays, arrays, amp_ref, int_ref, gap_ref, _, *refs):
     arrived, kept_ref, outs = refs[:arrays], refs[arrays], refs[arrays + 1 :]
     here = lax.axis_index("row")
-    put_cycles(order, here, amp_ref, int_ref, gap_ref[...], kept_ref, outs)
+    for slot, out_ref in zip(order, [*outs, None]):
+        index = lookup(slot, here)
+        put_cycle(amp_ref[0, index], int_ref[0, index], gap_ref[...], kept_ref.at[index], out_ref)
     for row, output, array in relays:
 
         @pl.when(here == row)
@@ -163,7 +159,7 @@
     if first:
         items.append((middle, None))
     for number, (index, ref) in enumerate(items):
-        integ, mine = int_ref[index], kept_ref[index]
+        integ, mine = int_ref[0, index], kept_ref[index]
         theirs = mine if ref is None else ref[:width, :]
         gap_other = gap_ref[:1, :] if ref is None else ref[width : width + 1, :]
         at_slot = lax.broadcasted_iota(jnp.int32, present_ref.shape, 1) == index
@@ -204,13 +200,19 @@
 
     cube = pltpu.VMEM((slots, width, width), F32)
     block = pltpu.VMEM((height, width), F32)
-    amp, integ, gap, flags, kept, *sent = pl.pallas_call(
-        functools.partial(first_kernel, order),
+    gap, flags, kept, *sent = pl.pallas_call(
+        functools.partial(first_kernel, order[:FIRST]),
         in_specs=[IN_HBM] * 4,
-        out_specs=[IN_VMEM] * (5 + FIRST),
-        out_shape=[cube, cube, pltpu.VMEM((EXTRA, width), F32), pltpu.VMEM(present.shape, present.dtype), cube]
+        out_specs=[IN_VMEM] * (3 + FIRST),
+        out_shape=[pltpu.VMEM((EXTRA, width), F32), pltpu.VMEM(present.shape, present.dtype), cube]
         + [block] * FIRST,
-        scratch_shapes=[pltpu.VMEM((1, width), F32), DMA((slots, 2)), DMA((2,))],
+        scratch_shapes=[
+            pltpu.VMEM((FIRST, width, width), F32),
+            pltpu.VMEM((FIRST, width, width), F32),
+            pltpu.VMEM((1, width), F32),
+            DMA((FIRST, 2)),
+            DMA((2,)),
+        ],
         compiler_params=PARAMS,
         cost_estimate=SMALL,
         name="first_blocks",
@@ -229,7 +231,7 @@
             compiler_params=PARAMS,
             cost_estimate=SMALL,
             name=name,
-        )(*vmem(amp, integ, gap, kept, *arrived))
+        )(*vmem(amplitude, integral, gap, kept, *arrived))
         return kept, sent
 
     def send(start, stop):
@@ -259,7 +261,7 @@
             cost_estimate=SMALL,
             name="update",
         )(
-            *vmem(integ, gap, flags, kept, *arrived[start:stop]),
+            *vmem(integral, gap, flags, kept, *arrived[start:stop]),
             *([] if first else [*hbm(before[0]), *vmem(before[1])]),
         )
 

time: 74.3 us -> 67.2 us (0.904)
  starting transfers between devices: 41 us -> 30.1 us
  waiting for transfers between devices: 1.26 us -> 8.71 us
  blocking collectives: 15.5 us -> 13.5 us
  Pallas kernels: 12.7 us -> 11.5 us
    ppermute x14, starting transfers between devices: 41 us -> 30.1 us  [send(): lax.ppermute(sent[number], 'row', rounds[number][0])]
    ppermute x14, waiting for transfers between devices: 1.26 us -> 8.71 us  [send(): lax.ppermute(sent[number], 'row', rounds[number][0])]
    all_to_all x1, blocking collectives: 15.5 us -> 13.5 us  [per_device(): every = lax.all_to_all(jnp.broadcast_to(summed, (count, 128)), 'row', 0, 0)]
    pallas_call x1, Pallas kernels: 4.76 us -> 3.16 us  [per_device(): pl.pallas_call(functools.partial(first_kernel, order[:FIRST]), in_specs=[...]
  transfers between devices with their start and end apart: 14 -> 14, of which waited for: 3 -> 5; matrix products, arithmetic and copies ran while one was open for 0% -> 0% of each run, Pallas kernels for 9% -> 10%
where the time goes in v3:
time: 67.2 us; the launch traced here: 67 us
  starting transfers between devices  30.1 us (45%)
  blocking collectives  13.5 us (20%)
  Pallas kernels  11.5 us (17%)
  waiting for transfers between devices  8.71 us (13%)
  between operations  2.51 us (4%)
    ppermute x14, starting transfers between devices, send(): lax.ppermute(sent[number], 'row', rounds[number][0])  30.1 us
    all_to_all x1, blocking collectives, per_device(): every = lax.all_to_all(jnp.broadcast_to(summed, (count, 128)), 'row', 0, 0)  13.5 us
    ppermute x14, waiting for transfers between devices, send(): lax.ppermute(sent[number], 'row', rounds[number][0])  8.71 us
    pallas_call x3, Pallas kernels, updates(): pl.pallas_call(functools.partial(update_kernel, some, first), in_specs=[I...  4.6 us
    pallas_call x2, Pallas kernels, cycles(): pl.pallas_call(functools.partial(cycle_kernel, some, passed, len(arrived)...  3.75 us
    pallas_call x1, Pallas kernels, per_device(): pl.pallas_call(functools.partial(first_kernel, order[:FIRST]), in_specs=[...  3.16 us
  transfers between devices with their start and end apart: 14, of which 5 were waited for; matrix products, arithmetic and copies ran while one was open for 0% of the time, Pallas kernels for 10%

profile of v3, /device:TPU:0, one launch (start us, length us, event | category | flops | bytes accessed | tf_op | source)
XLA Modules:
  0.0 67.0 jit_solution(13819682802786311952)
XLA Ops:
  0.6 0.0 copy-start
  0.6 0.0 copy-start.1
  0.7 3.2 %first_blocks.1 = (f32[8,256]{1,0:T(8,128)S(1)}, s32[1,15]{1,0:T(1,128)S(1)}, f32[15,256,256]{2,1,0:T(8,128)S(1)}, f32[264,256]{1,0:T(8,128)S(1)}, f32[264,256]{...) custom-call(f32[1,15,256,256]{3,2,1,0:T(8,128)} %amp_ref.3, f32[1,15,256,256]{3,2,1,0:T(8,128)} %int_ref.9, ...), custom_call_target="tpu_custom_call" | custom-call | flops 1 | bytes 1 | tf_op jit(solution)/shard_map/first_blocks/pallas_call | solution.py:203
  3.8 3.0 %collective-permute-start = (f32[264,256]{1,0:T(8,128)S(1)}, f32[264,256]{1,0:T(8,128)S(1)}, u32[]{:S(2)}, u32[]{:S(2)}) collective-permute-start(f32[264,256]{1,0:T(8,128)S(1)} %get-tuple-element.31), channel_id=1, source_target_pairs={{0,2},{1,7},{2,6},{4,0},{5,12},{6,3},{7,9},{8,10},{9,8},{10,14},{1... | collective-permute-start | bytes 811016 | tf_op jit(solution)/shard_map/ppermute | solution.py:238
  6.8 0.6 collective-permute-start.1
  7.4 2.5 %collective-permute-start.2 = (f32[264,256]{1,0:T(8,128)S(1)}, f32[264,256]{1,0:T(8,128)S(1)}, u32[]{:S(2)}, u32[]{:S(2)}) collective-permute-start(f32[264,256]{1,0:T(8,128)S(1)} %get-tuple-element.33), channel_id=1, source_target_pairs={{0,4},{1,0},{2,3},{4,11},{5,2},{6,7},{7,13},{8,9},{9,6},{10,5},{11... | collective-permute-start | bytes 811016 | tf_op jit(solution)/shard_map/ppermute | solution.py:238
  9.9 0.0 collective-permute-start.3
  9.9 0.0 copy-done
  9.9 0.0 copy-done.1
  9.9 1.5 %second_blocks.1 = (f32[15,256,256]{2,1,0:T(8,128)S(1)}, f32[264,256]{1,0:T(8,128)S(1)}, f32[264,256]{1,0:T(8,128)S(1)}, f32[264,256]{1,0:T(8,128)S(1)}, f32[264,256]{1,0:T(8,128)S(1)}) custom-call(f32[1,15,256,256]{3,2,1,0:T(8,128)S(1)} %copy-done.1, f32[1,15,256,256]{3,2,1,0:T(8,128)S(1)} %copy-done, ...), custom_call_target="tpu_custom_call", output_to_operand_aliasing={{0}: (3, {})} | custom-call | flops 1 | bytes 1 | tf_op jit(solution)/shard_map/second_blocks/pallas_call | solution.py:225
  11.4 1.3 %collective-permute-start.8 = (f32[264,256]{1,0:T(8,128)S(1)}, f32[264,256]{1,0:T(8,128)S(1)}, u32[]{:S(2)}, u32[]{:S(2)}) collective-permute-start(f32[264,256]{1,0:T(8,128)S(1)} %get-tuple-element.40), channel_id=1, source_target_pairs={{0,1},{1,5},{2,0},{3,2},{4,9},{5,7},{6,13},{7,6},{8,3},{9,15},{10,... | collective-permute-start | bytes 811016 | tf_op jit(solution)/shard_map/ppermute | solution.py:238
  12.7 4.0 %collective-permute-done.refs_0_ = f32[264,256]{1,0:T(8,128)S(1)} collective-permute-done((f32[264,256]{1,0:T(8,128)S(1)}, f32[264,256]{1,0:T(8,128)S(1)}, u32[]{:S(2)}, u32[]{:S(2)}) %collective-permute-start) | collective-permute-done | bytes 270368 | tf_op jit(solution)/shard_map/ppermute | solution.py:238
  16.7 0.0 collective-permute-start.9
  16.7 0.0 collective-permute-done.1.refs_1_
  16.7 8.6 %collective-permute-start.10 = (f32[264,256]{1,0:T(8,128)S(1)}, f32[264,256]{1,0:T(8,128)S(1)}, u32[]{:S(2)}, u32[]{:S(2)}) collective-permute-start(f32[264,256]{1,0:T(8,128)S(1)} %get-tuple-element.42), channel_id=1, source_target_pairs={{0,6},{1,3},{2,5},{3,1},{4,10},{5,0},{6,11},{7,2},{8,12},{9,4},{10... | collective-permute-start | bytes 811016 | tf_op jit(solution)/shard_map/ppermute | solution.py:238
  25.2 0.0 collective-permute-done.2.refs_2_
  25.2 0.0 collective-permute-start.13
  25.2 0.0 collective-permute-done.3.refs_3_
  25.2 2.3 %third_blocks.1 = (f32[15,256,256]{2,1,0:T(8,128)S(1)}, f32[264,256]{1,0:T(8,128)S(1)}, f32[264,256]{1,0:T(8,128)S(1)}, f32[264,256]{1,0:T(8,128)S(1)}, f32[264,...) custom-call(f32[1,15,256,256]{3,2,1,0:T(8,128)S(1)} %copy-done.1, ...), custom_call_target="tpu_custom_call", output_to_operand_aliasing={{0}: (3, {})} | custom-call | flops 1 | bytes 1 | tf_op jit(solution)/shard_map/third_blocks/pallas_call | solution.py:225
  27.5 1.2 %collective-permute-start.11 = (f32[264,256]{1,0:T(8,128)S(1)}, f32[264,256]{1,0:T(8,128)S(1)}, u32[]{:S(2)}, u32[]{:S(2)}) collective-permute-start(f32[264,256]{1,0:T(8,128)S(1)} %get-tuple-element.43), channel_id=1, source_target_pairs={{0,1},{2,3},{3,0},{4,5},{5,6},{6,4},{7,8},{8,14},{9,2},{10,11},{11... | collective-permute-start | bytes 811016 | tf_op jit(solution)/shard_map/ppermute | solution.py:238
  28.7 0.0 collective-permute-done.8.refs_0_
  28.7 0.1 collective-permute-start.4
  28.7 0.0 collective-permute-done.9.refs_1_
  28.7 3.0 %collective-permute-start.12 = (f32[264,256]{1,0:T(8,128)S(1)}, f32[264,256]{1,0:T(8,128)S(1)}, u32[]{:S(2)}, u32[]{:S(2)}) collective-permute-start(f32[264,256]{1,0:T(8,128)S(1)} %get-tuple-element.44), channel_id=1, source_target_pairs={{1,2},{2,3},{3,10},{4,0},{5,4},{6,5},{7,1},{8,15},{9,7},{10,6},{11... | collective-permute-start | bytes 811016 | tf_op jit(solution)/shard_map/ppermute | solution.py:238
  31.7 0.0 collective-permute-done.10.refs_2_
  31.7 3.1 %collective-permute-start.5 = (f32[264,256]{1,0:T(8,128)S(1)}, f32[264,256]{1,0:T(8,128)S(1)}, u32[]{:S(2)}, u32[]{:S(2)}) collective-permute-start(f32[264,256]{1,0:T(8,128)S(1)} %get-tuple-element.37), channel_id=1, source_target_pairs={{0,3},{2,0},{3,6},{4,1},{5,4},{6,2},{7,11},{8,5},{9,12},{10,15},{1... | collective-permute-start | bytes 811016 | tf_op jit(solution)/shard_map/ppermute | solution.py:238
  34.8 0.0 collective-permute-done.13.refs_4_
  34.8 6.9 %collective-permute-start.6 = (f32[264,256]{1,0:T(8,128)S(1)}, f32[264,256]{1,0:T(8,128)S(1)}, u32[]{:S(2)}, u32[]{:S(2)}) collective-permute-start(f32[264,256]{1,0:T(8,128)S(1)} %get-tuple-element.38), channel_id=1, source_target_pairs={{0,5},{1,0},{2,3},{3,4},{4,6},{5,10},{6,1},{7,12},{8,2},{9,14},{10... | collective-permute-start | bytes 811016 | tf_op jit(solution)/shard_map/ppermute | solution.py:238
  41.7 0.6 collective-permute-done.11.refs_3_
  42.3 0.0 collective-permute-start.7
  42.3 1.6 %update.3 = (f32[1,15,256,256]{3,2,1,0:T(8,128)}, f32[8,256]{1,0:T(8,128)S(1)}) custom-call(f32[1,15,256,256]{3,2,1,0:T(8,128)S(1)} %copy-done, f32[8,256]{1,0:T(8,128)S(1)} %get-tuple-element.27.gap_ref, s32[1,15]{1,0:T(1,128)S(1)} %get-tuple-element.28.present_ref, f32[15,256,256]{2,1,0:T(8,128)S(1)} %get-tuple-element.35.kept_ref, ...), custom_call_target="tpu_custom_call" | custom-call | flops 1 | bytes 1 | tf_op jit(solution)/shard_map/update/pallas_call | solution.py:253
  43.9 0.0 collective-permute-done.12.refs_4_
  43.9 1.5 %update.4 = (f32[1,15,256,256]{3,2,1,0:T(8,128)}, f32[8,256]{1,0:T(8,128)S(1)}) custom-call(f32[1,15,256,256]{3,2,1,0:T(8,128)S(1)} %copy-done, f32[8,256]{1,0:T(8,128)S(1)} %get-tuple-element.27.gap_ref, s32[1,15]{1,0:T(1,128)S(1)} %get-tuple-element.28.present_ref, ...), custom_call_target="tpu_custom_call", output_to_operand_aliasing={{0}: (9, {})} | custom-call | flops 1 | bytes 1 | tf_op jit(solution)/shard_map/update/pallas_call | solution.py:253
  45.5 0.0 collective-permute-done.4.refs_0_
  45.5 1.0 %collective-permute-done.5.refs_1_ = f32[264,256]{1,0:T(8,128)S(1)} collective-permute-done((f32[264,256]{1,0:T(8,128)S(1)}, f32[264,256]{1,0:T(8,128)S(1)}, u32[]{:S(2)}, u32[]{:S(2)}) %collective-permute-start.5) | collective-permute-done | bytes 270368 | tf_op jit(solution)/shard_map/ppermute | solution.py:238
  46.5 0.2 collective-permute-done.6.refs_2_
  46.7 2.9 %collective-permute-done.7.refs_3_ = f32[264,256]{1,0:T(8,128)S(1)} collective-permute-done((f32[264,256]{1,0:T(8,128)S(1)}, f32[264,256]{1,0:T(8,128)S(1)}, u32[]{:S(2)}, u32[]{:S(2)}) %collective-permute-start.7) | collective-permute-done | bytes 270368 | tf_op jit(solution)/shard_map/ppermute | solution.py:238
  49.6 1.4 %update.5 = (f32[1,15,256,256]{3,2,1,0:T(8,128)}, f32[8,256]{1,0:T(8,128)S(1)}) custom-call(f32[1,15,256,256]{3,2,1,0:T(8,128)S(1)} %copy-done, f32[8,256]{1,0:T(8,128)S(1)} %get-tuple-element.27.gap_ref, s32[1,15]{1,0:T(1,128)S(1)} %get-tuple-element.28.present_ref, ...), custom_call_target="tpu_custom_call", output_to_operand_aliasing={{0}: (8, {})} | custom-call | flops 1 | bytes 1 | tf_op jit(solution)/shard_map/update/pallas_call | solution.py:253
  51.1 13.5 %all_to_all.6 = f32[16,1,128]{2,1,0:T(1,128)S(1)} all-to-all(f32[16,1,128]{2,1,0:T(1,128)S(1)} %broadcast_in_dim.3), channel_id=1, replica_groups=mesh['mol'=2,'row'=16] {'row'}, dimensions={0} | all-to-all | bytes 16384 | tf_op jit(solution)/shard_map/all_to_all | solution.py:274
  64.6 0.6 reduce_sum.29
  (3 shorter events, 0.0 us)
Async XLA Ops:
  0.6 9.3 %copy-start = (f32[1,15,256,256]{3,2,1,0:T(8,128)S(1)}, f32[1,15,256,256]{3,2,1,0:T(8,128)}, u32[]{:S(2)}) copy-start(f32[1,15,256,256]{3,2,1,0:T(8,128)} %int_ref.9) | copy-start | bytes 11796484
  0.6 9.3 %copy-start.1 = (f32[1,15,256,256]{3,2,1,0:T(8,128)S(1)}, f32[1,15,256,256]{3,2,1,0:T(8,128)}, u32[]{:S(2)}) copy-start(f32[1,15,256,256]{3,2,1,0:T(8,128)} %amp_ref.3) | copy-start | bytes 11796484
  3.8 12.8 %collective-permute-start = (f32[264,256]{1,0:T(8,128)S(1)}, f32[264,256]{1,0:T(8,128)S(1)}, u32[]{:S(2)}, u32[]{:S(2)}) collective-permute-start(f32[264,256]{1,0:T(8,128)S(1)} %get-tuple-element.31), channel_id=1, source_target_pairs={{0,2},{1,7},{2,6},{4,0},{5,12},{6,3},{7,9},{8,10},{9,8},{10,14},{1... | collective-permute-start | bytes 811016 | tf_op jit(solution)/shard_map/ppermute | solution.py:238
  6.8 9.8 %collective-permute-start.1 = (f32[264,256]{1,0:T(8,128)S(1)}, f32[264,256]{1,0:T(8,128)S(1)}, u32[]{:S(2)}, u32[]{:S(2)}) collective-permute-start(f32[264,256]{1,0:T(8,128)S(1)} %get-tuple-element.32), channel_id=1, source_target_pairs={{0,1},{1,8},{3,7},{4,2},{5,4},{6,10},{7,5},{8,6},{9,12},{10,3},{11... | collective-permute-start | bytes 811016 | tf_op jit(solution)/shard_map/ppermute | solution.py:238
  7.4 17.8 %collective-permute-start.2 = (f32[264,256]{1,0:T(8,128)S(1)}, f32[264,256]{1,0:T(8,128)S(1)}, u32[]{:S(2)}, u32[]{:S(2)}) collective-permute-start(f32[264,256]{1,0:T(8,128)S(1)} %get-tuple-element.33), channel_id=1, source_target_pairs={{0,4},{1,0},{2,3},{4,11},{5,2},{6,7},{7,13},{8,9},{9,6},{10,5},{11... | collective-permute-start | bytes 811016 | tf_op jit(solution)/shard_map/ppermute | solution.py:238
  9.9 15.3 %collective-permute-start.3 = (f32[264,256]{1,0:T(8,128)S(1)}, f32[264,256]{1,0:T(8,128)S(1)}, u32[]{:S(2)}, u32[]{:S(2)}) collective-permute-start(f32[264,256]{1,0:T(8,128)S(1)} %get-tuple-element.34), channel_id=1, source_target_pairs={{0,2},{1,6},{3,5},{4,8},{5,1},{6,9},{7,3},{8,4},{9,11},{10,7},{11,... | collective-permute-start | bytes 811016 | tf_op jit(solution)/shard_map/ppermute | solution.py:238
  11.4 17.3 %collective-permute-start.8 = (f32[264,256]{1,0:T(8,128)S(1)}, f32[264,256]{1,0:T(8,128)S(1)}, u32[]{:S(2)}, u32[]{:S(2)}) collective-permute-start(f32[264,256]{1,0:T(8,128)S(1)} %get-tuple-element.40), channel_id=1, source_target_pairs={{0,1},{1,5},{2,0},{3,2},{4,9},{5,7},{6,13},{7,6},{8,3},{9,15},{10,... | collective-permute-start | bytes 811016 | tf_op jit(solution)/shard_map/ppermute | solution.py:238
  16.7 12.1 %collective-permute-start.9 = (f32[264,256]{1,0:T(8,128)S(1)}, f32[264,256]{1,0:T(8,128)S(1)}, u32[]{:S(2)}, u32[]{:S(2)}) collective-permute-start(f32[264,256]{1,0:T(8,128)S(1)} %get-tuple-element.41), channel_id=1, source_target_pairs={{0,7},{1,0},{2,1},{3,2},{4,5},{5,9},{6,8},{7,4},{8,11},{9,3},{10,1... | collective-permute-start | bytes 811016 | tf_op jit(solution)/shard_map/ppermute | solution.py:238
  16.7 15.0 %collective-permute-start.10 = (f32[264,256]{1,0:T(8,128)S(1)}, f32[264,256]{1,0:T(8,128)S(1)}, u32[]{:S(2)}, u32[]{:S(2)}) collective-permute-start(f32[264,256]{1,0:T(8,128)S(1)} %get-tuple-element.42), channel_id=1, source_target_pairs={{0,6},{1,3},{2,5},{3,1},{4,10},{5,0},{6,11},{7,2},{8,12},{9,4},{10... | collective-permute-start | bytes 811016 | tf_op jit(solution)/shard_map/ppermute | solution.py:238
  25.2 9.6 %collective-permute-start.13 = (f32[264,256]{1,0:T(8,128)S(1)}, f32[264,256]{1,0:T(8,128)S(1)}, u32[]{:S(2)}, u32[]{:S(2)}) collective-permute-start(f32[264,256]{1,0:T(8,128)S(1)} %get-tuple-element.45), channel_id=1, source_target_pairs={{0,3},{1,4},{2,7},{3,2},{4,6},{5,8},{6,12},{7,0},{8,1},{9,10},{10,... | collective-permute-start | bytes 811016 | tf_op jit(solution)/shard_map/ppermute | solution.py:238
  27.5 14.8 %collective-permute-start.11 = (f32[264,256]{1,0:T(8,128)S(1)}, f32[264,256]{1,0:T(8,128)S(1)}, u32[]{:S(2)}, u32[]{:S(2)}) collective-permute-start(f32[264,256]{1,0:T(8,128)S(1)} %get-tuple-element.43), channel_id=1, source_target_pairs={{0,1},{2,3},{3,0},{4,5},{5,6},{6,4},{7,8},{8,14},{9,2},{10,11},{11... | collective-permute-start | bytes 811016 | tf_op jit(solution)/shard_map/ppermute | solution.py:238
  28.7 16.8 %collective-permute-start.4 = (f32[264,256]{1,0:T(8,128)S(1)}, f32[264,256]{1,0:T(8,128)S(1)}, u32[]{:S(2)}, u32[]{:S(2)}) collective-permute-start(f32[264,256]{1,0:T(8,128)S(1)} %get-tuple-element.36), channel_id=1, source_target_pairs={{0,1},{1,5},{2,4},{3,2},{4,3},{5,11},{6,0},{7,10},{8,7},{9,13},{10... | collective-permute-start | bytes 811016 | tf_op jit(solution)/shard_map/ppermute | solution.py:238
  28.7 15.2 %collective-permute-start.12 = (f32[264,256]{1,0:T(8,128)S(1)}, f32[264,256]{1,0:T(8,128)S(1)}, u32[]{:S(2)}, u32[]{:S(2)}) collective-permute-start(f32[264,256]{1,0:T(8,128)S(1)} %get-tuple-element.44), channel_id=1, source_target_pairs={{1,2},{2,3},{3,10},{4,0},{5,4},{6,5},{7,1},{8,15},{9,7},{10,6},{11... | collective-permute-start | bytes 811016 | tf_op jit(solution)/shard_map/ppermute | solution.py:238
  31.7 14.8 %collective-permute-start.5 = (f32[264,256]{1,0:T(8,128)S(1)}, f32[264,256]{1,0:T(8,128)S(1)}, u32[]{:S(2)}, u32[]{:S(2)}) collective-permute-start(f32[264,256]{1,0:T(8,128)S(1)} %get-tuple-element.37), channel_id=1, source_target_pairs={{0,3},{2,0},{3,6},{4,1},{5,4},{6,2},{7,11},{8,5},{9,12},{10,15},{1... | collective-permute-start | bytes 811016 | tf_op jit(solution)/shard_map/ppermute | solution.py:238
  34.8 11.8 %collective-permute-start.6 = (f32[264,256]{1,0:T(8,128)S(1)}, f32[264,256]{1,0:T(8,128)S(1)}, u32[]{:S(2)}, u32[]{:S(2)}) collective-permute-start(f32[264,256]{1,0:T(8,128)S(1)} %get-tuple-element.38), channel_id=1, source_target_pairs={{0,5},{1,0},{2,3},{3,4},{4,6},{5,10},{6,1},{7,12},{8,2},{9,14},{10... | collective-permute-start | bytes 811016 | tf_op jit(solution)/shard_map/ppermute | solution.py:238
  42.3 7.3 %collective-permute-start.7 = (f32[264,256]{1,0:T(8,128)S(1)}, f32[264,256]{1,0:T(8,128)S(1)}, u32[]{:S(2)}, u32[]{:S(2)}) collective-permute-start(f32[264,256]{1,0:T(8,128)S(1)} %get-tuple-element.39), channel_id=1, source_target_pairs={{1,0},{2,1},{3,2},{4,7},{5,3},{6,4},{7,14},{8,13},{9,5},{10,11},{1... | collective-permute-start | bytes 811016 | tf_op jit(solution)/shard_map/ppermute | solution.py:238

commit v4 on v3

--- a/solution.py
+++ b/solution.py
@@ -9,32 +9,33 @@
 
 F32 = jnp.float32
 EXTRA = 8
+HALF = 128
 
 SENDS = (
-    (2, 7, 6, -1, 16, 12, 3, 9, 10, 8, 14, 4, 5, -1, 13, 11),
-    (17, 8, -1, 7, 2, 4, 10, 5, 6, 12, 3, 15, -1, 11, 9, 29),
-    (4, 0, 19, -1, 11, 2, 7, 13, 9, 6, 5, 10, -1, 28, 31, 8),
-    (18, 6, -1, 5, 8, 1, 9, 3, 4, 11, 7, 14, 29, -1, 10, 28),
-    (19, 4, 7, 18, 22, 8, 12, 0, 1, 10, 9, 5, 29, 31, 27, 30),
-    (17, 5, 0, 18, 9, 7, 13, 6, 3, 15, 4, 26, 11, 12, 8, 30),
-    (7, 16, 17, 18, 21, 9, 8, 4, 11, 3, 12, 6, 29, 30, 15, 10),
-    (6, 3, 5, 1, 10, 0, 11, 2, 12, 4, 13, 9, 8, 15, 7, 30),
-    (1, -1, 19, 0, 5, 6, 4, 8, 14, 2, 27, 13, 10, 28, 31, -1),
-    (-1, 2, 19, 10, 0, 20, 5, 1, 15, 7, 6, 12, 29, 25, 11, 14),
-    (17, 21, 4, 2, 3, 11, 0, 10, 7, 13, 8, 31, 14, 9, 12, -1),
-    (3, -1, 16, 6, 1, 20, 2, 11, 5, 28, 15, 26, 9, 14, -1, 13),
-    (5, 16, 3, 4, 6, 10, 1, 12, 2, 14, 11, 7, 13, 8, 31, 9),
-    (-1, 16, 1, 18, 7, 3, 20, 14, 13, 5, 27, 8, 15, 10, -1, 12),
+    (3, 5, -1, 6, 1, 8, 11, 2, 7, 13, 4, 14, 10, -1, 9, 12),
+    (17, 8, -1, 7, 3, 6, 18, 9, 5, 10, 14, 4, 29, -1, 27, 28),
+    (18, 6, 5, -1, 11, 0, 10, 3, 4, 8, 7, 31, -1, 28, 13, 9),
+    (5, 0, 3, -1, 8, 7, 13, 4, 2, 12, 9, 6, -1, 10, 15, 11),
+    (2, 7, 19, 0, 17, 10, 8, 6, 9, 4, 5, 15, 14, 28, 11, 13),
+    (18, 4, 6, 16, 21, 12, 3, 10, 1, 11, 13, 8, 31, 9, 7, 30),
+    (6, 3, 4, 18, 10, 1, 0, 14, 12, 5, 27, 7, 9, 31, 29, 8),
+    (4, 16, 17, 18, 9, 3, 7, 13, 14, 6, 27, 5, 8, 28, 31, 10),
+    (20, 16, 1, 10, 7, 9, 2, 5, 13, 3, 6, 12, 11, 15, 8, 30),
+    (1, -1, 7, 2, 5, 4, 9, 0, 3, 14, 15, 26, 29, 11, 12, -1),
+    (7, 16, 19, 1, 21, 11, 4, 12, 15, 2, 8, 10, 13, 25, -1, 14),
+    (17, -1, 0, 22, 2, 20, 5, 8, 11, 7, 3, 13, 15, 12, 10, 30),
+    (-1, 2, 19, 5, 0, 20, 1, 11, 6, 15, 12, 26, 29, 8, -1, 30),
+    (-1, 16, 19, 4, 6, 2, 12, 1, 10, 29, 11, 9, 5, 14, 31, -1),
 )
 RELAYS = (
-    (3, 1, 8, 0, 11),
-    (13, 15, 6, 0, 10),
-    (2, 0, 8, 1, 9),
-    (12, 14, 6, 1, 13),
-    (3, 1, 9, 2, 8),
-    (12, 14, 7, 2, 11),
-    (2, 0, 9, 3, 13),
-    (13, 15, 7, 3, 8),
+    (2, 0, 9, 0, 12),
+    (13, 15, 6, 0, 9),
+    (2, 0, 8, 1, 13),
+    (13, 15, 7, 1, 13),
+    (3, 1, 8, 2, 9),
+    (12, 14, 7, 2, 12),
+    (3, 1, 9, 3, 11),
+    (12, 14, 6, 3, 10),
 )
 
 
@@ -100,12 +101,18 @@
     return product(split(amp), split(inner))
 
 
-def put_cycle(amp, integ, gap_rows, kept_ref, out_ref):
+def halves(value):
+    return [value[:, :HALF], value[:, HALF:]]
+
+
+def put_cycle(amp, integ, gap_row, kept_ref, out_ref):
     cycle = cycle_of(amp, integ)
     kept_ref[...] = cycle
     if out_ref is not None:
-        out_ref[: cycle.shape[0], :] = cycle
-        out_ref[cycle.shape[0] :, :] = gap_rows
+        height = cycle.shape[0]
+        for side, part in enumerate(halves(cycle)):
+            out_ref[pl.ds(side * height, height), :] = part
+        out_ref[pl.ds(2 * height, EXTRA), :] = jnp.concatenate(halves(gap_row) * (EXTRA // 2), axis=0)
 
 
 def first_kernel(order, amp_hbm, int_hbm, gap_hbm, present_hbm, *refs):
@@ -125,10 +132,9 @@
     loads[-1].start()
     for copy in loads:
         copy.wait()
-    gap_rows = jnp.broadcast_to(gap_buf[...], (EXTRA, amp_buf.shape[-1]))
-    gap_ref[...] = gap_rows
+    gap_ref[...] = jnp.broadcast_to(gap_buf[...], gap_ref.shape)
     for number, index in enumerate(places):
-        put_cycle(amp_buf[number], int_buf[number], gap_rows, kept_ref.at[index], outs[number])
+        put_cycle(amp_buf[number], int_buf[number], gap_buf[...], kept_ref.at[index], outs[number])
 
 
 def cycle_kernel(order, relays, arrays, amp_ref, int_ref, gap_ref, _, *refs):
@@ -136,7 +142,7 @@
     here = lax.axis_index("row")
     for slot, out_ref in zip(order, [*outs, None]):
         index = lookup(slot, here)
-        put_cycle(amp_ref[0, index], int_ref[0, index], gap_ref[...], kept_ref.at[index], out_ref)
+        put_cycle(amp_ref[0, index], int_ref[0, index], gap_ref[:1, :], kept_ref.at[index], out_ref)
     for row, output, array in relays:
 
         @pl.when(here == row)
@@ -144,11 +150,14 @@
             outs[output][...] = arrived[array][...]
 
 
-def update_kernel(slots, first, int_ref, gap_ref, present_ref, kept_ref, *refs):
+def update_kernel(slots, first, held, int_ref, gap_ref, present_ref, kept_ref, *refs):
     arrived, refs = refs[: len(slots)], refs[len(slots) :]
     if not first:
-        before_ref, refs = refs[1], refs[2:]
-    out_ref, part_ref, out_buf, out_sem = refs
+        before_ref, refs = refs[-3 - 2 * (not held)], refs[-2 - 2 * (not held) :]
+    if held:
+        fresh_ref, part_ref = refs
+    else:
+        out_ref, part_ref, fresh_ref, out_sem = refs
     width = int_ref.shape[-1]
     middle = (present_ref.shape[1] - 1) // 2
     here = lax.axis_index("row")
@@ -160,17 +169,33 @@
         items.append((middle, None))
     for number, (index, ref) in enumerate(items):
         integ, mine = int_ref[0, index], kept_ref[index]
-        theirs = mine if ref is None else ref[:width, :]
-        gap_other = gap_ref[:1, :] if ref is None else ref[width : width + 1, :]
+        if ref is None:
+            theirs, gap_other = mine.T, gap_ref[:1, :]
+        else:
+            theirs = jnp.concatenate([ref[pl.ds(side * width, width), :].T for side in range(2)], axis=0)
+            gap_other = jnp.concatenate([ref[pl.ds(2 * width + side, 1), :] for side in range(2)], axis=1)
         at_slot = lax.broadcasted_iota(jnp.int32, present_ref.shape, 1) == index
         flag = jnp.sum(jnp.where(at_slot, present_ref[...], 0), axis=1, keepdims=True)
-        total = integ + mine + theirs.T
+        total = integ + mine + theirs
         fresh = jnp.where(flag > 0, total / (gap_column + gap_other), F32(0.0))
-        out_buf[number] = fresh
-        stores.append(pltpu.make_async_copy(out_buf.at[number], out_ref.at[0, index], out_sem.at[number]))
-        stores[-1].start()
+        fresh_ref[number] = fresh
+        if not held:
+            stores.append(pltpu.make_async_copy(fresh_ref.at[number], out_ref.at[0, index], out_sem.at[number]))
+            stores[-1].start()
         part = part + jnp.sum((fresh * integ).reshape(width // 8, 8, width), axis=0)
     part_ref[...] = part
+    for copy in stores:
+        copy.wait()
+
+
+def store_kernel(slots, _, *refs):
+    *fresh, out_ref, out_sem = refs
+    here = lax.axis_index("row")
+    blocks = [ref.at[number] for ref in fresh for number in range(ref.shape[0])]
+    stores = []
+    for number, (slot, block) in enumerate(zip(slots, blocks)):
+        stores.append(pltpu.make_async_copy(block, out_ref.at[0, lookup(slot, here)], out_sem.at[number]))
+        stores[-1].start()
     for copy in stores:
         copy.wait()
 
@@ -180,14 +205,14 @@
 IN_VMEM = pl.BlockSpec(memory_space=pltpu.VMEM)
 DMA = pltpu.SemaphoreType.DMA
 SMALL = pl.CostEstimate(flops=1, bytes_accessed=1, transcendentals=0)
-FIRST, SECOND = 4, 8
-UPDATES = (0, 5, 10, 14)
+CYCLES = (0, 2, 5, 8, 14)
+UPDATES = (0, 5, 9, 10, 11, 12, 13, 14)
+HELD = 1
 
 
 def per_device(amplitude, integral, pair_gap, present):
     slots, width = amplitude.shape[1], amplitude.shape[2]
     reach = (slots - 1) // 2
-    height = width + EXTRA
     count = lax.axis_size("row")
     rounds, relays = rounds_of(count, reach)
     order = [turn[1] for turn in rounds] + [[reach]]
@@ -199,18 +224,19 @@
         return [pltpu.with_memory_space_constraint(value, pltpu.VMEM) for value in values]
 
     cube = pltpu.VMEM((slots, width, width), F32)
-    block = pltpu.VMEM((height, width), F32)
+    block = pltpu.VMEM((2 * width + EXTRA, HALF), F32)
+    first = CYCLES[1]
     gap, flags, kept, *sent = pl.pallas_call(
-        functools.partial(first_kernel, order[:FIRST]),
+        functools.partial(first_kernel, order[:first]),
         in_specs=[IN_HBM] * 4,
-        out_specs=[IN_VMEM] * (3 + FIRST),
+        out_specs=[IN_VMEM] * (3 + first),
         out_shape=[pltpu.VMEM((EXTRA, width), F32), pltpu.VMEM(present.shape, present.dtype), cube]
-        + [block] * FIRST,
+        + [block] * first,
         scratch_shapes=[
-            pltpu.VMEM((FIRST, width, width), F32),
-            pltpu.VMEM((FIRST, width, width), F32),
+            pltpu.VMEM((first, width, width), F32),
+            pltpu.VMEM((first, width, width), F32),
             pltpu.VMEM((1, width), F32),
-            DMA((FIRST, 2)),
+            DMA((first, 2)),
             DMA((2,)),
         ],
         compiler_params=PARAMS,
@@ -218,7 +244,7 @@
         name="first_blocks",
     )(*hbm(amplitude, integral, pair_gap, present))
 
-    def cycles(name, start, stop, kept, arrived):
+    def cycles(start, stop, kept, arrived):
         passed = [(by, second - start, first) for _, by, _, first, second in relays if start <= second < stop]
         arrived = arrived if passed else []
         some = order[start:stop] + ([order[-1]] if stop == len(rounds) else [])
@@ -230,45 +256,62 @@
             input_output_aliases={3: 0},
             compiler_params=PARAMS,
             cost_estimate=SMALL,
-            name=name,
+            name="cycle_blocks",
         )(*vmem(amplitude, integral, gap, kept, *arrived))
         return kept, sent
 
     def send(start, stop):
         return [lax.ppermute(sent[number], "row", rounds[number][0]) for number in range(start, stop)]
 
-    arrived = send(0, FIRST)
-    kept, more = cycles("second_blocks", FIRST, SECOND, kept, [])
-    sent += more
-    arrived += send(FIRST, SECOND)
-    passing = 1 + max([first for _, _, _, first, _ in relays], default=-1)
-    kept, more = cycles("third_blocks", SECOND, len(rounds), kept, arrived[:passing])
-    sent += more
-    arrived += send(SECOND, len(rounds))
-
-    def updates(start, stop, before):
+    arrived = send(0, first)
+    passing = 1 + max([hop for _, _, _, hop, _ in relays], default=-1)
+    for start, stop in zip(CYCLES[1:-1], CYCLES[2:]):
+        kept, more = cycles(start, stop, kept, arrived[:passing])
+        sent += more
+        arrived += send(start, stop)
+
+    def updates(start, stop, held, before):
         some = [turn[2] for turn in rounds[start:stop]]
-        first = before is None
+        first = start == 0
         n = len(some) + int(first)
+        fresh = pltpu.VMEM((n, width, width), F32)
+        part = pltpu.VMEM((8, width), F32)
         return pl.pallas_call(
-            functools.partial(update_kernel, some, first),
-            in_specs=[IN_VMEM] * (4 + len(some)) + ([] if first else [IN_HBM, IN_VMEM]),
-            out_specs=[IN_HBM, IN_VMEM],
-            out_shape=[pltpu.HBM((1, slots, width, width), F32), pltpu.VMEM((8, width), F32)],
-            scratch_shapes=[pltpu.VMEM((n, width, width), F32), DMA((n,))],
-            input_output_aliases={} if first else {4 + len(some): 0},
+            functools.partial(update_kernel, some, first, held),
+            in_specs=[IN_VMEM] * (4 + len(some)) + ([] if first else [IN_VMEM] if held else [IN_HBM, IN_VMEM]),
+            out_specs=[IN_VMEM if held else IN_HBM, IN_VMEM],
+            out_shape=[fresh if held else pltpu.HBM((1, slots, width, width), F32), part],
+            scratch_shapes=[] if held else [fresh, DMA((n,))],
+            input_output_aliases={} if first or held else {4 + len(some): 0},
             compiler_params=PARAMS,
             cost_estimate=SMALL,
-            name="update",
+            name="held_update" if held else "update",
         )(
             *vmem(integral, gap, flags, kept, *arrived[start:stop]),
-            *([] if first else [*hbm(before[0]), *vmem(before[1])]),
+            *([] if first or held else hbm(before[0])),
+            *([] if first else vmem(before[1])),
         )
 
-    state = None
-    for start, stop in zip(UPDATES[:-1], UPDATES[1:]):
-        state = updates(start, stop, state)
-    updated, part = state
+    state, fresh = None, []
+    for number, (start, stop) in enumerate(zip(UPDATES[:-1], UPDATES[1:])):
+        state = updates(start, stop, number >= HELD, state)
+        if number < HELD:
+            updated = state[0]
+        else:
+            fresh.append(state[0])
+    part = state[1]
+    some = [turn[2] for turn in rounds[UPDATES[HELD] :]]
+    updated = pl.pallas_call(
+        functools.partial(store_kernel, some),
+        in_specs=[IN_HBM] + [IN_VMEM] * len(fresh),
+        out_specs=IN_HBM,
+        out_shape=pltpu.HBM((1, slots, width, width), F32),
+        scratch_shapes=[DMA((len(some),))],
+        input_output_aliases={0: 0},
+        compiler_params=PARAMS,
+        cost_estimate=SMALL,
+        name="store",
+    )(*hbm(updated), *vmem(*fresh))
 
     summed = jnp.sum(part, axis=0).reshape(-1, 128).sum(axis=0)
     every = lax.all_to_all(jnp.broadcast_to(summed, (count, 128)), "row", 0, 0)

time: 67.2 us -> 64.6 us (0.961)
  blocking collectives: 13.5 us -> 0 us
  waiting for transfers between devices: 8.71 us -> 14 us
  starting transfers between devices: 30.1 us -> 34.6 us
    all_to_all x1 -> x0, blocking collectives: 13.5 us -> none  [per_device(): every = lax.all_to_all(jnp.broadcast_to(summed, (count, 128)), 'row', 0, 0)]
    all_to_all x0 -> x1, waiting for transfers between devices: none -> 4.9 us  [per_device(): every = lax.all_to_all(jnp.broadcast_to(summed, (count, 128)), 'row', 0, 0)]
    all_to_all x0 -> x1, starting transfers between devices: none -> 4.83 us  [per_device(): every = lax.all_to_all(jnp.broadcast_to(summed, (count, 128)), 'row', 0, 0)]
    pallas_call x2 -> x3, Pallas kernels: 3.75 us -> 4.56 us  [cycles(): pl.pallas_call(functools.partial(cycle_kernel, some, passed, len(arrived)...]
    pallas_call x4 -> x9, Pallas kernels: 7.76 us -> 7.46 us  [the longest x7 3.59 us: updates(): pl.pallas_call(functools.partial(update_kernel, some, first, held), in_sp...]
  transfers between devices with their start and end apart: 14 -> 15, of which waited for: 5 -> 5; matrix products, arithmetic and copies ran while one was open for 0% -> 0% of each run, Pallas kernels for 10% -> 15%
where the time goes in v4:
time: 64.6 us; the launch traced here: 64.4 us
  starting transfers between devices  34.6 us (54%)
  waiting for transfers between devices  14 us (22%)
  Pallas kernels  12 us (19%)
  between operations  2.57 us (4%)
    ppermute x14, starting transfers between devices, send(): lax.ppermute(sent[number], 'row', rounds[number][0])  29.8 us
    ppermute x14, waiting for transfers between devices, send(): lax.ppermute(sent[number], 'row', rounds[number][0])  9.08 us
    all_to_all x1, waiting for transfers between devices, per_device(): every = lax.all_to_all(jnp.broadcast_to(summed, (count, 128)), 'row', 0, 0)  4.9 us
    all_to_all x1, starting transfers between devices, per_device(): every = lax.all_to_all(jnp.broadcast_to(summed, (count, 128)), 'row', 0, 0)  4.83 us
    pallas_call x3, Pallas kernels, cycles(): pl.pallas_call(functools.partial(cycle_kernel, some, passed, len(arrived)...  4.56 us
    pallas_call x7, Pallas kernels, updates(): pl.pallas_call(functools.partial(update_kernel, some, first, held), in_sp...  3.59 us
    pallas_call x1, Pallas kernels, per_device(): pl.pallas_call(functools.partial(first_kernel, order[:first]), in_specs=[...  2.39 us
    pallas_call x1, Pallas kernels, per_device(): pl.pallas_call(functools.partial(store_kernel, some), in_specs=[IN_HBM] +...  1.49 us
  transfers between devices with their start and end apart: 15, of which 5 were waited for; matrix products, arithmetic and copies ran while one was open for 0% of the time, Pallas kernels for 15%

profile of v4, /device:TPU:0, one launch (start us, length us, event | category | flops | bytes accessed | tf_op | source)
XLA Modules:
  0.0 64.4 jit_solution(267592128254621039)
XLA Ops:
  0.6 0.0 copy-start
  0.6 0.0 copy-start.1
  0.7 2.4 %first_blocks.1 = (f32[8,256]{1,0:T(8,128)S(1)}, s32[1,15]{1,0:T(1,128)S(1)}, f32[15,256,256]{2,1,0:T(8,128)S(1)}, f32[520,128]{1,0:T(8,128)S(1)}, f32[520,128]{1,0:T(8,128)S(1)}) custom-call(f32[1,15,256,256]{3,2,1,0:T(8,128)} %amp_ref.5, f32[1,15,256,256]{3,2,1,0:T(8,128)} %int_ref.19, f32[1,256]{1,0:T(1,128)} %gap_hbm.1, s32[1,15]{1,0:T(1,128)} %present_hbm.1), custom_call_target="tpu_custom_call" | custom-call | flops 1 | bytes 1 | tf_op jit(solution)/shard_map/first_blocks/pallas_call | solution.py:229
  3.0 2.5 %collective-permute-start = (f32[520,128]{1,0:T(8,128)S(1)}, f32[520,128]{1,0:T(8,128)S(1)}, u32[]{:S(2)}, u32[]{:S(2)}) collective-permute-start(f32[520,128]{1,0:T(8,128)S(1)} %get-tuple-element.41), channel_id=1, source_target_pairs={{0,3},{1,5},{3,6},{4,1},{5,8},{6,11},{7,2},{8,7},{9,13},{10,4},{11... | collective-permute-start | bytes 798728 | tf_op jit(solution)/shard_map/ppermute | solution.py:264
  5.5 0.2 collective-permute-start.1
  5.7 0.0 copy-done
  5.7 0.0 copy-done.1
  5.7 1.2 %cycle_blocks.3 = (f32[15,256,256]{2,1,0:T(8,128)S(1)}, f32[520,128]{1,0:T(8,128)S(1)}, f32[520,128]{1,0:T(8,128)S(1)}, f32[520,128]{1,0:T(8,128)S(1)}) custom-call(f32[1,15,256,256]{3,2,1,0:T(8,128)S(1)} %copy-done.1, f32[1,15,256,256]{3,2,1,0:T(8,128)S(1)} %copy-done, f32[8,256]{1,0:T(8,128)S(1)} %get-tuple-element.36.gap_ref, ...), custom_call_target="tpu_custom_call", output_to_operand_aliasing={{0}: (3, {})} | custom-call | flops 1 | bytes 1 | tf_op jit(solution)/shard_map/cycle_blocks/pallas_call | solution.py:251
  6.9 1.9 %collective-permute-start.2 = (f32[520,128]{1,0:T(8,128)S(1)}, f32[520,128]{1,0:T(8,128)S(1)}, u32[]{:S(2)}, u32[]{:S(2)}) collective-permute-start(f32[520,128]{1,0:T(8,128)S(1)} %get-tuple-element.43), channel_id=1, source_target_pairs={{0,2},{1,6},{2,5},{4,11},{5,0},{6,10},{7,3},{8,4},{9,8},{10,7},{11... | collective-permute-start | bytes 798728 | tf_op jit(solution)/shard_map/ppermute | solution.py:264
  8.8 0.9 %collective-permute-start.3 = (f32[520,128]{1,0:T(8,128)S(1)}, f32[520,128]{1,0:T(8,128)S(1)}, u32[]{:S(2)}, u32[]{:S(2)}) collective-permute-start(f32[520,128]{1,0:T(8,128)S(1)} %get-tuple-element.44), channel_id=1, source_target_pairs={{0,5},{1,0},{2,3},{4,8},{5,7},{6,13},{7,4},{8,2},{9,12},{10,9},{11... | collective-permute-start | bytes 798728 | tf_op jit(solution)/shard_map/ppermute | solution.py:264
  9.7 1.4 %collective-permute-start.4 = (f32[520,128]{1,0:T(8,128)S(1)}, f32[520,128]{1,0:T(8,128)S(1)}, u32[]{:S(2)}, u32[]{:S(2)}) collective-permute-start(f32[520,128]{1,0:T(8,128)S(1)} %get-tuple-element.46), channel_id=1, source_target_pairs={{0,2},{1,7},{2,3},{3,0},{4,1},{5,10},{6,8},{7,6},{8,9},{9,4},{10,5... | collective-permute-start | bytes 798728 | tf_op jit(solution)/shard_map/ppermute | solution.py:264
  11.1 1.2 %cycle_blocks.4 = (f32[15,256,256]{2,1,0:T(8,128)S(1)}, f32[520,128]{1,0:T(8,128)S(1)}, f32[520,128]{1,0:T(8,128)S(1)}, f32[520,128]{1,0:T(8,128)S(1)}) custom-call(f32[1,15,256,256]{3,2,1,0:T(8,128)S(1)} %copy-done.1, f32[1,15,256,256]{3,2,1,0:T(8,128)S(1)} %copy-done, f32[8,256]{1,0:T(8,128)S(1)} %get-tuple-element.36.gap_ref, ...), custom_call_target="tpu_custom_call", output_to_operand_aliasing={{0}: (3, {})} | custom-call | flops 1 | bytes 1 | tf_op jit(solution)/shard_map/cycle_blocks/pallas_call | solution.py:251
  12.3 0.0 collective-permute-done.refs_0_
  12.4 1.2 %collective-permute-start.5 = (f32[520,128]{1,0:T(8,128)S(1)}, f32[520,128]{1,0:T(8,128)S(1)}, u32[]{:S(2)}, u32[]{:S(2)}) collective-permute-start(f32[520,128]{1,0:T(8,128)S(1)} %get-tuple-element.48), channel_id=1, source_target_pairs={{0,2},{1,4},{2,6},{3,0},{4,5},{5,12},{6,3},{7,10},{8,1},{9,11},{10... | collective-permute-start | bytes 798728 | tf_op jit(solution)/shard_map/ppermute | solution.py:264
  13.6 1.0 %collective-permute-done.1.refs_1_ = f32[520,128]{1,0:T(8,128)S(1)} collective-permute-done((f32[520,128]{1,0:T(8,128)S(1)}, f32[520,128]{1,0:T(8,128)S(1)}, u32[]{:S(2)}, u32[]{:S(2)}) %collective-permute-start.1) | collective-permute-done | bytes 266272 | tf_op jit(solution)/shard_map/ppermute | solution.py:264
  14.6 2.6 %collective-permute-start.6 = (f32[520,128]{1,0:T(8,128)S(1)}, f32[520,128]{1,0:T(8,128)S(1)}, u32[]{:S(2)}, u32[]{:S(2)}) collective-permute-start(f32[520,128]{1,0:T(8,128)S(1)} %get-tuple-element.49), channel_id=1, source_target_pairs={{0,6},{1,3},{2,4},{3,2},{4,10},{5,1},{6,0},{7,14},{8,12},{9,5},{10... | collective-permute-start | bytes 798728 | tf_op jit(solution)/shard_map/ppermute | solution.py:264
  17.2 0.0 collective-permute-done.2.refs_2_
  17.2 9.1 %collective-permute-start.7 = (f32[520,128]{1,0:T(8,128)S(1)}, f32[520,128]{1,0:T(8,128)S(1)}, u32[]{:S(2)}, u32[]{:S(2)}) collective-permute-start(f32[520,128]{1,0:T(8,128)S(1)} %get-tuple-element.50), channel_id=1, source_target_pairs={{0,4},{1,0},{2,1},{3,2},{4,9},{5,3},{6,7},{7,13},{8,14},{9,6},{10,... | collective-permute-start | bytes 798728 | tf_op jit(solution)/shard_map/ppermute | solution.py:264
  26.3 0.0 collective-permute-done.3.refs_3_
  26.3 2.1 %cycle_blocks.5 = (f32[15,256,256]{2,1,0:T(8,128)S(1)}, f32[520,128]{1,0:T(8,128)S(1)}, f32[520,128]{1,0:T(8,128)S(1)}, f32[520,128]{1,0:T(8,128)S(1)}, f32[520,...) custom-call(f32[1,15,256,256]{3,2,1,0:T(8,128)S(1)} %copy-done.1, ...), custom_call_target="tpu_custom_call", output_to_operand_aliasing={{0}: (3, {})} | custom-call | flops 1 | bytes 1 | tf_op jit(solution)/shard_map/cycle_blocks/pallas_call | solution.py:251
  28.5 0.2 collective-permute-start.8
  28.7 0.0 collective-permute-done.4.refs_4_
  28.7 0.3 collective-permute-start.9
  29.1 2.5 %collective-permute-done.5.refs_0_ = f32[520,128]{1,0:T(8,128)S(1)} collective-permute-done((f32[520,128]{1,0:T(8,128)S(1)}, f32[520,128]{1,0:T(8,128)S(1)}, u32[]{:S(2)}, u32[]{:S(2)}) %collective-permute-start.5) | collective-permute-done | bytes 266272 | tf_op jit(solution)/shard_map/ppermute | solution.py:264
  31.5 1.0 %collective-permute-start.10 = (f32[520,128]{1,0:T(8,128)S(1)}, f32[520,128]{1,0:T(8,128)S(1)}, u32[]{:S(2)}, u32[]{:S(2)}) collective-permute-start(f32[520,128]{1,0:T(8,128)S(1)} %get-tuple-element.57), channel_id=1, source_target_pairs={{0,7},{1,0},{2,3},{3,1},{4,5},{5,11},{6,4},{7,12},{8,15},{9,2},{10... | collective-permute-start | bytes 798728 | tf_op jit(solution)/shard_map/ppermute | solution.py:264
  32.5 0.0 collective-permute-done.6.refs_1_
  32.5 2.5 %collective-permute-start.11 = (f32[520,128]{1,0:T(8,128)S(1)}, f32[520,128]{1,0:T(8,128)S(1)}, u32[]{:S(2)}, u32[]{:S(2)}) collective-permute-start(f32[520,128]{1,0:T(8,128)S(1)} %get-tuple-element.60), channel_id=1, source_target_pairs={{0,1},{2,0},{3,6},{4,2},{5,4},{6,5},{7,8},{8,11},{9,7},{10,3},{11,... | collective-permute-start | bytes 798728 | tf_op jit(solution)/shard_map/ppermute | solution.py:264
  35.1 0.0 collective-permute-done.7.refs_2_
  35.1 4.1 %collective-permute-start.12 = (f32[520,128]{1,0:T(8,128)S(1)}, f32[520,128]{1,0:T(8,128)S(1)}, u32[]{:S(2)}, u32[]{:S(2)}) collective-permute-start(f32[520,128]{1,0:T(8,128)S(1)} %get-tuple-element.63), channel_id=1, source_target_pairs={{1,2},{2,3},{3,5},{4,0},{5,4},{6,1},{7,11},{8,6},{9,15},{10,12},{1... | collective-permute-start | bytes 798728 | tf_op jit(solution)/shard_map/ppermute | solution.py:264
  39.2 0.0 collective-permute-done.8.refs_3_
  39.2 1.7 %collective-permute-start.13 = (f32[520,128]{1,0:T(8,128)S(1)}, f32[520,128]{1,0:T(8,128)S(1)}, u32[]{:S(2)}, u32[]{:S(2)}) collective-permute-start(f32[520,128]{1,0:T(8,128)S(1)} %get-tuple-element.66), channel_id=1, source_target_pairs={{1,0},{2,3},{3,4},{4,6},{5,2},{6,12},{7,1},{8,10},{9,13},{10,11},{... | collective-permute-start | bytes 798728 | tf_op jit(solution)/shard_map/ppermute | solution.py:264
  40.9 1.6 %update.1 = (f32[1,15,256,256]{3,2,1,0:T(8,128)}, f32[8,256]{1,0:T(8,128)S(1)}) custom-call(f32[1,15,256,256]{3,2,1,0:T(8,128)S(1)} %copy-done, f32[8,256]{1,0:T(8,128)S(1)} %get-tuple-element.36.gap_ref, s32[1,15]{1,0:T(1,128)S(1)} %get-tuple-element.37.present_ref, f32[15,256,256]{2,1,0:T(8,128)S(1)} %get-tuple-element.45.kept_ref, ...), custom_call_target="tpu_custom_call" | custom-call | flops 1 | bytes 1 | tf_op jit(solution)/shard_map/update/pallas_call | solution.py:279
  42.5 0.6 held_update.6
  43.1 0.0 collective-permute-done.9.refs_0_
  43.1 0.3 held_update.7
  43.4 0.0 collective-permute-done.10.refs_0_
  43.4 0.3 held_update.8
  43.7 2.8 %collective-permute-done.11.refs_0_ = f32[520,128]{1,0:T(8,128)S(1)} collective-permute-done((f32[520,128]{1,0:T(8,128)S(1)}, f32[520,128]{1,0:T(8,128)S(1)}, u32[]{:S(2)}, u32[]{:S(2)}) %collective-permute-start.11) | collective-permute-done | bytes 266272 | tf_op jit(solution)/shard_map/ppermute | solution.py:264
  46.5 0.3 held_update.9
  46.8 2.8 %collective-permute-done.12.refs_0_ = f32[520,128]{1,0:T(8,128)S(1)} collective-permute-done((f32[520,128]{1,0:T(8,128)S(1)}, f32[520,128]{1,0:T(8,128)S(1)}, u32[]{:S(2)}, u32[]{:S(2)}) %collective-permute-start.12) | collective-permute-done | bytes 266272 | tf_op jit(solution)/shard_map/ppermute | solution.py:264
  49.6 0.3 held_update.10
  49.9 0.0 collective-permute-done.13.refs_0_
  49.9 0.3 held_update.11
  50.2 0.6 broadcast_in_dim.3
  50.8 4.8 %all-to-all-start = ((f32[16,1,128]{2,1,0:T(1,128)}), f32[16,1,128]{2,1,0:T(1,128)S(1)}, u32[]{:S(2)}, u32[]{:S(2)}) async-start(f32[16,1,128]{2,1,0:T(1,128)} %broadcast_in_dim.3), calls=%async_computation | async-start | bytes 16384 | tf_op jit(solution)/shard_map/all_to_all | solution.py:317
  55.7 1.5 %store.1 = f32[1,15,256,256]{3,2,1,0:T(8,128)} custom-call(f32[1,15,256,256]{3,2,1,0:T(8,128)} %get-tuple-element.47._, f32[4,256,256]{2,1,0:T(8,128)S(1)} %get-tuple-element.53.refs_0_, f32[1,256,256]{2,1,0:T(8,128)S(1)} %get-tuple-element.56.refs_1_, f32[1,256,256]{2,1,0:T(8,128)S(1)} %get-tuple-element.59.refs_2_, ...), custom_call_target="tpu_custom_call", output_to_operand_aliasing={{}: (0, {})} | custom-call | flops 1 | bytes 1 | tf_op jit(solution)/shard_map/store/pallas_call | solution.py:304
  57.2 4.9 %all-to-all-done = f32[16,1,128]{2,1,0:T(1,128)S(1)} async-done(((f32[16,1,128]{2,1,0:T(1,128)}), f32[16,1,128]{2,1,0:T(1,128)S(1)}, u32[]{:S(2)}, u32[]{:S(2)}) %all-to-all-start) | async-done | bytes 8224 | tf_op jit(solution)/shard_map/all_to_all | solution.py:317
  62.1 0.6 reduce_sum.29
  (2 shorter events, 0.0 us)
Async XLA Ops:
  0.6 5.1 %copy-start = (f32[1,15,256,256]{3,2,1,0:T(8,128)S(1)}, f32[1,15,256,256]{3,2,1,0:T(8,128)}, u32[]{:S(2)}) copy-start(f32[1,15,256,256]{3,2,1,0:T(8,128)} %int_ref.19) | copy-start | bytes 11796484
  0.6 5.1 %copy-start.1 = (f32[1,15,256,256]{3,2,1,0:T(8,128)S(1)}, f32[1,15,256,256]{3,2,1,0:T(8,128)}, u32[]{:S(2)}) copy-start(f32[1,15,256,256]{3,2,1,0:T(8,128)} %amp_ref.5) | copy-start | bytes 11796484
  3.0 9.3 %collective-permute-start = (f32[520,128]{1,0:T(8,128)S(1)}, f32[520,128]{1,0:T(8,128)S(1)}, u32[]{:S(2)}, u32[]{:S(2)}) collective-permute-start(f32[520,128]{1,0:T(8,128)S(1)} %get-tuple-element.41), channel_id=1, source_target_pairs={{0,3},{1,5},{3,6},{4,1},{5,8},{6,11},{7,2},{8,7},{9,13},{10,4},{11... | collective-permute-start | bytes 798728 | tf_op jit(solution)/shard_map/ppermute | solution.py:264
  5.5 9.1 %collective-permute-start.1 = (f32[520,128]{1,0:T(8,128)S(1)}, f32[520,128]{1,0:T(8,128)S(1)}, u32[]{:S(2)}, u32[]{:S(2)}) collective-permute-start(f32[520,128]{1,0:T(8,128)S(1)} %get-tuple-element.42), channel_id=1, source_target_pairs={{0,1},{1,8},{3,7},{4,3},{5,6},{6,2},{7,9},{8,5},{9,10},{10,14},{11... | collective-permute-start | bytes 798728 | tf_op jit(solution)/shard_map/ppermute | solution.py:264
  6.9 10.3 %collective-permute-start.2 = (f32[520,128]{1,0:T(8,128)S(1)}, f32[520,128]{1,0:T(8,128)S(1)}, u32[]{:S(2)}, u32[]{:S(2)}) collective-permute-start(f32[520,128]{1,0:T(8,128)S(1)} %get-tuple-element.43), channel_id=1, source_target_pairs={{0,2},{1,6},{2,5},{4,11},{5,0},{6,10},{7,3},{8,4},{9,8},{10,7},{11... | collective-permute-start | bytes 798728 | tf_op jit(solution)/shard_map/ppermute | solution.py:264
  8.8 17.5 %collective-permute-start.3 = (f32[520,128]{1,0:T(8,128)S(1)}, f32[520,128]{1,0:T(8,128)S(1)}, u32[]{:S(2)}, u32[]{:S(2)}) collective-permute-start(f32[520,128]{1,0:T(8,128)S(1)} %get-tuple-element.44), channel_id=1, source_target_pairs={{0,5},{1,0},{2,3},{4,8},{5,7},{6,13},{7,4},{8,2},{9,12},{10,9},{11... | collective-permute-start | bytes 798728 | tf_op jit(solution)/shard_map/ppermute | solution.py:264
  9.7 19.0 %collective-permute-start.4 = (f32[520,128]{1,0:T(8,128)S(1)}, f32[520,128]{1,0:T(8,128)S(1)}, u32[]{:S(2)}, u32[]{:S(2)}) collective-permute-start(f32[520,128]{1,0:T(8,128)S(1)} %get-tuple-element.46), channel_id=1, source_target_pairs={{0,2},{1,7},{2,3},{3,0},{4,1},{5,10},{6,8},{7,6},{8,9},{9,4},{10,5... | collective-permute-start | bytes 798728 | tf_op jit(solution)/shard_map/ppermute | solution.py:264
  12.4 19.2 %collective-permute-start.5 = (f32[520,128]{1,0:T(8,128)S(1)}, f32[520,128]{1,0:T(8,128)S(1)}, u32[]{:S(2)}, u32[]{:S(2)}) collective-permute-start(f32[520,128]{1,0:T(8,128)S(1)} %get-tuple-element.48), channel_id=1, source_target_pairs={{0,2},{1,4},{2,6},{3,0},{4,5},{5,12},{6,3},{7,10},{8,1},{9,11},{10... | collective-permute-start | bytes 798728 | tf_op jit(solution)/shard_map/ppermute | solution.py:264
  14.6 17.9 %collective-permute-start.6 = (f32[520,128]{1,0:T(8,128)S(1)}, f32[520,128]{1,0:T(8,128)S(1)}, u32[]{:S(2)}, u32[]{:S(2)}) collective-permute-start(f32[520,128]{1,0:T(8,128)S(1)} %get-tuple-element.49), channel_id=1, source_target_pairs={{0,6},{1,3},{2,4},{3,2},{4,10},{5,1},{6,0},{7,14},{8,12},{9,5},{10... | collective-permute-start | bytes 798728 | tf_op jit(solution)/shard_map/ppermute | solution.py:264
  17.2 17.8 %collective-permute-start.7 = (f32[520,128]{1,0:T(8,128)S(1)}, f32[520,128]{1,0:T(8,128)S(1)}, u32[]{:S(2)}, u32[]{:S(2)}) collective-permute-start(f32[520,128]{1,0:T(8,128)S(1)} %get-tuple-element.50), channel_id=1, source_target_pairs={{0,4},{1,0},{2,1},{3,2},{4,9},{5,3},{6,7},{7,13},{8,14},{9,6},{10,... | collective-permute-start | bytes 798728 | tf_op jit(solution)/shard_map/ppermute | solution.py:264
  28.5 10.7 %collective-permute-start.8 = (f32[520,128]{1,0:T(8,128)S(1)}, f32[520,128]{1,0:T(8,128)S(1)}, u32[]{:S(2)}, u32[]{:S(2)}) collective-permute-start(f32[520,128]{1,0:T(8,128)S(1)} %get-tuple-element.51), channel_id=1, source_target_pairs={{0,4},{1,0},{2,1},{3,10},{4,7},{5,9},{6,2},{7,5},{8,13},{9,3},{10,... | collective-permute-start | bytes 798728 | tf_op jit(solution)/shard_map/ppermute | solution.py:264
  28.7 14.4 %collective-permute-start.9 = (f32[520,128]{1,0:T(8,128)S(1)}, f32[520,128]{1,0:T(8,128)S(1)}, u32[]{:S(2)}, u32[]{:S(2)}) collective-permute-start(f32[520,128]{1,0:T(8,128)S(1)} %get-tuple-element.54), channel_id=1, source_target_pairs={{0,1},{2,7},{3,2},{4,5},{5,4},{6,9},{7,0},{8,3},{9,14},{10,15},{11... | collective-permute-start | bytes 798728 | tf_op jit(solution)/shard_map/ppermute | solution.py:264
  31.5 11.9 %collective-permute-start.10 = (f32[520,128]{1,0:T(8,128)S(1)}, f32[520,128]{1,0:T(8,128)S(1)}, u32[]{:S(2)}, u32[]{:S(2)}) collective-permute-start(f32[520,128]{1,0:T(8,128)S(1)} %get-tuple-element.57), channel_id=1, source_target_pairs={{0,7},{1,0},{2,3},{3,1},{4,5},{5,11},{6,4},{7,12},{8,15},{9,2},{10... | collective-permute-start | bytes 798728 | tf_op jit(solution)/shard_map/ppermute | solution.py:264
  32.5 14.0 %collective-permute-start.11 = (f32[520,128]{1,0:T(8,128)S(1)}, f32[520,128]{1,0:T(8,128)S(1)}, u32[]{:S(2)}, u32[]{:S(2)}) collective-permute-start(f32[520,128]{1,0:T(8,128)S(1)} %get-tuple-element.60), channel_id=1, source_target_pairs={{0,1},{2,0},{3,6},{4,2},{5,4},{6,5},{7,8},{8,11},{9,7},{10,3},{11,... | collective-permute-start | bytes 798728 | tf_op jit(solution)/shard_map/ppermute | solution.py:264
  35.1 14.5 %collective-permute-start.12 = (f32[520,128]{1,0:T(8,128)S(1)}, f32[520,128]{1,0:T(8,128)S(1)}, u32[]{:S(2)}, u32[]{:S(2)}) collective-permute-start(f32[520,128]{1,0:T(8,128)S(1)} %get-tuple-element.63), channel_id=1, source_target_pairs={{1,2},{2,3},{3,5},{4,0},{5,4},{6,1},{7,11},{8,6},{9,15},{10,12},{1... | collective-permute-start | bytes 798728 | tf_op jit(solution)/shard_map/ppermute | solution.py:264
  39.2 10.7 %collective-permute-start.13 = (f32[520,128]{1,0:T(8,128)S(1)}, f32[520,128]{1,0:T(8,128)S(1)}, u32[]{:S(2)}, u32[]{:S(2)}) collective-permute-start(f32[520,128]{1,0:T(8,128)S(1)} %get-tuple-element.66), channel_id=1, source_target_pairs={{1,0},{2,3},{3,4},{4,6},{5,2},{6,12},{7,1},{8,10},{9,13},{10,11},{... | collective-permute-start | bytes 798728 | tf_op jit(solution)/shard_map/ppermute | solution.py:264
  50.8 11.2 %all-to-all-start = ((f32[16,1,128]{2,1,0:T(1,128)}), f32[16,1,128]{2,1,0:T(1,128)S(1)}, u32[]{:S(2)}, u32[]{:S(2)}) async-start(f32[16,1,128]{2,1,0:T(1,128)} %broadcast_in_dim.3), calls=%async_computation | async-start | bytes 16384 | tf_op jit(solution)/shard_map/all_to_all | solution.py:317

commit v5 on v4

--- a/solution.py
+++ b/solution.py
@@ -12,30 +12,30 @@
 HALF = 128
 
 SENDS = (
-    (3, 5, -1, 6, 1, 8, 11, 2, 7, 13, 4, 14, 10, -1, 9, 12),
-    (17, 8, -1, 7, 3, 6, 18, 9, 5, 10, 14, 4, 29, -1, 27, 28),
-    (18, 6, 5, -1, 11, 0, 10, 3, 4, 8, 7, 31, -1, 28, 13, 9),
-    (5, 0, 3, -1, 8, 7, 13, 4, 2, 12, 9, 6, -1, 10, 15, 11),
-    (2, 7, 19, 0, 17, 10, 8, 6, 9, 4, 5, 15, 14, 28, 11, 13),
-    (18, 4, 6, 16, 21, 12, 3, 10, 1, 11, 13, 8, 31, 9, 7, 30),
-    (6, 3, 4, 18, 10, 1, 0, 14, 12, 5, 27, 7, 9, 31, 29, 8),
-    (4, 16, 17, 18, 9, 3, 7, 13, 14, 6, 27, 5, 8, 28, 31, 10),
-    (20, 16, 1, 10, 7, 9, 2, 5, 13, 3, 6, 12, 11, 15, 8, 30),
-    (1, -1, 7, 2, 5, 4, 9, 0, 3, 14, 15, 26, 29, 11, 12, -1),
-    (7, 16, 19, 1, 21, 11, 4, 12, 15, 2, 8, 10, 13, 25, -1, 14),
-    (17, -1, 0, 22, 2, 20, 5, 8, 11, 7, 3, 13, 15, 12, 10, 30),
-    (-1, 2, 19, 5, 0, 20, 1, 11, 6, 15, 12, 26, 29, 8, -1, 30),
-    (-1, 16, 19, 4, 6, 2, 12, 1, 10, 29, 11, 9, 5, 14, 31, -1),
+    (7, 16, 6, 18, 21, 10, 9, 1, 3, 8, 4, 30, 31, 28, 13, 11),
+    (6, 0, 19, -1, 21, 8, 11, 4, 12, 2, 13, 26, 9, -1, 7, 14),
+    (4, 16, 7, -1, 8, 3, 13, 2, 6, 10, 11, 5, -1, 28, 31, 9),
+    (2, 8, -1, 4, 6, 1, 3, 11, 10, 29, 14, 7, 5, -1, 9, 12),
+    (17, 5, -1, 6, 7, 12, 4, 9, 2, 11, 3, 13, -1, 8, 31, 10),
+    (19, 7, 22, 1, 16, 9, 18, 10, 5, 14, 15, 4, 8, 12, 27, 29),
+    (5, 19, 1, 18, 10, 0, 7, 8, 9, 4, 6, 14, 15, 28, 11, 13),
+    (17, 4, 19, 7, 9, 2, 8, 0, 11, 5, 12, 6, 29, 15, 10, 30),
+    (-1, 3, 17, 2, 0, 4, 12, 5, 13, 7, 9, 10, 14, 11, 31, -1),
+    (1, 6, 16, 5, 2, 11, 10, 3, 4, 15, 7, 12, 29, 9, 8, 30),
+    (-1, 16, 4, 18, 5, 6, 1, 12, 14, 3, 27, 8, 13, 10, 15, -1),
+    (3, -1, 5, 0, 1, 20, 2, 13, 7, 12, 8, 26, 11, 31, -1, 30),
+    (17, -1, 0, 18, 3, 20, 5, 14, 15, 6, 27, 9, 10, 28, -1, 29),
+    (20, 2, 3, 10, 11, 7, 0, 6, 1, 13, 5, 15, 25, 14, 12, 8),
 )
 RELAYS = (
-    (2, 0, 9, 0, 12),
-    (13, 15, 6, 0, 9),
-    (2, 0, 8, 1, 13),
-    (13, 15, 7, 1, 13),
-    (3, 1, 8, 2, 9),
+    (3, 1, 8, 1, 12),
+    (13, 15, 6, 1, 8),
+    (3, 1, 9, 2, 11),
     (12, 14, 7, 2, 12),
-    (3, 1, 9, 3, 11),
-    (12, 14, 6, 3, 10),
+    (2, 0, 9, 3, 10),
+    (13, 15, 7, 3, 10),
+    (2, 0, 8, 4, 8),
+    (12, 14, 6, 4, 11),
 )
 
 
@@ -137,12 +137,16 @@
         put_cycle(amp_buf[number], int_buf[number], gap_buf[...], kept_ref.at[index], outs[number])
 
 
-def cycle_kernel(order, relays, arrays, amp_ref, int_ref, gap_ref, _, *refs):
-    arrived, kept_ref, outs = refs[:arrays], refs[arrays], refs[arrays + 1 :]
+def cycle_kernel(order, amp_ref, int_ref, gap_ref, _, kept_ref, *outs):
     here = lax.axis_index("row")
     for slot, out_ref in zip(order, [*outs, None]):
         index = lookup(slot, here)
         put_cycle(amp_ref[0, index], int_ref[0, index], gap_ref[:1, :], kept_ref.at[index], out_ref)
+
+
+def relay_kernel(relays, arrays, *refs):
+    arrived, outs = refs[:arrays], refs[arrays + (len(refs) - arrays) // 2 :]
+    here = lax.axis_index("row")
     for row, output, array in relays:
 
         @pl.when(here == row)
@@ -244,30 +248,43 @@
         name="first_blocks",
     )(*hbm(amplitude, integral, pair_gap, present))
 
-    def cycles(start, stop, kept, arrived):
-        passed = [(by, second - start, first) for _, by, _, first, second in relays if start <= second < stop]
-        arrived = arrived if passed else []
+    def cycles(start, stop, kept):
         some = order[start:stop] + ([order[-1]] if stop == len(rounds) else [])
         kept, *sent = pl.pallas_call(
-            functools.partial(cycle_kernel, some, passed, len(arrived)),
-            in_specs=[IN_VMEM] * (4 + len(arrived)),
+            functools.partial(cycle_kernel, some),
+            in_specs=[IN_VMEM] * 4,
             out_specs=[IN_VMEM] * (1 + stop - start),
             out_shape=[cube] + [block] * (stop - start),
             input_output_aliases={3: 0},
             compiler_params=PARAMS,
             cost_estimate=SMALL,
             name="cycle_blocks",
-        )(*vmem(amplitude, integral, gap, kept, *arrived))
+        )(*vmem(amplitude, integral, gap, kept))
         return kept, sent
+
+    def relayed(arrived, start, sent):
+        passed = [(by, second - start, first) for _, by, _, first, second in relays]
+        if not passed:
+            return sent
+        arrived = arrived[: 1 + max(first for _, _, first in passed)]
+        return pl.pallas_call(
+            functools.partial(relay_kernel, passed, len(arrived)),
+            in_specs=[IN_VMEM] * (len(arrived) + len(sent)),
+            out_specs=[IN_VMEM] * len(sent),
+            out_shape=[block] * len(sent),
+            input_output_aliases={len(arrived) + number: number for number in range(len(sent))},
+            compiler_params=PARAMS,
+            cost_estimate=SMALL,
+            name="relayed_blocks",
+        )(*vmem(*arrived, *sent))
 
     def send(start, stop):
         return [lax.ppermute(sent[number], "row", rounds[number][0]) for number in range(start, stop)]
 
     arrived = send(0, first)
-    passing = 1 + max([hop for _, _, _, hop, _ in relays], default=-1)
     for start, stop in zip(CYCLES[1:-1], CYCLES[2:]):
-        kept, more = cycles(start, stop, kept, arrived[:passing])
-        sent += more
+        kept, more = cycles(start, stop, kept)
+        sent += relayed(arrived, start, more) if stop == len(rounds) else more
         arrived += send(start, stop)
 
     def updates(start, stop, held, before):

time: 64.6 us -> 63.7 us (0.986)
  starting transfers between devices: 34.6 us -> 22.2 us
  waiting for transfers between devices: 14 us -> 25.4 us
    ppermute x14, starting transfers between devices: 29.8 us -> 16.1 us  [send(): lax.ppermute(sent[number], 'row', rounds[number][0])]
    ppermute x14, waiting for transfers between devices: 9.08 us -> 20.5 us  [send(): lax.ppermute(sent[number], 'row', rounds[number][0])]
    all_to_all x1, starting transfers between devices: 4.83 us -> 6.08 us  [per_device(): every = lax.all_to_all(jnp.broadcast_to(summed, (count, 128)), 'row', 0, 0)]
    pallas_call x3 -> x4, Pallas kernels: 4.56 us -> 4.57 us  [the longest x3 4.53 us: cycles(): pl.pallas_call(functools.partial(cycle_kernel, some), in_specs=[IN_VMEM]...]
  transfers between devices with their start and end apart: 15 -> 15, of which waited for: 5 -> 9; matrix products, arithmetic and copies ran while one was open for 0% -> 0% of each run, Pallas kernels for 15% -> 15%
where the time goes in v5:
time: 63.7 us; the launch traced here: 63.5 us
  waiting for transfers between devices  25.4 us (40%)
  starting transfers between devices  22.2 us (35%)
  Pallas kernels  12 us (19%)
  between operations  2.59 us (4%)
  other arithmetic  0.64 us (1%)
    ppermute x14, waiting for transfers between devices, send(): lax.ppermute(sent[number], 'row', rounds[number][0])  20.5 us
    ppermute x14, starting transfers between devices, send(): lax.ppermute(sent[number], 'row', rounds[number][0])  16.1 us
    all_to_all x1, starting transfers between devices, per_device(): every = lax.all_to_all(jnp.broadcast_to(summed, (count, 128)), 'row', 0, 0)  6.08 us
    all_to_all x1, waiting for transfers between devices, per_device(): every = lax.all_to_all(jnp.broadcast_to(summed, (count, 128)), 'row', 0, 0)  4.9 us
    pallas_call x3, Pallas kernels, cycles(): pl.pallas_call(functools.partial(cycle_kernel, some), in_specs=[IN_VMEM]...  4.53 us
    pallas_call x7, Pallas kernels, updates(): pl.pallas_call(functools.partial(update_kernel, some, first, held), in_sp...  3.59 us
    pallas_call x1, Pallas kernels, per_device(): pl.pallas_call(functools.partial(first_kernel, order[:first]), in_specs=[...  2.39 us
    pallas_call x1, Pallas kernels, per_device(): pl.pallas_call(functools.partial(store_kernel, some), in_specs=[IN_HBM] +...  1.49 us
  transfers between devices with their start and end apart: 15, of which 9 were waited for; matrix products, arithmetic and copies ran while one was open for 0% of the time, Pallas kernels for 15%

profile of v5, /device:TPU:0, one launch (start us, length us, event | category | flops | bytes accessed | tf_op | source)
XLA Modules:
  0.0 63.5 jit_solution(17591571292410310757)
XLA Ops:
  0.6 0.0 copy-start
  0.6 0.0 copy-start.1
  0.7 2.4 %first_blocks.1 = (f32[8,256]{1,0:T(8,128)S(1)}, s32[1,15]{1,0:T(1,128)S(1)}, f32[15,256,256]{2,1,0:T(8,128)S(1)}, f32[520,128]{1,0:T(8,128)S(1)}, f32[520,128]{1,0:T(8,128)S(1)}) custom-call(f32[1,15,256,256]{3,2,1,0:T(8,128)} %amp_ref.5, f32[1,15,256,256]{3,2,1,0:T(8,128)} %int_ref.19, f32[1,256]{1,0:T(1,128)} %gap_hbm.1, s32[1,15]{1,0:T(1,128)} %present_hbm.1), custom_call_target="tpu_custom_call" | custom-call | flops 1 | bytes 1 | tf_op jit(solution)/shard_map/first_blocks/pallas_call | solution.py:233
  3.0 3.5 %collective-permute-start = (f32[520,128]{1,0:T(8,128)S(1)}, f32[520,128]{1,0:T(8,128)S(1)}, u32[]{:S(2)}, u32[]{:S(2)}) collective-permute-start(f32[520,128]{1,0:T(8,128)S(1)} %get-tuple-element.48), channel_id=1, source_target_pairs={{0,7},{1,0},{2,6},{3,2},{4,5},{5,10},{6,9},{7,1},{8,3},{9,8},{10,4... | collective-permute-start | bytes 798728 | tf_op jit(solution)/shard_map/ppermute | solution.py:282
  6.5 1.5 %collective-permute-start.1 = (f32[520,128]{1,0:T(8,128)S(1)}, f32[520,128]{1,0:T(8,128)S(1)}, u32[]{:S(2)}, u32[]{:S(2)}) collective-permute-start(f32[520,128]{1,0:T(8,128)S(1)} %get-tuple-element.49), channel_id=1, source_target_pairs={{0,6},{1,0},{2,3},{4,5},{5,8},{6,11},{7,4},{8,12},{9,2},{10,13},{1... | collective-permute-start | bytes 798728 | tf_op jit(solution)/shard_map/ppermute | solution.py:282
  8.0 0.0 copy-done
  8.0 0.0 copy-done.1
  8.1 1.2 %cycle_blocks.3 = (f32[15,256,256]{2,1,0:T(8,128)S(1)}, f32[520,128]{1,0:T(8,128)S(1)}, f32[520,128]{1,0:T(8,128)S(1)}, f32[520,128]{1,0:T(8,128)S(1)}) custom-call(f32[1,15,256,256]{3,2,1,0:T(8,128)S(1)} %copy-done.1, f32[1,15,256,256]{3,2,1,0:T(8,128)S(1)} %copy-done, f32[8,256]{1,0:T(8,128)S(1)} %get-tuple-element.42.gap_ref, ...), custom_call_target="tpu_custom_call", output_to_operand_aliasing={{0}: (3, {})} | custom-call | flops 1 | bytes 1 | tf_op jit(solution)/shard_map/cycle_blocks/pallas_call | solution.py:253
  9.3 0.8 %collective-permute-start.2 = (f32[520,128]{1,0:T(8,128)S(1)}, f32[520,128]{1,0:T(8,128)S(1)}, u32[]{:S(2)}, u32[]{:S(2)}) collective-permute-start(f32[520,128]{1,0:T(8,128)S(1)} %get-tuple-element.50), channel_id=1, source_target_pairs={{0,4},{1,0},{2,7},{4,8},{5,3},{6,13},{7,2},{8,6},{9,10},{10,11},{1... | collective-permute-start | bytes 798728 | tf_op jit(solution)/shard_map/ppermute | solution.py:282
  10.1 0.0 collective-permute-start.3
  10.1 2.8 %collective-permute-start.4 = (f32[520,128]{1,0:T(8,128)S(1)}, f32[520,128]{1,0:T(8,128)S(1)}, u32[]{:S(2)}, u32[]{:S(2)}) collective-permute-start(f32[520,128]{1,0:T(8,128)S(1)} %get-tuple-element.52), channel_id=1, source_target_pairs={{0,1},{1,5},{3,6},{4,7},{5,12},{6,4},{7,9},{8,2},{9,11},{10,3},{11... | collective-permute-start | bytes 798728 | tf_op jit(solution)/shard_map/ppermute | solution.py:282
  12.8 1.2 %cycle_blocks.4 = (f32[15,256,256]{2,1,0:T(8,128)S(1)}, f32[520,128]{1,0:T(8,128)S(1)}, f32[520,128]{1,0:T(8,128)S(1)}, f32[520,128]{1,0:T(8,128)S(1)}) custom-call(f32[1,15,256,256]{3,2,1,0:T(8,128)S(1)} %copy-done.1, f32[1,15,256,256]{3,2,1,0:T(8,128)S(1)} %copy-done, f32[8,256]{1,0:T(8,128)S(1)} %get-tuple-element.42.gap_ref, ...), custom_call_target="tpu_custom_call", output_to_operand_aliasing={{0}: (3, {})} | custom-call | flops 1 | bytes 1 | tf_op jit(solution)/shard_map/cycle_blocks/pallas_call | solution.py:253
  14.0 2.1 %cycle_blocks.5 = (f32[15,256,256]{2,1,0:T(8,128)S(1)}, f32[520,128]{1,0:T(8,128)S(1)}, f32[520,128]{1,0:T(8,128)S(1)}, f32[520,128]{1,0:T(8,128)S(1)}, f32[520,...) custom-call(f32[1,15,256,256]{3,2,1,0:T(8,128)S(1)} %copy-done.1, ...), custom_call_target="tpu_custom_call", output_to_operand_aliasing={{0}: (3, {})} | custom-call | flops 1 | bytes 1 | tf_op jit(solution)/shard_map/cycle_blocks/pallas_call | solution.py:253
  16.2 0.0 collective-permute-done.refs_0_
  16.2 0.1 collective-permute-start.5
  16.2 0.0 collective-permute-done.1.refs_1_
  16.3 2.4 %collective-permute-start.6 = (f32[520,128]{1,0:T(8,128)S(1)}, f32[520,128]{1,0:T(8,128)S(1)}, u32[]{:S(2)}, u32[]{:S(2)}) collective-permute-start(f32[520,128]{1,0:T(8,128)S(1)} %get-tuple-element.55), channel_id=1, source_target_pairs={{0,5},{1,3},{2,1},{3,2},{4,10},{5,0},{6,7},{7,8},{8,9},{9,4},{10,6... | collective-permute-start | bytes 798728 | tf_op jit(solution)/shard_map/ppermute | solution.py:282
  18.6 0.4 collective-permute-done.2.refs_2_
  19.1 0.0 collective-permute-start.7
  19.1 3.1 %collective-permute-done.3.refs_3_ = f32[520,128]{1,0:T(8,128)S(1)} collective-permute-done((f32[520,128]{1,0:T(8,128)S(1)}, f32[520,128]{1,0:T(8,128)S(1)}, u32[]{:S(2)}, u32[]{:S(2)}) %collective-permute-start.3) | collective-permute-done | bytes 266272 | tf_op jit(solution)/shard_map/ppermute | solution.py:282
  22.2 5.2 %collective-permute-done.4.refs_4_ = f32[520,128]{1,0:T(8,128)S(1)} collective-permute-done((f32[520,128]{1,0:T(8,128)S(1)}, f32[520,128]{1,0:T(8,128)S(1)}, u32[]{:S(2)}, u32[]{:S(2)}) %collective-permute-start.4) | collective-permute-done | bytes 266272 | tf_op jit(solution)/shard_map/ppermute | solution.py:282
  27.4 0.1 collective-permute-start.8
  27.5 0.1 collective-permute-start.9
  27.6 4.9 %collective-permute-done.5.refs_0_ = f32[520,128]{1,0:T(8,128)S(1)} collective-permute-done((f32[520,128]{1,0:T(8,128)S(1)}, f32[520,128]{1,0:T(8,128)S(1)}, u32[]{:S(2)}, u32[]{:S(2)}) %collective-permute-start.5) | collective-permute-done | bytes 266272 | tf_op jit(solution)/shard_map/ppermute | solution.py:282
  32.5 1.7 %collective-permute-start.10 = (f32[520,128]{1,0:T(8,128)S(1)}, f32[520,128]{1,0:T(8,128)S(1)}, u32[]{:S(2)}, u32[]{:S(2)}) collective-permute-start(f32[520,128]{1,0:T(8,128)S(1)} %get-tuple-element.69), channel_id=1, source_target_pairs={{1,0},{2,4},{3,2},{4,5},{5,6},{6,1},{7,12},{8,14},{9,3},{10,11},{1... | collective-permute-start | bytes 798728 | tf_op jit(solution)/shard_map/ppermute | solution.py:282
  34.2 0.0 collective-permute-done.6.refs_1_
  34.2 0.5 collective-permute-start.11
  34.7 0.0 collective-permute-done.7.refs_2_
  34.7 2.2 %collective-permute-start.12 = (f32[520,128]{1,0:T(8,128)S(1)}, f32[520,128]{1,0:T(8,128)S(1)}, u32[]{:S(2)}, u32[]{:S(2)}) collective-permute-start(f32[520,128]{1,0:T(8,128)S(1)} %get-tuple-element.75), channel_id=1, source_target_pairs={{0,1},{2,0},{3,2},{4,3},{5,4},{6,5},{7,14},{8,15},{9,6},{10,11},{1... | collective-permute-start | bytes 798728 | tf_op jit(solution)/shard_map/ppermute | solution.py:282
  36.9 0.0 collective-permute-done.8.refs_3_
  36.9 0.5 collective-permute-start.13
  37.4 1.6 %update.1 = (f32[1,15,256,256]{3,2,1,0:T(8,128)}, f32[8,256]{1,0:T(8,128)S(1)}) custom-call(f32[1,15,256,256]{3,2,1,0:T(8,128)S(1)} %copy-done, f32[8,256]{1,0:T(8,128)S(1)} %get-tuple-element.42.gap_ref, s32[1,15]{1,0:T(1,128)S(1)} %get-tuple-element.43.present_ref, f32[15,256,256]{2,1,0:T(8,128)S(1)} %get-tuple-element.47.kept_ref, ...), custom_call_target="tpu_custom_call" | custom-call | flops 1 | bytes 1 | tf_op jit(solution)/shard_map/update/pallas_call | solution.py:296
  39.0 0.6 held_update.6
  39.7 0.7 %collective-permute-done.9.refs_0_ = f32[520,128]{1,0:T(8,128)S(1)} collective-permute-done((f32[520,128]{1,0:T(8,128)S(1)}, f32[520,128]{1,0:T(8,128)S(1)}, u32[]{:S(2)}, u32[]{:S(2)}) %collective-permute-start.9) | collective-permute-done | bytes 266272 | tf_op jit(solution)/shard_map/ppermute | solution.py:282
  40.4 0.3 held_update.7
  40.6 0.1 collective-permute-done.10.refs_0_
  40.8 0.3 held_update.8
  41.0 5.6 %collective-permute-done.11.refs_0_ = f32[520,128]{1,0:T(8,128)S(1)} collective-permute-done((f32[520,128]{1,0:T(8,128)S(1)}, f32[520,128]{1,0:T(8,128)S(1)}, u32[]{:S(2)}, u32[]{:S(2)}) %collective-permute-start.11) | collective-permute-done | bytes 266272 | tf_op jit(solution)/shard_map/ppermute | solution.py:282
  46.6 0.3 held_update.9
  46.9 0.5 collective-permute-done.12.refs_0_
  47.4 0.3 held_update.10
  47.7 0.0 collective-permute-done.13.refs_0_
  47.7 0.3 held_update.11
  48.0 0.6 broadcast_in_dim.3
  48.6 6.1 %all-to-all-start = ((f32[16,1,128]{2,1,0:T(1,128)}), f32[16,1,128]{2,1,0:T(1,128)S(1)}, u32[]{:S(2)}, u32[]{:S(2)}) async-start(f32[16,1,128]{2,1,0:T(1,128)} %broadcast_in_dim.3), calls=%async_computation | async-start | bytes 16384 | tf_op jit(solution)/shard_map/all_to_all | solution.py:334
  54.7 1.5 %store.1 = f32[1,15,256,256]{3,2,1,0:T(8,128)} custom-call(f32[1,15,256,256]{3,2,1,0:T(8,128)} %get-tuple-element.53._, f32[4,256,256]{2,1,0:T(8,128)S(1)} %get-tuple-element.65.refs_0_, f32[1,256,256]{2,1,0:T(8,128)S(1)} %get-tuple-element.68.refs_1_, f32[1,256,256]{2,1,0:T(8,128)S(1)} %get-tuple-element.71.refs_2_, ...), custom_call_target="tpu_custom_call", output_to_operand_aliasing={{}: (0, {})} | custom-call | flops 1 | bytes 1 | tf_op jit(solution)/shard_map/store/pallas_call | solution.py:321
  56.2 4.9 %all-to-all-done = f32[16,1,128]{2,1,0:T(1,128)S(1)} async-done(((f32[16,1,128]{2,1,0:T(1,128)}), f32[16,1,128]{2,1,0:T(1,128)S(1)}, u32[]{:S(2)}, u32[]{:S(2)}) %all-to-all-start) | async-done | bytes 8224 | tf_op jit(solution)/shard_map/all_to_all | solution.py:334
  61.1 0.6 reduce_sum.29
  (3 shorter events, 0.1 us)
Async XLA Ops:
  0.6 7.4 %copy-start = (f32[1,15,256,256]{3,2,1,0:T(8,128)S(1)}, f32[1,15,256,256]{3,2,1,0:T(8,128)}, u32[]{:S(2)}) copy-start(f32[1,15,256,256]{3,2,1,0:T(8,128)} %int_ref.19) | copy-start | bytes 11796484
  0.6 7.4 %copy-start.1 = (f32[1,15,256,256]{3,2,1,0:T(8,128)S(1)}, f32[1,15,256,256]{3,2,1,0:T(8,128)}, u32[]{:S(2)}) copy-start(f32[1,15,256,256]{3,2,1,0:T(8,128)} %amp_ref.5) | copy-start | bytes 11796484
  3.0 13.1 %collective-permute-start = (f32[520,128]{1,0:T(8,128)S(1)}, f32[520,128]{1,0:T(8,128)S(1)}, u32[]{:S(2)}, u32[]{:S(2)}) collective-permute-start(f32[520,128]{1,0:T(8,128)S(1)} %get-tuple-element.48), channel_id=1, source_target_pairs={{0,7},{1,0},{2,6},{3,2},{4,5},{5,10},{6,9},{7,1},{8,3},{9,8},{10,4... | collective-permute-start | bytes 798728 | tf_op jit(solution)/shard_map/ppermute | solution.py:282
  6.5 9.7 %collective-permute-start.1 = (f32[520,128]{1,0:T(8,128)S(1)}, f32[520,128]{1,0:T(8,128)S(1)}, u32[]{:S(2)}, u32[]{:S(2)}) collective-permute-start(f32[520,128]{1,0:T(8,128)S(1)} %get-tuple-element.49), channel_id=1, source_target_pairs={{0,6},{1,0},{2,3},{4,5},{5,8},{6,11},{7,4},{8,12},{9,2},{10,13},{1... | collective-permute-start | bytes 798728 | tf_op jit(solution)/shard_map/ppermute | solution.py:282
  9.3 9.8 %collective-permute-start.2 = (f32[520,128]{1,0:T(8,128)S(1)}, f32[520,128]{1,0:T(8,128)S(1)}, u32[]{:S(2)}, u32[]{:S(2)}) collective-permute-start(f32[520,128]{1,0:T(8,128)S(1)} %get-tuple-element.50), channel_id=1, source_target_pairs={{0,4},{1,0},{2,7},{4,8},{5,3},{6,13},{7,2},{8,6},{9,10},{10,11},{1... | collective-permute-start | bytes 798728 | tf_op jit(solution)/shard_map/ppermute | solution.py:282
  10.1 12.2 %collective-permute-start.3 = (f32[520,128]{1,0:T(8,128)S(1)}, f32[520,128]{1,0:T(8,128)S(1)}, u32[]{:S(2)}, u32[]{:S(2)}) collective-permute-start(f32[520,128]{1,0:T(8,128)S(1)} %get-tuple-element.51), channel_id=1, source_target_pairs={{0,2},{1,8},{3,4},{4,6},{5,1},{6,3},{7,11},{8,10},{9,13},{10,14},{... | collective-permute-start | bytes 798728 | tf_op jit(solution)/shard_map/ppermute | solution.py:282
  10.1 17.3 %collective-permute-start.4 = (f32[520,128]{1,0:T(8,128)S(1)}, f32[520,128]{1,0:T(8,128)S(1)}, u32[]{:S(2)}, u32[]{:S(2)}) collective-permute-start(f32[520,128]{1,0:T(8,128)S(1)} %get-tuple-element.52), channel_id=1, source_target_pairs={{0,1},{1,5},{3,6},{4,7},{5,12},{6,4},{7,9},{8,2},{9,11},{10,3},{11... | collective-permute-start | bytes 798728 | tf_op jit(solution)/shard_map/ppermute | solution.py:282
  16.2 16.3 %collective-permute-start.5 = (f32[520,128]{1,0:T(8,128)S(1)}, f32[520,128]{1,0:T(8,128)S(1)}, u32[]{:S(2)}, u32[]{:S(2)}) collective-permute-start(f32[520,128]{1,0:T(8,128)S(1)} %get-tuple-element.54), channel_id=1, source_target_pairs={{0,3},{1,7},{2,6},{3,1},{4,0},{5,9},{6,2},{7,10},{8,5},{9,14},{10,... | collective-permute-start | bytes 798728 | tf_op jit(solution)/shard_map/ppermute | solution.py:282
  16.3 18.0 %collective-permute-start.6 = (f32[520,128]{1,0:T(8,128)S(1)}, f32[520,128]{1,0:T(8,128)S(1)}, u32[]{:S(2)}, u32[]{:S(2)}) collective-permute-start(f32[520,128]{1,0:T(8,128)S(1)} %get-tuple-element.55), channel_id=1, source_target_pairs={{0,5},{1,3},{2,1},{3,2},{4,10},{5,0},{6,7},{7,8},{8,9},{9,4},{10,6... | collective-permute-start | bytes 798728 | tf_op jit(solution)/shard_map/ppermute | solution.py:282
  19.1 15.7 %collective-permute-start.7 = (f32[520,128]{1,0:T(8,128)S(1)}, f32[520,128]{1,0:T(8,128)S(1)}, u32[]{:S(2)}, u32[]{:S(2)}) collective-permute-start(f32[520,128]{1,0:T(8,128)S(1)} %get-tuple-element.56), channel_id=1, source_target_pairs={{0,1},{1,4},{2,3},{3,7},{4,9},{5,2},{6,8},{7,0},{8,11},{9,5},{10,1... | collective-permute-start | bytes 798728 | tf_op jit(solution)/shard_map/ppermute | solution.py:282
  27.4 9.5 %collective-permute-start.8 = (f32[520,128]{1,0:T(8,128)S(1)}, f32[520,128]{1,0:T(8,128)S(1)}, u32[]{:S(2)}, u32[]{:S(2)}) collective-permute-start(f32[520,128]{1,0:T(8,128)S(1)} %get-tuple-element.63), channel_id=1, source_target_pairs={{1,3},{2,1},{3,2},{4,0},{5,4},{6,12},{7,5},{8,13},{9,7},{10,9},{11... | collective-permute-start | bytes 798728 | tf_op jit(solution)/shard_map/ppermute | solution.py:282
  27.5 12.9 %collective-permute-start.9 = (f32[520,128]{1,0:T(8,128)S(1)}, f32[520,128]{1,0:T(8,128)S(1)}, u32[]{:S(2)}, u32[]{:S(2)}) collective-permute-start(f32[520,128]{1,0:T(8,128)S(1)} %get-tuple-element.66), channel_id=1, source_target_pairs={{0,1},{1,6},{2,0},{3,5},{4,2},{5,11},{6,10},{7,3},{8,4},{9,15},{10... | collective-permute-start | bytes 798728 | tf_op jit(solution)/shard_map/ppermute | solution.py:282
  32.5 8.3 %collective-permute-start.10 = (f32[520,128]{1,0:T(8,128)S(1)}, f32[520,128]{1,0:T(8,128)S(1)}, u32[]{:S(2)}, u32[]{:S(2)}) collective-permute-start(f32[520,128]{1,0:T(8,128)S(1)} %get-tuple-element.69), channel_id=1, source_target_pairs={{1,0},{2,4},{3,2},{4,5},{5,6},{6,1},{7,12},{8,14},{9,3},{10,11},{1... | collective-permute-start | bytes 798728 | tf_op jit(solution)/shard_map/ppermute | solution.py:282
  34.2 12.4 %collective-permute-start.11 = (f32[520,128]{1,0:T(8,128)S(1)}, f32[520,128]{1,0:T(8,128)S(1)}, u32[]{:S(2)}, u32[]{:S(2)}) collective-permute-start(f32[520,128]{1,0:T(8,128)S(1)} %get-tuple-element.72), channel_id=1, source_target_pairs={{0,3},{2,5},{3,0},{4,1},{5,4},{6,2},{7,13},{8,7},{9,12},{10,8},{11... | collective-permute-start | bytes 798728 | tf_op jit(solution)/shard_map/ppermute | solution.py:282
  34.7 12.6 %collective-permute-start.12 = (f32[520,128]{1,0:T(8,128)S(1)}, f32[520,128]{1,0:T(8,128)S(1)}, u32[]{:S(2)}, u32[]{:S(2)}) collective-permute-start(f32[520,128]{1,0:T(8,128)S(1)} %get-tuple-element.75), channel_id=1, source_target_pairs={{0,1},{2,0},{3,2},{4,3},{5,4},{6,5},{7,14},{8,15},{9,6},{10,11},{1... | collective-permute-start | bytes 798728 | tf_op jit(solution)/shard_map/ppermute | solution.py:282
  36.9 10.7 %collective-permute-start.13 = (f32[520,128]{1,0:T(8,128)S(1)}, f32[520,128]{1,0:T(8,128)S(1)}, u32[]{:S(2)}, u32[]{:S(2)}) collective-permute-start(f32[520,128]{1,0:T(8,128)S(1)} %get-tuple-element.78), channel_id=1, source_target_pairs={{0,4},{1,2},{2,3},{3,10},{4,11},{5,7},{6,0},{7,6},{8,1},{9,13},{10... | collective-permute-start | bytes 798728 | tf_op jit(solution)/shard_map/ppermute | solution.py:282
  48.6 12.5 %all-to-all-start = ((f32[16,1,128]{2,1,0:T(1,128)}), f32[16,1,128]{2,1,0:T(1,128)S(1)}, u32[]{:S(2)}, u32[]{:S(2)}) async-start(f32[16,1,128]{2,1,0:T(1,128)} %broadcast_in_dim.3), calls=%async_computation | async-start | bytes 16384 | tf_op jit(solution)/shard_map/all_to_all | solution.py:334
